TPU v7x, 32 devices: a whole 2x2x4 slice. The times are simulated.
32 devices in a mesh: gx: 8 (over z, core), gy: 4 (over y, x).
Axes of the slice: x: 2, y: 2, z: 4, core: 2. Of those that a mesh axis runs over, the one named last changes fastest.
Arguments:
- velocity: float32 [3, 6144, 2048], P(None, 'gx', 'gy'), may hold values from -6 to 6
- row_owner: int32 [8, 16], P('gx'), may hold values from 0 to 3, as said below
- cell_list: int32 [4, 16384], P(None, ('gx', 'gy')), may hold values from 0 to 786431
- weights: float32 [4, 16384], P(None, ('gx', 'gy')), may hold values from 0.05 to 0.5
- offsets: float32 [16384], P(('gx', 'gy')), may hold values from -0.5 to 0.5
- relax_rate: float32 [16384], P(('gx', 'gy')), may hold values from 0.05 to 0.8
- particle_velocity: float32 [3, 16384], P(None, ('gx', 'gy')), may hold values from -6 to 6
- live_counts: int32 [128], P(('gx', 'gy')), may hold values from 1 to 128, as said below
Outputs:
- gradient: float32 [3, 6144, 2048], P(None, 'gx', 'gy')
- fluid_at_particle: float32 [3, 16384], P(None, ('gx', 'gy'))
- updated_velocity: float32 [3, 16384], P(None, ('gx', 'gy'))
Inputs may be any that keep to these rules, and one draw needn't show every extreme that they name: `row_owner`: for every gx index and every gy index, at most 2 of that device's 4 row blocks name one owner; in every row of devices along gy one owner is named by exactly 2 blocks of every device; every owner is named by some block of the row. `live_counts`: the live particles of a block are its first slots.
All inputs are finite; a program needn't handle non-finite values.
Results may differ from a plain program's by a relative error of at most 0.0029.
Values may be sent and summed in bfloat16 or wider, within the bound.
No kernel may reach another device: no remote copies, remote signals or barrier semaphores. Data moves between devices by JAX's collectives and lax.ppermute only.
A program may use at most 128 MiB of HBM per device.

v0:
```python
import math

import jax
import jax.numpy as jnp
from jax import lax
from jax.sharding import PartitionSpec as P

ROWB = 128
PSIZE = 128
STEN = 4


R_DECAY = (3.0 - math.sqrt(5.0)) / 2.0
A_COEF = 14.0 / 9.0
B_COEF = 1.0 / 9.0
PRECISION_HIGH = lax.Precision.HIGHEST


def extended(cells, sides, width):
    for axis, dim in sides:
        count = lax.axis_size(axis)
        head = lax.slice_in_dim(cells, 0, width, axis=dim)
        tail = lax.slice_in_dim(cells, cells.shape[dim] - width, cells.shape[dim], axis=dim)
        cells = jnp.concatenate(
            [
                lax.ppermute(tail, axis, [(i, (i + 1) % count) for i in range(count)]),
                cells,
                lax.ppermute(head, axis, [((i + 1) % count, i) for i in range(count)]),
            ],
            axis=dim,
        )
    return cells


def stencil_sum(values, weights, offsets):
    carried = values[:3].astype(jnp.float32)
    slopes = values[3:].astype(jnp.float32)
    return jnp.sum(weights[None] * (carried + offsets[None, None] * slopes), 1)


def pick_cells(table, row_ids, line_ids):
    row_width = table.shape[2]
    picked = jnp.take(table, row_ids.reshape(-1), axis=1)
    select = jnp.arange(row_width)[None, :] == line_ids.reshape(-1)[:, None]
    values = jnp.sum(jnp.where(select[None], picked, jnp.zeros((), table.dtype)), -1)
    return values.reshape((table.shape[0],) + row_ids.shape)


def signed_power(exponent):
    parity = 1.0 - 2.0 * (exponent % 2).astype(jnp.float32)
    return parity * R_DECAY ** exponent.astype(jnp.float32)


def triangle(x_cells, backward):
    position = jnp.arange(x_cells)
    distance = position[:, None] - position[None, :]
    if backward:
        distance = -distance
    return jnp.where(distance >= 0, signed_power(jnp.abs(distance)), 0.0)


def widened_solve(velocity):
    components, x_cells, local_lines = velocity.shape
    margin = 20
    extent = x_cells + 2 * margin
    padded = extended(velocity, (("gx", 1),), margin + 2)
    right_side = 0.5 * A_COEF * (
        padded[:, 3 : extent + 3] - padded[:, 1 : extent + 1]
    ) + 0.25 * B_COEF * (padded[:, 4 : extent + 4] - padded[:, 0:extent])
    forward = jnp.einsum(
        "ij,cjl->cil", triangle(extent, False), right_side, precision=PRECISION_HIGH
    )
    backward = jnp.einsum("ij,cjl->cil", triangle(extent, True), forward, precision=PRECISION_HIGH)
    return 3.0 * R_DECAY * backward[:, margin : margin + x_cells]


def per_device(
    velocity, row_owner, cell_list, weights, offsets, relax_rate, particle_velocity, live_counts
):
    components, x_cells, local_lines = velocity.shape
    gradient = widened_solve(velocity)
    fields = jnp.concatenate([velocity, gradient], 0).astype(jnp.bfloat16)
    my_owner = lax.axis_index("gy")
    owners = lax.axis_size("gy")
    block_total = local_lines // ROWB
    capacity = block_total // 2
    column = row_owner[0]
    x_index = cell_list % x_cells
    remainder = cell_list // x_cells
    line_index = remainder % ROWB
    slot_ids = remainder // ROWB
    column_routes = column.reshape(owners, block_total)
    running = jnp.cumsum((column_routes == my_owner).astype(jnp.int32), 1)
    chosen = jnp.sum(
        (running[:, None, :] <= jnp.arange(capacity)[None, :, None]).astype(jnp.int32), 2
    )
    lookup = chosen.reshape(-1)
    matches = slot_ids[..., None] == jnp.arange(owners * capacity)
    block_id = jnp.sum(jnp.where(matches, lookup, 0), -1)
    holder = slot_ids // capacity
    local_spot = (x_index * block_total + block_id) * ROWB + line_index
    peer_ids = jnp.arange(owners)[:, None, None]
    belongs = holder[None] == peer_ids
    send_spots = jnp.where(belongs, local_spot[None], 0)
    send_weights = jnp.where(belongs, weights[None], 0.0)
    particle_slots = weights.shape[1]
    send_offsets = jnp.broadcast_to(offsets[None, None], (owners, 1, particle_slots))
    send_floats = jnp.concatenate([send_weights, send_offsets], 1)
    table = fields.reshape(6, x_cells * block_total, ROWB)
    got_spots = lax.all_to_all(send_spots, "gy", split_axis=0, concat_axis=0, tiled=True)
    got_floats = lax.all_to_all(send_floats, "gy", split_axis=0, concat_axis=0, tiled=True)
    values = pick_cells(table, got_spots // ROWB, got_spots % ROWB)
    partial_value = jax.vmap(stencil_sum, (1, 0, 0))(
        values, got_floats[:, :STEN], got_floats[:, STEN]
    )
    returned = lax.all_to_all(partial_value, "gy", split_axis=0, concat_axis=0, tiled=True)
    raw = jnp.sum(returned, 0)
    particle_slots = weights.shape[1]
    alive = (jnp.arange(PSIZE)[None, :] < live_counts[:, None]).reshape(particle_slots)
    fluid_at_particle = jnp.where(alive[None], raw, 0.0)
    updated_velocity = jnp.where(
        alive[None],
        particle_velocity + relax_rate[None] * (fluid_at_particle - particle_velocity),
        particle_velocity,
    )
    return (gradient, fluid_at_particle, updated_velocity)


def solution(mesh):
    return jax.shard_map(
        per_device,
        mesh=mesh,
        in_specs=(
            P(None, "gx", "gy"),
            P("gx", None),
            P(None, ("gx", "gy")),
            P(None, ("gx", "gy")),
            P(("gx", "gy")),
            P(("gx", "gy")),
            P(None, ("gx", "gy")),
            P(("gx", "gy")),
        ),
        out_specs=(P(None, "gx", "gy"), P(None, ("gx", "gy")), P(None, ("gx", "gy"))),
        check_vma=False,
    )
```

profile of v0, /device:TPU:0, one launch (start us, length us, event | category | flops | bytes accessed | tf_op | source)
XLA Modules:
  0.0 226.3 jit_solution(3165891383015165271)
XLA Ops:
  4.1 5.2 %all-to-all-start.1 = ((s32[4,4,512]{2,1,0:T(4,128)}), s32[4,4,512]{2,1,0:T(4,128)S(1)}, u32[]{:S(2)}, u32[]{:S(2)}) async-start(s32[4,4,512]{2,1,0:T(4,128)} %fusion.74), calls=%async_computation.1 | async-start | bytes 65536 | tf_op jit(solution)/shard_map/all_to_all | solution.py:110
  9.3 1.0 fusion.104
  10.4 3.5 %collective-permute-start.1 = (f32[3,22,512]{2,1,0:T(8,128)S(1)}, f32[3,22,512]{2,1,0:T(8,128)}, u32[]{:S(2)}, u32[]{:S(2)}) collective-permute-start(f32[3,22,512]{2,1,0:T(8,128)S(1)} %get-tuple-element.10), channel_id=1, source_target_pairs={{4,0},{8,4},{12,8},{16,12},{20,16},{24,20},{28,24},{0,28},{5,1},{9... | collective-permute-start | bytes 405512 | tf_op jit(solution)/shard_map/ppermute | solution.py:28
  15.9 2.6 %convert.12 = bf16[3,768,512]{2,1,0:T(8,128)(2,1)S(1)} convert(f32[3,768,512]{2,1,0:T(8,128)} %param.8) | non-fusion elementwise | flops 1179648 | bytes 7077888 | tf_op jit(solution)/shard_map/convert.7
  18.5 2.7 %concatenate.17 = bf16[3,3072,128]{2,1,0:T(8,128)(2,1)} reshape(bf16[3,768,512]{2,1,0:T(8,128)(2,1)S(1)} %convert.12) | data formatting | bytes 4718592 | tf_op jit(solution)/shard_map/concatenate | solution.py:82
  21.3 4.3 %copy.24 = bf16[3,3072,128]{2,0,1:T(4,128)(2,1)S(1)} copy(bf16[3,3072,128]{2,1,0:T(8,128)(2,1)} %concatenate.17) | data formatting | bytes 4718592 | tf_op jit(solution)/shard_map/concatenate | solution.py:82
  26.2 4.2 %all-to-all-start = ((f32[4,5,512]{2,1,0:T(8,128)}), f32[4,5,512]{2,1,0:T(8,128)S(1)}, u32[]{:S(2)}, u32[]{:S(2)}) async-start(f32[4,5,512]{2,1,0:T(8,128)} %pad_maximum_fusion.2), calls=%async_computation | async-start | bytes 131072 | tf_op jit(solution)/shard_map/all_to_all | solution.py:111
  30.4 1.4 fusion.73
  32.5 0.8 compare_select_fusion
  33.9 0.8 copy.28
  34.7 4.6 %iota_compare_fusion = pred[8192,128]{1,0:T(8,128)(4,1)} fusion(s32[8192]{0:T(1024)S(1)} %bitcast.37), kind=kLoop, calls=%fused_computation.25 | loop fusion | flops 1048576 | bytes 1081344 | tf_op jit(solution)/shard_map/eq | solution.py:44
  39.4 3.3 %pad_maximum_fusion.1 = f32[3,812,512]{2,1,0:T(8,128)S(1)} fusion(f32[3,22,512]{2,1,0:T(8,128)} %collective-permute-done.1, f32[3,768,512]{2,1,0:T(8,128)} %param.8, f32[3,22,512]{2,1,0:T(8,128)} %collective-permute-done), kind=kLoop, calls=%fused_computation.3 | loop fusion | flops 2494464 | bytes 9977856 | tf_op jit(solution)/shard_map/concatenate | solution.py:24
  42.7 18.5 %fusion.2 = f32[3,512,808]{1,2,0:T(8,128)S(1)} fusion(f32[3,812,512]{2,1,0:T(8,128)S(1)} %pad_maximum_fusion.1), kind=kOutput, calls=%fused_computation.7 | convolution fusion | flops 12052851712 | bytes 24821760 | tf_op jit(solution)/shard_map/ij,cjl->cil/dot_general | solution.py:70
  61.2 18.5 %fusion.54 = f32[3,808,512]{2,1,0:T(8,128)S(1)} fusion(f32[3,512,808]{1,2,0:T(8,128)S(1)} %fusion.2), kind=kOutput, calls=%fused_computation.58 | convolution fusion | flops 12047299584 | bytes 9928704 | tf_op jit(solution)/shard_map/ij,cjl->cil/dot_general | solution.py:73
  79.8 3.7 %fusion.103 = (bf16[3,768,512]{2,1,0:T(8,128)(2,1)}, f32[3,768,512]{2,1,0:T(8,128)}) fusion(f32[3,808,512]{2,1,0:T(8,128)S(1)} %fusion.54), kind=kLoop, calls=%fused_computation.141 | loop fusion | flops 2359296 | bytes 11796480 | tf_op jit(solution)/shard_map/convert.6
  83.5 5.1 %concatenate.18 = bf16[3,3072,128]{2,1,0:T(8,128)(2,1)} reshape(bf16[3,768,512]{2,1,0:T(8,128)(2,1)} %get-tuple-element.7) | data formatting | bytes 4718592 | tf_op jit(solution)/shard_map/concatenate | solution.py:82
  88.6 4.3 %copy.25 = bf16[3,3072,128]{2,0,1:T(4,128)(2,1)S(1)} copy(bf16[3,3072,128]{2,1,0:T(8,128)(2,1)} %concatenate.18) | data formatting | bytes 4718592 | tf_op jit(solution)/shard_map/concatenate | solution.py:82
  93.0 4.8 %pad_maximum_fusion = bf16[6,3072,128]{2,0,1:T(8,128)(2,1)} fusion(bf16[3,3072,128]{2,0,1:T(4,128)(2,1)S(1)} %copy.25, bf16[3,3072,128]{2,0,1:T(4,128)(2,1)S(1)} %copy.24), kind=kLoop, calls=%fused_computation.2 | loop fusion | flops 9437184 | bytes 9437184 | tf_op jit(solution)/shard_map/concatenate | solution.py:82
  97.8 60.2 %gather_fusion = bf16[8192,6,128]{2,1,0:T(8,128)(2,1)} fusion(bf16[6,3072,128]{2,0,1:T(8,128)(2,1)} %pad_maximum_fusion, s32[8192]{0:T(1024)S(1)} %copy-done.2), kind=kCustom, calls=%fused_computation | custom fusion | bytes 25198592 | tf_op jit(solution)/shard_map/jit(_take)/gather | solution.py:43
  158.0 55.0 %select_reduce_fusion = bf16[8192,6]{1,0:T(8,128)(2,1)S(1)} fusion(bf16[8192,6,128]{2,1,0:T(8,128)(2,1)} %gather_fusion, pred[8192]{0:T(1024)(128)(4,1)S(1)} %compare_and_fusion, pred[8192,128]{1,0:T(8,128)(4,1)S(1)} %copy-done), kind=kLoop, calls=%fused_computation.1 | loop fusion | flops 18825216 | bytes 13737984 | tf_op jit(solution)/shard_map/reduce_sum | solution.py:45
  213.8 1.8 fusion.12
  215.6 0.9 copy.26
  216.5 4.2 %all-to-all-start.2 = ((f32[4,3,512]{2,1,0:T(4,128)}), f32[4,3,512]{2,1,0:T(4,128)S(1)}, u32[]{:S(2)}, u32[]{:S(2)}) async-start(f32[4,3,512]{2,1,0:T(4,128)} %copy.26), calls=%async_computation.2 | async-start | bytes 65536 | tf_op jit(solution)/shard_map/all_to_all | solution.py:116
  220.8 4.7 %all-to-all-done.2 = f32[4,3,512]{2,1,0:T(4,128)S(1)} async-done(((f32[4,3,512]{2,1,0:T(4,128)}), f32[4,3,512]{2,1,0:T(4,128)S(1)}, u32[]{:S(2)}, u32[]{:S(2)}) %all-to-all-start.2) | async-done | bytes 24608 | tf_op jit(solution)/shard_map/all_to_all | solution.py:116
  (44 shorter events, 9.0 us)
Async XLA Ops:
  4.1 21.5 %all-to-all-start.1 = ((s32[4,4,512]{2,1,0:T(4,128)}), s32[4,4,512]{2,1,0:T(4,128)S(1)}, u32[]{:S(2)}, u32[]{:S(2)}) async-start(s32[4,4,512]{2,1,0:T(4,128)} %fusion.74), calls=%async_computation.1 | async-start | bytes 65536 | tf_op jit(solution)/shard_map/all_to_all | solution.py:110
  10.3 29.1 %collective-permute-start = (f32[3,22,512]{2,1,0:T(8,128)S(1)}, f32[3,22,512]{2,1,0:T(8,128)}, u32[]{:S(2)}, u32[]{:S(2)}) collective-permute-start(f32[3,22,512]{2,1,0:T(8,128)S(1)} %get-tuple-element.9), channel_id=1, source_target_pairs={{0,4},{4,8},{8,12},{12,16},{16,20},{20,24},{24,28},{28,0},{1,5},{5... | collective-permute-start | bytes 405512 | tf_op jit(solution)/shard_map/ppermute | solution.py:26
  10.4 29.1 %collective-permute-start.1 = (f32[3,22,512]{2,1,0:T(8,128)S(1)}, f32[3,22,512]{2,1,0:T(8,128)}, u32[]{:S(2)}, u32[]{:S(2)}) collective-permute-start(f32[3,22,512]{2,1,0:T(8,128)S(1)} %get-tuple-element.10), channel_id=1, source_target_pairs={{4,0},{8,4},{12,8},{16,12},{20,16},{24,20},{28,24},{0,28},{5,1},{9... | collective-permute-start | bytes 405512 | tf_op jit(solution)/shard_map/ppermute | solution.py:28
  25.6 0.6 copy-start.3
  26.2 13.2 %all-to-all-start = ((f32[4,5,512]{2,1,0:T(8,128)}), f32[4,5,512]{2,1,0:T(8,128)S(1)}, u32[]{:S(2)}, u32[]{:S(2)}) async-start(f32[4,5,512]{2,1,0:T(8,128)} %pad_maximum_fusion.2), calls=%async_computation | async-start | bytes 131072 | tf_op jit(solution)/shard_map/all_to_all | solution.py:111
  39.4 3.3 %copy-start.1 = (f32[4,5,512]{2,1,0:T(8,128)}, f32[4,5,512]{2,1,0:T(8,128)S(1)}, u32[]{:S(2)}) copy-start(f32[4,5,512]{2,1,0:T(8,128)S(1)} %all-to-all-done) | copy-start | bytes 122884
  92.9 4.9 %copy-start.2 = (s32[8192]{0:T(1024)S(1)}, s32[8192]{0:T(1024)}, u32[]{:S(2)}) copy-start(s32[8192]{0:T(1024)} %broadcast_clamp_fusion) | copy-start | bytes 98308
  97.8 60.2 %copy-start = (pred[8192,128]{1,0:T(8,128)(4,1)S(1)}, pred[8192,128]{1,0:T(8,128)(4,1)}, u32[]{:S(2)}) copy-start(pred[8192,128]{1,0:T(8,128)(4,1)} %iota_compare_fusion) | copy-start | bytes 3145732
  213.0 0.8 slice-start
  213.8 6.9 %copy-start.6 = (s32[4]{0:T(128)S(1)}, s32[4]{0:T(128)}, u32[]{:S(2)}) copy-start(s32[4]{0:T(128)} %param.15) | copy-start | bytes 52
  213.8 11.7 %copy-start.4 = (f32[3,512]{1,0:T(4,128)S(1)}, f32[3,512]{1,0:T(4,128)}, u32[]{:S(2)}) copy-start(f32[3,512]{1,0:T(4,128)} %param.14) | copy-start | bytes 18436
  213.8 11.7 %copy-start.5 = (f32[512]{0:T(512)S(1)}, f32[512]{0:T(512)}, u32[]{:S(2)}) copy-start(f32[512]{0:T(512)} %param.13) | copy-start | bytes 6148
  216.5 9.0 %all-to-all-start.2 = ((f32[4,3,512]{2,1,0:T(4,128)}), f32[4,3,512]{2,1,0:T(4,128)S(1)}, u32[]{:S(2)}, u32[]{:S(2)}) async-start(f32[4,3,512]{2,1,0:T(4,128)} %copy.26), calls=%async_computation.2 | async-start | bytes 65536 | tf_op jit(solution)/shard_map/all_to_all | solution.py:116
where the time goes:
time: 231 us; the launch traced here: 226 us
  other arithmetic  83.9 us (36%)
  local copies, waits for them, and re-layouts  82.4 us (36%)
  matrix products  37 us (16%)
  starting transfers between devices  17.1 us (7%)
  waiting for transfers between devices  4.69 us (2%)
    gather x1, local copies, waits for them, and re-layouts, pick_cells(): picked = jnp.take(table, row_ids.reshape(-1), axis=1)  60.2 us
    reduce_sum x1, other arithmetic, pick_cells(): jnp.sum(jnp.where(select[None], picked, jnp.zeros((), table.dtype)), -1)  55 us
    dot_general x1, matrix products, widened_solve(): jnp.einsum('ij,cjl->cil', triangle(extent, False), right_side, precision=...  18.5 us
    dot_general x1, matrix products, widened_solve(): jnp.einsum('ij,cjl->cil', triangle(extent, True), forward, precision=PREC...  18.5 us
    concatenate x4, local copies, waits for them, and re-layouts, per_device(): fields = jnp.concatenate([velocity, gradient], 0).astype(jnp.bfloat16)  16.5 us
    another operation x2, other arithmetic  6.34 us
    all_to_all x1, starting transfers between devices, per_device(): lax.all_to_all(send_spots, 'gy', split_axis=0, concat_axis=0, tiled=True)  5.16 us
    concatenate x1, other arithmetic, per_device(): fields = jnp.concatenate([velocity, gradient], 0).astype(jnp.bfloat16)  4.84 us
  transfers between devices with their start and end apart: 5, of which 1 were waited for; matrix products, arithmetic and copies ran while one was open for 10% of the time, Pallas kernels for 0%

commit v1 on v0

v1 whole, which is shorter than its diff:
```python
import math

import jax
import jax.numpy as jnp
import numpy as np
from jax import lax
from jax.experimental import pallas as pl
from jax.experimental.pallas import tpu as pltpu
from jax.sharding import PartitionSpec as P

ROWB = 128
PSIZE = 128
STEN = 4
EDGE = 32
ROWS = 192
CHUNK = 64
R_DECAY = (3.0 - math.sqrt(5.0)) / 2.0
F32 = jnp.float32
BF16 = jnp.bfloat16


def kernel_taps(reach):
    level = 3.0 / math.sqrt(5.0)

    def inverse(n):
        return level * (-R_DECAY) ** abs(n)

    taps = np.zeros(reach + 1)
    for n in range(reach + 1):
        taps[n] = (7.0 / 9.0) * (inverse(n + 1) - inverse(n - 1)) + (1.0 / 36.0) * (
            inverse(n + 2) - inverse(n - 2)
        )
    return taps


TAPS = kernel_taps(300)
TAIL = TAPS[2] / R_DECAY**2
FIRST = TAPS[1] + TAIL * R_DECAY


def split(values, terms):
    parts = []
    for _ in range(terms):
        part = values.astype(BF16)
        parts.append(part)
        values = values - part.astype(F32)
    return parts


def toeplitz(offset, rows, window):
    distance = offset + np.arange(rows)[:, None] - np.arange(window)[None, :]
    full = np.sign(distance) * TAPS[np.abs(distance)]
    high = full.astype(BF16)
    low = (full - high.astype(np.float64)).astype(BF16)
    return np.stack([high, low])


def edge_state(rows, from_first):
    index = lax.broadcasted_iota(jnp.int32, rows.shape, 0)
    steps = index + 1 if from_first else EDGE - index
    parity = 1.0 - 2.0 * (steps & 1).astype(F32)
    decay = parity * jnp.exp(steps.astype(F32) * math.log(R_DECAY))
    return jnp.sum(rows * decay, 0, keepdims=True)


def prep_body(x_cells, live, head, tail, cells, weights, offsets, to_right, to_left, request):
    zero = jnp.zeros((2, head.shape[2]), F32)
    to_left[...] = jnp.concatenate(
        [edge_state(head[c], True) for c in range(3)] + [head[c, 0:1, :] for c in range(3)] + [zero], 0
    )
    to_right[...] = jnp.concatenate(
        [edge_state(tail[c], False) for c in range(3)]
        + [tail[c, EDGE - 1 : EDGE, :] for c in range(3)]
        + [zero],
        0,
    )
    cell = cells[...]
    slots = cell.shape[1]
    row = jnp.floor((cell.astype(F32) + 0.5) * (1.0 / x_cells)).astype(jnp.int32)
    x = cell - row * x_cells
    line = row & (ROWB - 1)
    slot = (row >> 7)[0:1]
    lane = lax.broadcasted_iota(jnp.int32, (1, slots), 1)
    limit = jnp.zeros((1, slots), jnp.int32)
    for k in range(slots // PSIZE):
        limit = jnp.where(lane // PSIZE == k, live[k], limit)
    alive = lane % PSIZE < limit
    key = jnp.where(alive, slot, -1).astype(F32)
    w_high, w_low = split(weights[...], 2)
    o_high, o_low = split(offsets[...].reshape(1, slots), 2)
    request[...] = jnp.concatenate(
        [
            (x >> 3).astype(F32),
            (x & 7).astype(F32),
            line.astype(F32),
            w_high.astype(F32),
            w_low.astype(F32),
            o_high.astype(F32),
            o_low.astype(F32),
            key,
            jnp.zeros((9, slots), F32),
        ],
        0,
    ).astype(BF16)


def derivative_body(plan, v_ref, t_ref, g_ref, fv_ref, fg_ref, edge_ref):
    window = t_ref.shape[3]
    high, low = split(v_ref[0], 2)
    lanes = high.shape[1]
    x_cells = high.shape[0]
    for k in range(lanes // ROWB):
        fv_ref[0, k] = high[:, k * ROWB : (k + 1) * ROWB]
    for row, start, kind in plan:
        hi = high[start : start + window]
        lo = low[start : start + window]
        t_high, t_low = t_ref[kind, 0], t_ref[kind, 1]
        out = (
            jnp.dot(t_high, hi, preferred_element_type=F32)
            + jnp.dot(t_high, lo, preferred_element_type=F32)
            + jnp.dot(t_low, hi, preferred_element_type=F32)
        )
        g_ref[0, row : row + ROWS] = out
        rounded = out.astype(BF16)
        for k in range(lanes // ROWB):
            fg_ref[0, k, row : row + ROWS] = rounded[:, k * ROWB : (k + 1) * ROWB]
        if row == 0:
            edge_ref[0, :EDGE] = out[:EDGE]
        if row + ROWS == x_cells:
            edge_ref[0, EDGE:] = out[ROWS - EDGE :]


def edge_fix(rows, state, plane, is_left):
    index = lax.broadcasted_iota(jnp.int32, rows.shape, 0)
    steps = index if is_left else EDGE - 1 - index
    parity = 1.0 - 2.0 * (steps & 1).astype(F32)
    decay = parity * jnp.exp(steps.astype(F32) * math.log(R_DECAY))
    sign = 1.0 if is_left else -1.0
    return rows + (sign * TAIL) * decay * state + jnp.where(steps == 0, sign * FIRST, 0.0) * plane


def lookup_body(
    owners, xor, owner_ref, fv_ref, fg_ref, edge_ref, left_ref, right_ref, *refs
):
    request_refs = refs[:owners]
    grad_in = refs[owners]
    grad_out = refs[owners + 1]
    out_refs = refs[owners + 2 : 2 * owners + 2]
    requests, fixed, ranks, counts, totals, sems = refs[2 * owners + 2 :]
    del grad_in
    step = pl.program_id(0)
    blocks = pl.num_programs(0)
    me = lax.axis_index("gy")
    capacity = 2
    slots = requests.shape[2]
    groups = slots // ROWB
    x_cells = fv_ref.shape[2]
    block_total = 4

    def peer_of(block):
        owner = owner_ref[0, me * block_total + block]
        return (owner ^ me) if xor else lax.rem(owner - me + owners, owners)

    def edge_copies():
        return (
            pltpu.make_async_copy(
                fixed.at[:, pl.ds(0, EDGE)], grad_out.at[:, pl.ds(0, EDGE)], sems.at[0]
            ),
            pltpu.make_async_copy(
                fixed.at[:, pl.ds(EDGE, EDGE)],
                grad_out.at[:, pl.ds(x_cells - EDGE, EDGE)],
                sems.at[1],
            ),
        )

    @pl.when(step == 0)
    def _():
        for c in range(3):
            fixed[c, :EDGE] = edge_fix(
                edge_ref[c, :EDGE], left_ref[c : c + 1], left_ref[c + 3 : c + 4], True
            )
            fixed[c, EDGE:] = edge_fix(
                edge_ref[c, EDGE:], right_ref[c : c + 1], right_ref[c + 3 : c + 4], False
            )
        for copy in edge_copies():
            copy.start()
        for k in range(owners):
            requests[k] = request_refs[k][...]
            totals[k] = jnp.zeros(totals.shape[1:], F32)
        matched = []
        for block in range(block_total):
            peer = peer_of(block)
            rank = jnp.int32(0)
            for earlier in range(block):
                rank += (peer_of(earlier) == peer).astype(jnp.int32)
            key = requests[peer, 16:32, :].astype(F32)[6:7]
            matched.append(jnp.where(key == (me * capacity + rank).astype(F32), 1.0, 0.0))
        stacked = jnp.concatenate(
            [m[:, k * ROWB : (k + 1) * ROWB] for m in matched for k in range(groups)], 0
        )
        upto = lax.broadcasted_iota(jnp.int32, (ROWB, ROWB), 0) <= lax.broadcasted_iota(
            jnp.int32, (ROWB, ROWB), 1
        )
        running = jnp.dot(
            stacked.astype(BF16), jnp.where(upto, 1.0, 0.0).astype(BF16), preferred_element_type=F32
        )
        for block in range(block_total):
            before = jnp.zeros((1, 1), F32)
            pieces = []
            for k in range(groups):
                r = block * groups + k
                here = stacked[r : r + 1]
                line = running[r : r + 1]
                pieces.append(jnp.where(here > 0.5, line - 1.0 + before, -1.0))
                before = before + line[:, ROWB - 1 : ROWB]
            ranks[block] = jnp.concatenate(pieces, 1)
            counts[block] = before[0, 0].astype(jnp.int32)

    peer = peer_of(step)
    lanes_at = pl.ds(pl.multiple_of(step * ROWB, ROWB), ROWB)
    count = counts[step]
    lane = lax.broadcasted_iota(jnp.int32, (CHUNK, ROWB), 1).astype(F32)
    lane_x = lax.broadcasted_iota(jnp.int32, (CHUNK, x_cells), 1).astype(F32)
    tables = [fv_ref[c, 0] for c in range(3)] + [
        jnp.concatenate(
            [
                fixed[c, :EDGE, lanes_at].astype(BF16),
                fg_ref[c, 0, EDGE : x_cells - EDGE],
                fixed[c, EDGE:, lanes_at].astype(BF16),
            ],
            0,
        )
        for c in range(3)
    ]
    table = jnp.concatenate(tables, 1)

    def chunk(i, carry):
        place = (lax.broadcasted_iota(jnp.int32, (CHUNK, slots), 0) + i * CHUNK).astype(F32)
        chosen = jnp.where(ranks[step] == place, 1.0, 0.0).astype(BF16)
        data = lax.dot_general(
            chosen, requests[peer], (((1,), (1,)), ((), ())), preferred_element_type=F32
        )
        picks, masks = [], []
        for s in range(STEN):
            x = data[:, s : s + 1] * 8.0 + data[:, 4 + s : 5 + s]
            weight = data[:, 12 + s : 13 + s] + data[:, 16 + s : 17 + s]
            picks.append(jnp.where(lane_x == x, 1.0, 0.0).astype(BF16))
            masks.append(jnp.where(lane == data[:, 8 + s : 9 + s], weight, 0.0))
        offset = data[:, 20:21] + data[:, 21:22]
        rows = jnp.dot(jnp.concatenate(picks, 0), table, preferred_element_type=F32)
        sums = []
        for c in range(6):
            total = jnp.zeros((CHUNK, ROWB), F32)
            for s in range(STEN):
                total += masks[s] * rows[s * CHUNK : (s + 1) * CHUNK, c * ROWB : (c + 1) * ROWB]
            sums.append(total)
        value = jnp.zeros((CHUNK, ROWB), F32)
        for c in range(3):
            mixed = jnp.sum(sums[c] + offset * sums[3 + c], 1, keepdims=True)
            for k, part in enumerate(split(mixed, 3)):
                value = jnp.where(lane == float(k * 4 + c), part.astype(F32), value)
        back = jnp.transpose(value)[:16].astype(BF16)
        placed = jnp.dot(back, chosen, preferred_element_type=F32)
        totals[peer] += placed
        return carry

    lax.fori_loop(0, (count + CHUNK - 1) // CHUNK, chunk, 0)

    @pl.when(step == blocks - 1)
    def _():
        for k in range(owners):
            total = totals[k]
            both = total[0:8] + pltpu.roll(total[0:8], 4, 0) + total[8:16]
            out_refs[k][...] = both
        for copy in edge_copies():
            copy.wait()


def final_body(live, relax, particle, *refs):
    parts, (fluid_ref, updated_ref) = refs[:-2], refs[-2:]
    raw = parts[0][0:3]
    for part in parts[1:]:
        raw = raw + part[0:3]
    slots = raw.shape[1]
    lane = lax.broadcasted_iota(jnp.int32, (3, slots), 1)
    limit = jnp.zeros((3, slots), jnp.int32)
    for k in range(slots // PSIZE):
        limit = jnp.where(lane // PSIZE == k, live[k], limit)
    alive = lane % PSIZE < limit
    fluid = jnp.where(alive, raw, 0.0)
    velocity = particle[...]
    fluid_ref[...] = fluid
    updated_ref[...] = jnp.where(
        alive, velocity + relax[...].reshape(1, slots) * (fluid - velocity), velocity
    )


def sent(values, axis, pairs):
    return lax.ppermute(values, axis, pairs)


def per_device(
    velocity, row_owner, cell_list, weights, offsets, relax_rate, particle_velocity, live_counts
):
    components, x_cells, lines = velocity.shape
    slots = weights.shape[1]
    columns = lax.axis_size("gx")
    owners = lax.axis_size("gy")
    blocks = lines // ROWB
    xor = owners & (owners - 1) == 0
    vmem = pl.BlockSpec(memory_space=pltpu.VMEM)
    smem = pl.BlockSpec(memory_space=pltpu.SMEM)
    anywhere = pl.BlockSpec(memory_space=pl.ANY)
    limit = 48 * 1024 * 1024

    last = x_cells // EDGE - 1
    one = lambda shape: pl.BlockSpec(shape, lambda i: (0,) * len(shape))
    to_right, to_left, request = pl.pallas_call(
        lambda *refs: prep_body(x_cells, *refs),
        grid=(1,),
        in_specs=[
            smem,
            pl.BlockSpec((3, EDGE, lines), lambda i: (0, 0, 0)),
            pl.BlockSpec((3, EDGE, lines), lambda i: (0, last, 0)),
            one((STEN, slots)),
            one((STEN, slots)),
            one((slots,)),
        ],
        out_specs=[one((8, lines)), one((8, lines)), one((32, slots))],
        out_shape=[
            jax.ShapeDtypeStruct((8, lines), F32),
            jax.ShapeDtypeStruct((8, lines), F32),
            jax.ShapeDtypeStruct((32, slots), BF16),
        ],
        name="prepare",
    )(live_counts, velocity, velocity, cell_list, weights, offsets)

    from_left = sent(to_right, "gx", [(i, (i + 1) % columns) for i in range(columns)])
    from_right = sent(to_left, "gx", [((i + 1) % columns, i) for i in range(columns)])

    def peer(i, k):
        return i ^ k if xor else (i + k) % owners

    requests = [request] + [
        sent(request, "gy", [(peer(i, k), i) for i in range(owners)]) for k in range(1, owners)
    ]

    window = min(256, x_cells)
    plan, kinds = [], []
    for row in range(0, x_cells, ROWS):
        start = min(max(row - EDGE, 0), x_cells - window)
        if row - start not in kinds:
            kinds.append(row - start)
        plan.append((row, start, kinds.index(row - start)))
    matrices = jnp.asarray(np.stack([toeplitz(o, ROWS, window) for o in kinds]))
    tile = 256
    per_tile = tile // ROWB
    gradient, table_v, table_g, edges = pl.pallas_call(
        lambda *refs: derivative_body(plan, *refs),
        grid=(components, lines // tile),
        in_specs=[
            pl.BlockSpec((1, x_cells, tile), lambda c, t: (c, 0, t)),
            pl.BlockSpec(matrices.shape, lambda c, t: (0, 0, 0, 0)),
        ],
        out_specs=[
            pl.BlockSpec((1, x_cells, tile), lambda c, t: (c, 0, t)),
            pl.BlockSpec((1, per_tile, x_cells, ROWB), lambda c, t: (c, t, 0, 0)),
            pl.BlockSpec((1, per_tile, x_cells, ROWB), lambda c, t: (c, t, 0, 0)),
            pl.BlockSpec((1, 2 * EDGE, tile), lambda c, t: (c, 0, t)),
        ],
        out_shape=[
            jax.ShapeDtypeStruct(velocity.shape, F32),
            jax.ShapeDtypeStruct((components, blocks, x_cells, ROWB), BF16),
            jax.ShapeDtypeStruct((components, blocks, x_cells, ROWB), BF16),
            jax.ShapeDtypeStruct((components, 2 * EDGE, lines), F32),
        ],
        compiler_params=pltpu.CompilerParams(vmem_limit_bytes=limit),
        cost_estimate=pl.CostEstimate(
            flops=6 * window * velocity.size, bytes_accessed=14 * velocity.size, transcendentals=0
        ),
        name="derivative",
    )(velocity, matrices)

    outs = pl.pallas_call(
        lambda *refs: lookup_body(owners, xor, *refs),
        grid=(blocks,),
        in_specs=[
            smem,
            pl.BlockSpec((components, 1, x_cells, ROWB), lambda b: (0, b, 0, 0)),
            pl.BlockSpec((components, 1, x_cells, ROWB), lambda b: (0, b, 0, 0)),
            one((components, 2 * EDGE, lines)),
            one((8, lines)),
            one((8, lines)),
        ]
        + [one((32, slots))] * owners
        + [anywhere],
        out_specs=[anywhere] + [one((8, slots))] * owners,
        out_shape=[jax.ShapeDtypeStruct(velocity.shape, F32)]
        + [jax.ShapeDtypeStruct((8, slots), F32)] * owners,
        scratch_shapes=[
            pltpu.VMEM((owners, 32, slots), BF16),
            pltpu.VMEM((components, 2 * EDGE, lines), F32),
            pltpu.VMEM((blocks, 1, slots), F32),
            pltpu.SMEM((blocks,), jnp.int32),
            pltpu.VMEM((owners, 16, slots), F32),
            pltpu.SemaphoreType.DMA((2,)),
        ],
        input_output_aliases={6 + owners: 0},
        compiler_params=pltpu.CompilerParams(vmem_limit_bytes=limit),
        cost_estimate=pl.CostEstimate(
            flops=2 * 768 * 6 * x_cells * 1024, bytes_accessed=4 * velocity.size, transcendentals=0
        ),
        name="lookup",
    )(row_owner, table_v, table_g, edges, from_left, from_right, *requests, gradient)
    gradient, partials = outs[0], outs[1:]

    returned = [partials[0]] + [
        sent(partials[k], "gy", [(i, peer(i, k)) for i in range(owners)]) for k in range(1, owners)
    ]
    shape = jax.ShapeDtypeStruct((3, slots), F32)
    fluid, updated = pl.pallas_call(
        final_body,
        grid=(1,),
        in_specs=[smem, one((slots,)), one((3, slots))] + [one((8, slots))] * owners,
        out_specs=[one((3, slots))] * 2,
        out_shape=[shape, shape],
        name="finish",
    )(live_counts, relax_rate, particle_velocity, *returned)
    return (gradient, fluid, updated)


def solution(mesh):
    return jax.shard_map(
        per_device,
        mesh=mesh,
        in_specs=(
            P(None, "gx", "gy"),
            P("gx", None),
            P(None, ("gx", "gy")),
            P(None, ("gx", "gy")),
            P(("gx", "gy")),
            P(("gx", "gy")),
            P(None, ("gx", "gy")),
            P(("gx", "gy")),
        ),
        out_specs=(P(None, "gx", "gy"), P(None, ("gx", "gy")), P(None, ("gx", "gy"))),
        check_vma=False,
    )
```

time: 231 us -> 35.4 us (0.15); the launches traced: 226 us -> 35.1 us
  other arithmetic: 83.9 us -> 0 us
  local copies, waits for them, and re-layouts: 82.4 us -> 1.21 us
  matrix products: 37 us -> 0 us
  Pallas kernels: 0 us -> 16 us
  starting transfers between devices: 17.1 us -> 12.6 us
    gather x1 -> x0, local copies, waits for them, and re-layouts: 60.2 us -> none  [pick_cells(): picked = jnp.take(table, row_ids.reshape(-1), axis=1)]
    reduce_sum x5 -> x0, other arithmetic: 57 us -> none  [the longest x1 55 us: pick_cells(): jnp.sum(jnp.where(select[None], picked, jnp.zeros((), table.dtype)), -1)]
    dot_general x2 -> x0, matrix products: 37 us -> none  [the longest x1 18.5 us: widened_solve(): jnp.einsum('ij,cjl->cil', triangle(extent, False), right_side, precision=...]
    concatenate x4 -> x0, local copies, waits for them, and re-layouts: 16.5 us -> none  [per_device(): fields = jnp.concatenate([velocity, gradient], 0).astype(jnp.bfloat16)]
    pallas_call x0 -> x4, Pallas kernels: none -> 16 us  [the longest x1 7.04 us: per_device(): pl.pallas_call(lambda *refs: derivative_body(plan, *refs), grid=(componen...]
    all_to_all x3 -> x0, starting transfers between devices: 13.6 us -> none  [the longest x1 5.16 us: per_device(): lax.all_to_all(send_spots, 'gy', split_axis=0, concat_axis=0, tiled=True)]
    ppermute x2 -> x8, starting transfers between devices: 3.59 us -> 12.6 us  [sent(): return lax.ppermute(values, axis, pairs)]
    concatenate x3 -> x0, other arithmetic: 8.73 us -> none  [the longest x1 4.84 us: per_device(): fields = jnp.concatenate([velocity, gradient], 0).astype(jnp.bfloat16)]
  transfers between devices with their start and end apart: 5 -> 8, of which waited for: 1 -> 3; matrix products, arithmetic and copies ran while one was open for 10% -> 0% of each run, Pallas kernels for 0% -> 20%
where the time goes in v1:
time: 35.4 us; the launch traced here: 35.1 us
  Pallas kernels  16 us (45%)
  starting transfers between devices  12.6 us (36%)
  waiting for transfers between devices  4.64 us (13%)
  local copies, waits for them, and re-layouts  1.21 us (3%)
  between operations  0.7 us (2%)
    ppermute x8, starting transfers between devices, sent(): return lax.ppermute(values, axis, pairs)  12.6 us
    pallas_call x1, Pallas kernels, per_device(): pl.pallas_call(lambda *refs: derivative_body(plan, *refs), grid=(componen...  7.04 us
    pallas_call x1, Pallas kernels, per_device(): pl.pallas_call(lambda *refs: lookup_body(owners, xor, *refs), grid=(block...  5.71 us
    ppermute x8, waiting for transfers between devices, sent(): return lax.ppermute(values, axis, pairs)  4.64 us
    pallas_call x1, Pallas kernels, per_device(): pl.pallas_call(lambda *refs: prep_body(x_cells, *refs), grid=(1,), in_spe...  1.81 us
    pallas_call x1, Pallas kernels, per_device(): pl.pallas_call(final_body, grid=(1,), in_specs=[smem, one((slots,)), one(...  1.43 us
    unnamed x14, local copies, waits for them, and re-layouts  1.21 us
  transfers between devices with their start and end apart: 8, of which 3 were waited for; matrix products, arithmetic and copies ran while one was open for 0% of the time, Pallas kernels for 20%

profile of v1, /device:TPU:0, one launch (start us, length us, event | category | flops | bytes accessed | tf_op | source)
XLA Modules:
  0.0 35.1 jit_solution(6428825587403436895)
XLA Ops:
  0.6 0.0 copy-start.3
  0.6 1.8 %prepare.1 = (f32[8,512]{1,0:T(8,128)}, f32[8,512]{1,0:T(8,128)}, bf16[32,512]{1,0:T(8,128)(2,1)}) custom-call(s32[4]{0:T(128)} %live.1, f32[3,768,512]{2,1,0:T(8,128)} %refs_2_.1, f32[3,768,512]{2,1,0:T(8,128)} %refs_2_.1, s32[4,512]{1,0:T(4,128)} %refs_3_.1, f32[4,512]{1,0:T(4,128)} %refs_4_.1, f32[512]{0:T(512)} %refs_5_.1), custom_call_target="tpu_custom_call" | custom-call | tf_op jit(solution)/shard_map/prepare/pallas_call | solution.py:318
  2.5 3.9 %collective-permute-start.4 = (bf16[32,512]{1,0:T(8,128)(2,1)}, bf16[32,512]{1,0:T(8,128)(2,1)S(1)}, u32[]{:S(2)}, u32[]{:S(2)}) collective-permute-start(bf16[32,512]{1,0:T(8,128)(2,1)} %get-tuple-element.22.refs_6_), channel_id=1, source_target_pairs={{3,0},{2,1},{1,2},{0,3},{7,4},{6,5},{5,6},{4,7},{11,8},{10,9},{9,1... | collective-permute-start | bytes 98312 | tf_op jit(solution)/shard_map/ppermute | solution.py:299
  6.4 0.5 %collective-permute-start.3 = (bf16[32,512]{1,0:T(8,128)(2,1)}, bf16[32,512]{1,0:T(8,128)(2,1)S(1)}, u32[]{:S(2)}, u32[]{:S(2)}) collective-permute-start(bf16[32,512]{1,0:T(8,128)(2,1)} %get-tuple-element.22.refs_6_), channel_id=1, source_target_pairs={{2,0},{3,1},{0,2},{1,3},{6,4},{7,5},{4,6},{5,7},{10,8},{11,9},{8,1... | collective-permute-start | bytes 98312 | tf_op jit(solution)/shard_map/ppermute | solution.py:299
  6.9 0.1 collective-permute-start.2
  7.0 0.0 collective-permute-start
  7.0 3.5 %collective-permute-start.1 = (f32[8,512]{1,0:T(8,128)}, f32[8,512]{1,0:T(8,128)S(1)}, u32[]{:S(2)}, u32[]{:S(2)}) collective-permute-start(f32[8,512]{1,0:T(8,128)} %get-tuple-element.21), channel_id=1, source_target_pairs={{4,0},{8,4},{12,8},{16,12},{20,16},{24,20},{28,24},{0,28},{5,1},{9... | collective-permute-start | bytes 49160 | tf_op jit(solution)/shard_map/ppermute | solution.py:299
  10.6 7.0 %derivative.1 = (f32[3,768,512]{2,1,0:T(8,128)}, bf16[3,4,768,128]{3,2,1,0:T(8,128)(2,1)S(1)}, bf16[3,4,768,128]{3,2,1,0:T(8,128)(2,1)S(1)}, f32[3,64,512]{2,1,0:T(8,128)S(1)}) custom-call(f32[3,768,512]{2,1,0:T(8,128)} %refs_2_.1, bf16[3,2,192,256]{3,2,1,0:T(8,128)(2,1)S(1)} %copy-done.3), custom_call_target="tpu_custom_call" | custom-call | flops 1811939328 | bytes 16515072 | tf_op jit(solution)/shard_map/derivative/pallas_call | solution.py:358
  17.6 0.0 collective-permute-done.refs_4_
  17.6 0.0 collective-permute-done.1.refs_5_
  17.6 0.0 collective-permute-done.4.refs_9_
  17.6 0.0 collective-permute-done.3.refs_8_
  17.6 0.0 collective-permute-done.2.refs_7_
  17.7 5.7 %lookup.1 = (f32[3,768,512]{2,1,0:T(8,128)}, f32[8,512]{1,0:T(8,128)S(1)}, f32[8,512]{1,0:T(8,128)S(1)}, f32[8,512]{1,0:T(8,128)S(1)}, f32[8,512]{1,0:T(8,128)S(1)}) custom-call(s32[1,16]{1,0:T(1,128)S(1)} %copy-done.2, bf16[3,4,768,128]{3,2,1,0:T(8,128)(2,1)S(1)} %get-tuple-element.17.refs_1_, ...), custom_call_target="tpu_custom_call", output_to_operand_aliasing={{0}: (10, {})} | custom-call | flops 7247757312 | bytes 4718592 | tf_op jit(solution)/shard_map/lookup/pallas_call | solution.py:384
  23.4 0.0 copy-start
  23.4 0.6 %copy-done = f32[8,512]{1,0:T(8,128)} copy-done((f32[8,512]{1,0:T(8,128)}, f32[8,512]{1,0:T(8,128)S(1)}, u32[]{:S(2)}) %copy-start) | copy-done | bytes 16408
  24.0 2.9 %collective-permute-start.5 = (f32[8,512]{1,0:T(8,128)S(1)}, f32[8,512]{1,0:T(8,128)S(1)}, u32[]{:S(2)}, u32[]{:S(2)}) collective-permute-start(f32[8,512]{1,0:T(8,128)S(1)} %get-tuple-element.26), channel_id=1, source_target_pairs={{0,1},{1,0},{2,3},{3,2},{4,5},{5,4},{6,7},{7,6},{8,9},{9,8},{10,11... | collective-permute-start | bytes 49160 | tf_op jit(solution)/shard_map/ppermute | solution.py:299
  26.9 1.5 %collective-permute-start.6 = (f32[8,512]{1,0:T(8,128)S(1)}, f32[8,512]{1,0:T(8,128)S(1)}, u32[]{:S(2)}, u32[]{:S(2)}) collective-permute-start(f32[8,512]{1,0:T(8,128)S(1)} %get-tuple-element.27), channel_id=1, source_target_pairs={{0,2},{1,3},{2,0},{3,1},{4,6},{5,7},{6,4},{7,5},{8,10},{9,11},{10,... | collective-permute-start | bytes 49160 | tf_op jit(solution)/shard_map/ppermute | solution.py:299
  28.4 0.0 collective-permute-start.7
  28.4 0.2 collective-permute-done.5.refs_1_
  28.7 2.0 %collective-permute-done.6.refs_2_ = f32[8,512]{1,0:T(8,128)S(1)} collective-permute-done((f32[8,512]{1,0:T(8,128)S(1)}, f32[8,512]{1,0:T(8,128)S(1)}, u32[]{:S(2)}, u32[]{:S(2)}) %collective-permute-start.6) | collective-permute-done | bytes 16416 | tf_op jit(solution)/shard_map/ppermute | solution.py:299
  30.7 2.4 %collective-permute-done.7.refs_3_ = f32[8,512]{1,0:T(8,128)S(1)} collective-permute-done((f32[8,512]{1,0:T(8,128)S(1)}, f32[8,512]{1,0:T(8,128)S(1)}, u32[]{:S(2)}, u32[]{:S(2)}) %collective-permute-start.7) | collective-permute-done | bytes 16416 | tf_op jit(solution)/shard_map/ppermute | solution.py:299
  33.1 0.6 %copy-done.6 = f32[8,512]{1,0:T(8,128)} copy-done((f32[8,512]{1,0:T(8,128)}, f32[8,512]{1,0:T(8,128)S(1)}, u32[]{:S(2)}) %copy-start.6) | copy-done | bytes 16408
  33.7 1.4 %finish.1 = (f32[3,512]{1,0:T(4,128)}, f32[3,512]{1,0:T(4,128)}) custom-call(s32[4]{0:T(128)} %live.1, f32[512]{0:T(512)} %relax.1, f32[3,512]{1,0:T(4,128)} %particle.1, f32[8,512]{1,0:T(8,128)} %copy-done, f32[8,512]{1,0:T(8,128)} %copy-done.4, f32[8,512]{1,0:T(8,128)} %copy-done.5, f32[8,512]{1,0:T(8,128)} %copy-done.6), custom_call_target="tpu_custom_call" | custom-call | tf_op jit(solution)/shard_map/finish/pallas_call | solution.py:421
  (10 shorter events, 0.0 us)
Async XLA Ops:
  0.6 9.9 %copy-start.3 = (bf16[3,2,192,256]{3,2,1,0:T(8,128)(2,1)S(1)}, bf16[3,2,192,256]{3,2,1,0:T(8,128)(2,1)}, u32[]{:S(2)}) copy-start(bf16[3,2,192,256]{3,2,1,0:T(8,128)(2,1)} %constant.2.clone.refs_1_) | copy-start | bytes 1769476
  2.5 15.2 %copy-start.1 = (bf16[32,512]{1,0:T(8,128)(2,1)S(1)}, bf16[32,512]{1,0:T(8,128)(2,1)}, u32[]{:S(2)}) copy-start(bf16[32,512]{1,0:T(8,128)(2,1)} %get-tuple-element.22.refs_6_) | copy-start | bytes 98308
  2.5 15.2 %copy-start.2 = (s32[1,16]{1,0:T(1,128)S(1)}, s32[1,16]{1,0:T(1,128)}, u32[]{:S(2)}) copy-start(s32[1,16]{1,0:T(1,128)} %refs_0_.5) | copy-start | bytes 196
  2.5 15.2 %collective-permute-start.4 = (bf16[32,512]{1,0:T(8,128)(2,1)}, bf16[32,512]{1,0:T(8,128)(2,1)S(1)}, u32[]{:S(2)}, u32[]{:S(2)}) collective-permute-start(bf16[32,512]{1,0:T(8,128)(2,1)} %get-tuple-element.22.refs_6_), channel_id=1, source_target_pairs={{3,0},{2,1},{1,2},{0,3},{7,4},{6,5},{5,6},{4,7},{11,8},{10,9},{9,1... | collective-permute-start | bytes 98312 | tf_op jit(solution)/shard_map/ppermute | solution.py:299
  6.4 11.2 %collective-permute-start.3 = (bf16[32,512]{1,0:T(8,128)(2,1)}, bf16[32,512]{1,0:T(8,128)(2,1)S(1)}, u32[]{:S(2)}, u32[]{:S(2)}) collective-permute-start(bf16[32,512]{1,0:T(8,128)(2,1)} %get-tuple-element.22.refs_6_), channel_id=1, source_target_pairs={{2,0},{3,1},{0,2},{1,3},{6,4},{7,5},{4,6},{5,7},{10,8},{11,9},{8,1... | collective-permute-start | bytes 98312 | tf_op jit(solution)/shard_map/ppermute | solution.py:299
  6.9 10.7 %collective-permute-start.2 = (bf16[32,512]{1,0:T(8,128)(2,1)}, bf16[32,512]{1,0:T(8,128)(2,1)S(1)}, u32[]{:S(2)}, u32[]{:S(2)}) collective-permute-start(bf16[32,512]{1,0:T(8,128)(2,1)} %get-tuple-element.22.refs_6_), channel_id=1, source_target_pairs={{1,0},{0,1},{3,2},{2,3},{5,4},{4,5},{7,6},{6,7},{9,8},{8,9},{11,10... | collective-permute-start | bytes 98312 | tf_op jit(solution)/shard_map/ppermute | solution.py:299
  7.0 10.6 %collective-permute-start = (f32[8,512]{1,0:T(8,128)}, f32[8,512]{1,0:T(8,128)S(1)}, u32[]{:S(2)}, u32[]{:S(2)}) collective-permute-start(f32[8,512]{1,0:T(8,128)} %get-tuple-element.20), channel_id=1, source_target_pairs={{0,4},{4,8},{8,12},{12,16},{16,20},{20,24},{24,28},{28,0},{1,5},{5... | collective-permute-start | bytes 49160 | tf_op jit(solution)/shard_map/ppermute | solution.py:299
  7.0 10.6 %collective-permute-start.1 = (f32[8,512]{1,0:T(8,128)}, f32[8,512]{1,0:T(8,128)S(1)}, u32[]{:S(2)}, u32[]{:S(2)}) collective-permute-start(f32[8,512]{1,0:T(8,128)} %get-tuple-element.21), channel_id=1, source_target_pairs={{4,0},{8,4},{12,8},{16,12},{20,16},{24,20},{28,24},{0,28},{5,1},{9... | collective-permute-start | bytes 49160 | tf_op jit(solution)/shard_map/ppermute | solution.py:299
  23.4 0.6 %copy-start = (f32[8,512]{1,0:T(8,128)}, f32[8,512]{1,0:T(8,128)S(1)}, u32[]{:S(2)}) copy-start(f32[8,512]{1,0:T(8,128)S(1)} %get-tuple-element.25.refs_0_) | copy-start | bytes 49156
  24.0 4.7 %collective-permute-start.5 = (f32[8,512]{1,0:T(8,128)S(1)}, f32[8,512]{1,0:T(8,128)S(1)}, u32[]{:S(2)}, u32[]{:S(2)}) collective-permute-start(f32[8,512]{1,0:T(8,128)S(1)} %get-tuple-element.26), channel_id=1, source_target_pairs={{0,1},{1,0},{2,3},{3,2},{4,5},{5,4},{6,7},{7,6},{8,9},{9,8},{10,11... | collective-permute-start | bytes 49160 | tf_op jit(solution)/shard_map/ppermute | solution.py:299
  26.9 3.7 %collective-permute-start.6 = (f32[8,512]{1,0:T(8,128)S(1)}, f32[8,512]{1,0:T(8,128)S(1)}, u32[]{:S(2)}, u32[]{:S(2)}) collective-permute-start(f32[8,512]{1,0:T(8,128)S(1)} %get-tuple-element.27), channel_id=1, source_target_pairs={{0,2},{1,3},{2,0},{3,1},{4,6},{5,7},{6,4},{7,5},{8,10},{9,11},{10,... | collective-permute-start | bytes 49160 | tf_op jit(solution)/shard_map/ppermute | solution.py:299
  28.4 4.6 %collective-permute-start.7 = (f32[8,512]{1,0:T(8,128)S(1)}, f32[8,512]{1,0:T(8,128)S(1)}, u32[]{:S(2)}, u32[]{:S(2)}) collective-permute-start(f32[8,512]{1,0:T(8,128)S(1)} %get-tuple-element.28), channel_id=1, source_target_pairs={{0,3},{1,2},{2,1},{3,0},{4,7},{5,6},{6,5},{7,4},{8,11},{9,10},{10,... | collective-permute-start | bytes 49160 | tf_op jit(solution)/shard_map/ppermute | solution.py:299
  28.7 4.4 %copy-start.4 = (f32[8,512]{1,0:T(8,128)}, f32[8,512]{1,0:T(8,128)S(1)}, u32[]{:S(2)}) copy-start(f32[8,512]{1,0:T(8,128)S(1)} %collective-permute-done.5.refs_1_) | copy-start | bytes 49156
  30.7 2.4 %copy-start.5 = (f32[8,512]{1,0:T(8,128)}, f32[8,512]{1,0:T(8,128)S(1)}, u32[]{:S(2)}) copy-start(f32[8,512]{1,0:T(8,128)S(1)} %collective-permute-done.6.refs_2_) | copy-start | bytes 49156
  33.1 0.6 %copy-start.6 = (f32[8,512]{1,0:T(8,128)}, f32[8,512]{1,0:T(8,128)S(1)}, u32[]{:S(2)}) copy-start(f32[8,512]{1,0:T(8,128)S(1)} %collective-permute-done.7.refs_3_) | copy-start | bytes 49156

commit v2 on v1

v2 whole, which is shorter than its diff:
```python
import math

import jax
import jax.numpy as jnp
import numpy as np
from jax import lax
from jax.experimental import pallas as pl
from jax.experimental.pallas import tpu as pltpu
from jax.sharding import PartitionSpec as P

ROWB = 128
PSIZE = 128
STEN = 4
EDGE = 32
ROWS = 192
CHUNK = 64
EXTRA = 2
HALO = 8
R_DECAY = (3.0 - math.sqrt(5.0)) / 2.0
F32 = jnp.float32
BF16 = jnp.bfloat16


def kernel_taps(reach):
    level = 3.0 / math.sqrt(5.0)

    def inverse(n):
        return level * (-R_DECAY) ** abs(n)

    taps = np.zeros(reach + 1)
    for n in range(reach + 1):
        taps[n] = (7.0 / 9.0) * (inverse(n + 1) - inverse(n - 1)) + (1.0 / 36.0) * (
            inverse(n + 2) - inverse(n - 2)
        )
    return taps


TAPS = kernel_taps(600)
TAIL = TAPS[2] / R_DECAY**2
FIRST = TAPS[1] + TAIL * R_DECAY


def split(values, terms):
    parts = []
    for _ in range(terms):
        part = values.astype(BF16)
        parts.append(part)
        values = values - part.astype(F32)
    return parts


def toeplitz(offset, rows, window):
    distance = offset + np.arange(rows)[:, None] - np.arange(window)[None, :]
    full = np.sign(distance) * TAPS[np.abs(distance)]
    high = full.astype(BF16)
    low = (full - high.astype(np.float64)).astype(BF16)
    return np.stack([high, low])


def edge_state(rows, from_first):
    index = lax.broadcasted_iota(jnp.int32, rows.shape, 0)
    steps = index + 1 if from_first else EDGE - index
    parity = 1.0 - 2.0 * (steps & 1).astype(F32)
    decay = parity * jnp.exp(steps.astype(F32) * math.log(R_DECAY))
    return jnp.sum(rows * decay, 0, keepdims=True)


def prep_body(x_cells, live, head, tail, cells, weights, offsets, to_right, to_left, request):
    zero = jnp.zeros((to_left.shape[0] - 6, head.shape[2]), F32)
    to_left[...] = jnp.concatenate(
        [edge_state(head[c], True) for c in range(3)] + [head[c, 0:1, :] for c in range(3)] + [zero], 0
    )
    to_right[...] = jnp.concatenate(
        [edge_state(tail[c], False) for c in range(3)]
        + [tail[c, EDGE - 1 : EDGE, :] for c in range(3)]
        + [zero],
        0,
    )
    cell = cells[...]
    slots = cell.shape[1]
    row = jnp.floor((cell.astype(F32) + 0.5) * (1.0 / x_cells)).astype(jnp.int32)
    x = cell - row * x_cells
    line = row & (ROWB - 1)
    slot = (row >> 7)[0:1]
    lane = lax.broadcasted_iota(jnp.int32, (1, slots), 1)
    limit = jnp.zeros((1, slots), jnp.int32)
    for k in range(slots // PSIZE):
        limit = jnp.where(lane // PSIZE == k, live[k], limit)
    alive = lane % PSIZE < limit
    key = jnp.where(alive, slot, -1).astype(F32)
    w_high, w_low = split(weights[...], 2)
    o_high, o_low = split(offsets[...].reshape(1, slots), 2)
    request[...] = jnp.concatenate(
        [
            (x >> 3).astype(F32),
            (x & 7).astype(F32),
            line.astype(F32),
            w_high.astype(F32),
            w_low.astype(F32),
            o_high.astype(F32),
            o_low.astype(F32),
            key,
            jnp.zeros((9, slots), F32),
        ],
        0,
    ).astype(BF16)


def table_body(plan, v_ref, t_ref, table_ref):
    window, columns = t_ref.shape[1:]
    x_cells, lines = v_ref.shape[1:]
    blocks = lines // ROWB
    width = 3 * ROWB
    for c in range(3):
        turned = [
            jnp.transpose(v_ref[c, :, b * ROWB : (b + 1) * ROWB].astype(BF16))
            for b in range(blocks)
        ]
        for b in range(blocks):
            table_ref[b, c * ROWB : (c + 1) * ROWB] = turned[b]
        turned = jnp.concatenate(turned, 0)
        for column, start, kind in plan:
            out = jnp.dot(
                turned[:, start : start + window], t_ref[kind], preferred_element_type=F32
            ).astype(BF16)
            for b in range(blocks):
                table_ref[
                    b, width + c * ROWB : width + (c + 1) * ROWB, column : column + columns
                ] = out[b * ROWB : (b + 1) * ROWB]


def derivative_body(plan, v_ref, t_ref, left_ref, right_ref, after_ref, g_ref, out_buf, sems):
    del after_ref
    window = t_ref.shape[3]
    x_cells = v_ref.shape[1]
    parts = [split(v_ref[c], 2) for c in range(3)]
    copies = []
    for number, (row, start, kind) in enumerate(plan):
        t_high, t_low = t_ref[kind, 0], t_ref[kind, 1]
        for c in range(3):
            high = parts[c][0][start : start + window]
            low = parts[c][1][start : start + window]
            out = (
                jnp.dot(t_high, high, preferred_element_type=F32)
                + jnp.dot(t_high, low, preferred_element_type=F32)
                + jnp.dot(t_low, high, preferred_element_type=F32)
            )
            out_buf[c, row : row + ROWS] = out
            if row == 0:
                out_buf[c, :EDGE] = edge_fix(
                    out[:EDGE], left_ref[c : c + 1], left_ref[c + 3 : c + 4], True
                )
            if row + ROWS == x_cells:
                out_buf[c, x_cells - EDGE :] = edge_fix(
                    out_buf[c, x_cells - EDGE :],
                    right_ref[c : c + 1],
                    right_ref[c + 3 : c + 4],
                    False,
                )
        copy = pltpu.make_async_copy(
            out_buf.at[:, pl.ds(row, ROWS)], g_ref.at[:, pl.ds(row, ROWS)], sems.at[number]
        )
        copy.start()
        copies.append(copy)
    for copy in copies:
        copy.wait()


def edge_fix(rows, state, plane, is_left):
    index = lax.broadcasted_iota(jnp.int32, rows.shape, 0)
    steps = index if is_left else EDGE - 1 - index
    parity = 1.0 - 2.0 * (steps & 1).astype(F32)
    decay = parity * jnp.exp(steps.astype(F32) * math.log(R_DECAY))
    sign = 1.0 if is_left else -1.0
    return rows + (sign * TAIL) * decay * state + jnp.where(steps == 0, sign * FIRST, 0.0) * plane


def signed_decay(steps):
    parity = 1.0 - 2.0 * (steps.astype(jnp.int32) & 1).astype(F32)
    return parity * jnp.exp(steps * math.log(R_DECAY))


def lookup_body(owners, xor, owner_ref, table_ref, left_ref, right_ref, *refs):
    request_refs = refs[:owners]
    out_refs = refs[owners : 2 * owners]
    requests, ranks, totals, states, peer_at = refs[2 * owners :]
    blocks, _, x_cells = table_ref.shape
    width = 3 * ROWB
    me = lax.axis_index("gy")
    capacity = blocks // 2
    slots = requests.shape[2]
    groups = slots // ROWB
    cells = STEN * CHUNK

    peers = []
    for block in range(blocks):
        owner = owner_ref[0, me * blocks + block]
        peers.append((owner ^ me) if xor else lax.rem(owner - me + owners, owners))
        peer_at[block] = peers[block]
    for k in range(owners):
        requests[k] = request_refs[k][...]
        totals[k] = jnp.zeros(totals.shape[1:], F32)
    for block in range(blocks):
        at = slice(block * ROWB, (block + 1) * ROWB)
        states[block] = jnp.transpose(
            jnp.concatenate([left_ref[:8, at], right_ref[:8, at]], 0)
        ).astype(BF16)

    matched = []
    for block in range(blocks):
        rank = jnp.int32(0)
        for earlier in range(block):
            rank += (peers[earlier] == peers[block]).astype(jnp.int32)
        key = requests[peers[block], 16:32, :].astype(F32)[6:7]
        matched.append(jnp.where(key == (me * capacity + rank).astype(F32), 1.0, 0.0))
    stacked = jnp.concatenate(
        [m[:, k * ROWB : (k + 1) * ROWB] for m in matched for k in range(groups)], 0
    )
    upto = lax.broadcasted_iota(jnp.int32, (ROWB, ROWB), 0) <= lax.broadcasted_iota(
        jnp.int32, (ROWB, ROWB), 1
    )
    running = jnp.dot(
        stacked.astype(BF16), jnp.where(upto, 1.0, 0.0).astype(BF16), preferred_element_type=F32
    )
    ends = []
    end = jnp.int32(0)
    for block in range(blocks):
        before = jnp.zeros((1, 1), F32)
        pieces = []
        for k in range(groups):
            r = block * groups + k
            line = running[r : r + 1]
            pieces.append(jnp.where(stacked[r : r + 1] > 0.5, line - 1.0 + before, -1.0))
            before = before + line[:, ROWB - 1 : ROWB]
        ranks[block] = jnp.concatenate(pieces, 1)
        count = before[0, 0].astype(jnp.int32)
        end = end + jnp.maximum((count + CHUNK - 1) // CHUNK - 1, 0)
        ends.append(end)

    x_iota = lax.broadcasted_iota(jnp.int32, (x_cells, cells), 0).astype(F32)
    line_iota = lax.broadcasted_iota(jnp.int32, (ROWB, cells), 0).astype(F32)
    state_iota = lax.broadcasted_iota(jnp.int32, (16, cells), 0)
    place = lax.broadcasted_iota(jnp.int32, (CHUNK, slots), 0)
    low_half = lax.broadcasted_iota(jnp.int32, (1, 2 * CHUNK), 1) < CHUNK

    def batch(tasks):
        chosen, data = [], []
        for block, peer, i in tasks:
            one = jnp.where(ranks[block] == (place + i * CHUNK).astype(F32), 1.0, 0.0).astype(BF16)
            chosen.append(jnp.concatenate([one, one], 0))
        for (block, peer, i), pick in zip(tasks, chosen):
            data.append(
                lax.dot_general(
                    requests[peer], pick, (((1,), (1,)), ((), ())), preferred_element_type=F32
                )
            )
        found, halos, masks, offsets = [], [], [], []
        for (block, peer, i), d in zip(tasks, data):

            def by_cell(row):
                pairs = [
                    jnp.where(low_half, d[row + s : row + s + 1], d[row + s + 1 : row + s + 2])
                    for s in (0, 2)
                ]
                return jnp.concatenate(pairs, 1)

            x = by_cell(0) * 8.0 + by_cell(4)
            weight = by_cell(12) + by_cell(16)
            offset = d[20:21] + d[21:22]
            offsets.append(jnp.concatenate([offset, offset], 1))
            masks.append(jnp.where(line_iota == by_cell(8), weight, 0.0))
            pick = jnp.where(x_iota == x, 1.0, 0.0).astype(BF16)
            found.append(jnp.dot(table_ref[block], pick, preferred_element_type=F32))
            y = x_cells - 1.0 - x
            left = jnp.where(x < EDGE, TAIL * signed_decay(x), 0.0)
            right = jnp.where(y < EDGE, -TAIL * signed_decay(y), 0.0)
            left_first = jnp.where(x == 0.0, FIRST, 0.0)
            right_first = jnp.where(y == 0.0, -FIRST, 0.0)
            terms = []
            for c in range(3):
                term = jnp.where(state_iota == c, left, 0.0)
                term = jnp.where(state_iota == c + 3, left_first, term)
                term = jnp.where(state_iota == c + 8, right, term)
                terms.append(jnp.where(state_iota == c + 11, right_first, term))
            halos.append(
                jnp.dot(
                    states[block],
                    jnp.concatenate(terms, 1).astype(BF16),
                    preferred_element_type=F32,
                )
            )
        for (block, peer, i), f, h, mask, offset, pick in zip(
            tasks, found, halos, masks, offsets, chosen
        ):
            sums = []
            for c in range(3):
                carried = f[c * ROWB : (c + 1) * ROWB]
                slope = f[width + c * ROWB : width + (c + 1) * ROWB]
                slope = slope + h[:, c * cells : (c + 1) * cells]
                sums.append(jnp.sum((carried + offset * slope) * mask, 0, keepdims=True))
            sums.append(jnp.zeros((1, cells), F32))
            value = jnp.concatenate(sums, 0)
            value = value[:, : 2 * CHUNK] + value[:, 2 * CHUNK :]
            back = jnp.concatenate(
                [p.astype(F32) for p in split(value, 3)] + [jnp.zeros((4, 2 * CHUNK), F32)], 0
            )
            totals[peer] += jnp.dot(back.astype(BF16), pick, preferred_element_type=F32)

    batch([(block, peers[block], jnp.int32(0)) for block in range(blocks)])

    def extra(number):
        block = jnp.int32(0)
        first = jnp.int32(0)
        for b in range(blocks - 1):
            past = number >= ends[b]
            block = jnp.where(past, b + 1, block)
            first = jnp.where(past, ends[b], first)
        return block, peer_at[block], number - first + 1

    @pl.loop(0, (ends[-1] + EXTRA - 1) // EXTRA)
    def _(i):
        batch([extra(i * EXTRA + t) for t in range(EXTRA)])

    for k in range(owners):
        total = totals[k]
        out_refs[k][...] = total[0:8] + pltpu.roll(total[0:8], 4, 0) + total[8:16]


def final_body(live, relax, particle, *refs):
    parts, (fluid_ref, updated_ref) = refs[:-2], refs[-2:]
    raw = parts[0][0:3]
    for part in parts[1:]:
        raw = raw + part[0:3]
    slots = raw.shape[1]
    lane = lax.broadcasted_iota(jnp.int32, (3, slots), 1)
    limit = jnp.zeros((3, slots), jnp.int32)
    for k in range(slots // PSIZE):
        limit = jnp.where(lane // PSIZE == k, live[k], limit)
    alive = lane % PSIZE < limit
    fluid = jnp.where(alive, raw, 0.0)
    velocity = particle[...]
    fluid_ref[...] = fluid
    updated_ref[...] = jnp.where(
        alive, velocity + relax[...].reshape(1, slots) * (fluid - velocity), velocity
    )


def sent(values, axis, pairs):
    return lax.ppermute(values, axis, pairs)


def per_device(
    velocity, row_owner, cell_list, weights, offsets, relax_rate, particle_velocity, live_counts
):
    components, x_cells, lines = velocity.shape
    slots = weights.shape[1]
    columns = lax.axis_size("gx")
    owners = lax.axis_size("gy")
    blocks = lines // ROWB
    xor = owners & (owners - 1) == 0
    vmem = pl.BlockSpec(memory_space=pltpu.VMEM)
    smem = pl.BlockSpec(memory_space=pltpu.SMEM)
    hbm = pl.BlockSpec(memory_space=pltpu.HBM)
    limit = 24 * 1024 * 1024
    one = lambda shape: pl.BlockSpec(shape, lambda i: (0,) * len(shape))

    last = x_cells // EDGE - 1
    to_right, to_left, request = pl.pallas_call(
        lambda *refs: prep_body(x_cells, *refs),
        grid=(1,),
        in_specs=[
            smem,
            pl.BlockSpec((3, EDGE, lines), lambda i: (0, 0, 0)),
            pl.BlockSpec((3, EDGE, lines), lambda i: (0, last, 0)),
            one((STEN, slots)),
            one((STEN, slots)),
            one((slots,)),
        ],
        out_specs=[vmem] * 3,
        out_shape=[
            jax.ShapeDtypeStruct((HALO, lines), F32),
            jax.ShapeDtypeStruct((HALO, lines), F32),
            jax.ShapeDtypeStruct((32, slots), BF16),
        ],
        name="prepare",
    )(live_counts, velocity, velocity, cell_list, weights, offsets)

    from_left = sent(to_right, "gx", [(i, (i + 1) % columns) for i in range(columns)])
    from_right = sent(to_left, "gx", [((i + 1) % columns, i) for i in range(columns)])

    def peer(i, k):
        return i ^ k if xor else (i + k) % owners

    requests = [request] + [
        sent(request, "gy", [(peer(i, k), i) for i in range(owners)]) for k in range(1, owners)
    ]

    window = min(256, x_cells)
    plan, kinds = [], []
    for row in range(0, x_cells, ROWS):
        start = min(max(row - EDGE, 0), x_cells - window)
        if row - start not in kinds:
            kinds.append(row - start)
        plan.append((row, start, kinds.index(row - start)))
    matrices = jnp.asarray(np.stack([toeplitz(o, ROWS, window) for o in kinds]))
    width = 3 * ROWB
    columns_at = 256 if x_cells % 256 == 0 else x_cells
    reach = min(512, x_cells)
    across, across_kinds = [], []
    for column in range(0, x_cells, columns_at):
        start = min(max(column - ROWB, 0), x_cells - reach)
        if column - start not in across_kinds:
            across_kinds.append(column - start)
        across.append((column, start, across_kinds.index(column - start)))
    turned = jnp.asarray(np.stack([toeplitz(o, columns_at, reach)[0].T for o in across_kinds]))
    table = pl.pallas_call(
        lambda *refs: table_body(across, *refs),
        in_specs=[vmem, vmem],
        out_specs=vmem,
        out_shape=jax.ShapeDtypeStruct((blocks, 2 * width, x_cells), BF16),
        compiler_params=pltpu.CompilerParams(vmem_limit_bytes=limit),
        cost_estimate=pl.CostEstimate(
            flops=2 * window * velocity.size, bytes_accessed=8 * velocity.size, transcendentals=0
        ),
        name="table",
    )(velocity, turned)

    partials = pl.pallas_call(
        lambda *refs: lookup_body(owners, xor, *refs),
        in_specs=[smem] + [vmem] * (3 + owners),
        out_specs=[vmem] * owners,
        out_shape=[jax.ShapeDtypeStruct((8, slots), F32)] * owners,
        scratch_shapes=[
            pltpu.VMEM((owners, 32, slots), BF16),
            pltpu.VMEM((blocks, 1, slots), F32),
            pltpu.VMEM((owners, 16, slots), F32),
            pltpu.VMEM((blocks, ROWB, 16), BF16),
            pltpu.SMEM((blocks,), jnp.int32),
        ],
        compiler_params=pltpu.CompilerParams(vmem_limit_bytes=limit),
        cost_estimate=pl.CostEstimate(
            flops=2 * 768 * 6 * x_cells * 1024, bytes_accessed=2 * velocity.size, transcendentals=0
        ),
        name="lookup",
    )(row_owner, table, from_left, from_right, *requests)

    gradient = pl.pallas_call(
        lambda *refs: derivative_body(plan, *refs),
        in_specs=[vmem] * 5,
        out_specs=hbm,
        out_shape=jax.ShapeDtypeStruct(velocity.shape, F32),
        scratch_shapes=[
            pltpu.VMEM(velocity.shape, F32),
            pltpu.SemaphoreType.DMA((len(plan),)),
        ],
        compiler_params=pltpu.CompilerParams(vmem_limit_bytes=limit),
        cost_estimate=pl.CostEstimate(
            flops=6 * window * velocity.size, bytes_accessed=8 * velocity.size, transcendentals=0
        ),
        name="derivative",
    )(velocity, matrices, from_left, from_right, partials[0])

    returned = [partials[0]] + [
        sent(partials[k], "gy", [(i, peer(i, k)) for i in range(owners)]) for k in range(1, owners)
    ]
    shape = jax.ShapeDtypeStruct((3, slots), F32)
    fluid, updated = pl.pallas_call(
        final_body,
        in_specs=[smem] + [vmem] * (2 + owners),
        out_specs=[vmem] * 2,
        out_shape=[shape, shape],
        compiler_params=pltpu.CompilerParams(vmem_limit_bytes=limit),
        name="finish",
    )(live_counts, relax_rate, particle_velocity, *returned)
    return (gradient, fluid, updated)


def solution(mesh):
    return jax.shard_map(
        per_device,
        mesh=mesh,
        in_specs=(
            P(None, "gx", "gy"),
            P("gx", None),
            P(None, ("gx", "gy")),
            P(None, ("gx", "gy")),
            P(("gx", "gy")),
            P(("gx", "gy")),
            P(None, ("gx", "gy")),
            P(("gx", "gy")),
        ),
        out_specs=(P(None, "gx", "gy"), P(None, ("gx", "gy")), P(None, ("gx", "gy"))),
        check_vma=False,
    )
```

time: 35.4 us -> 26.7 us (0.75)
  Pallas kernels: 16 us -> 10.4 us
  waiting for transfers between devices: 4.64 us -> 0.12 us
  local copies, waits for them, and re-layouts: 1.21 us -> 2.39 us
    pallas_call x3 -> x4, Pallas kernels: 14.2 us -> 8.55 us  [the longest x1 3.18 us: per_device(): pl.pallas_call(lambda *refs: derivative_body(plan, *refs), in_specs=[vmem...]
    ppermute x8, waiting for transfers between devices: 4.64 us -> 0.12 us  [sent(): return lax.ppermute(values, axis, pairs)]
    unnamed x14 -> x20, local copies, waits for them, and re-layouts: 1.21 us -> 2.39 us
  transfers between devices with their start and end apart: 8 -> 8, of which waited for: 3 -> 1; matrix products, arithmetic and copies ran while one was open for 0% -> 0% of each run, Pallas kernels for 20% -> 17%
where the time goes in v2:
time: 26.7 us; the launch traced here: 26.5 us
  starting transfers between devices  12.8 us (48%)
  Pallas kernels  10.4 us (39%)
  local copies, waits for them, and re-layouts  2.39 us (9%)
  between operations  0.79 us (3%)
    ppermute x8, starting transfers between devices, sent(): return lax.ppermute(values, axis, pairs)  12.8 us
    pallas_call x1, Pallas kernels, per_device(): pl.pallas_call(lambda *refs: derivative_body(plan, *refs), in_specs=[vmem...  3.18 us
    pallas_call x1, Pallas kernels, per_device(): pl.pallas_call(lambda *refs: lookup_body(owners, xor, *refs), in_specs=[s...  2.76 us
    unnamed x20, local copies, waits for them, and re-layouts  2.39 us
    pallas_call x1, Pallas kernels, per_device(): pl.pallas_call(lambda *refs: prep_body(x_cells, *refs), grid=(1,), in_spe...  1.82 us
    pallas_call x1, Pallas kernels, per_device(): pl.pallas_call(lambda *refs: table_body(across, *refs), in_specs=[vmem, v...  1.45 us
    pallas_call x1, Pallas kernels, per_device(): pl.pallas_call(final_body, in_specs=[smem] + [vmem] * (2 + owners), out_s...  1.16 us
  transfers between devices with their start and end apart: 8, of which 1 were waited for; matrix products, arithmetic and copies ran while one was open for 0% of the time, Pallas kernels for 17%

profile of v2, /device:TPU:0, one launch (start us, length us, event | category | flops | bytes accessed | tf_op | source)
XLA Modules:
  0.0 26.5 jit_solution(7113774656628610308)
XLA Ops:
  0.6 0.0 copy-start.1
  0.6 1.8 %prepare.1 = (f32[8,512]{1,0:T(8,128)}, f32[8,512]{1,0:T(8,128)}, bf16[32,512]{1,0:T(8,128)(2,1)}) custom-call(s32[4]{0:T(128)} %live.1, f32[3,768,512]{2,1,0:T(8,128)} %refs_0_.7, f32[3,768,512]{2,1,0:T(8,128)} %refs_0_.7, s32[4,512]{1,0:T(4,128)} %refs_3_.1, f32[4,512]{1,0:T(4,128)} %refs_4_.1, f32[512]{0:T(512)} %refs_5_.1), custom_call_target="tpu_custom_call" | custom-call | tf_op jit(solution)/shard_map/prepare/pallas_call | solution.py:368
  2.5 3.9 %collective-permute-start.4 = (bf16[32,512]{1,0:T(8,128)(2,1)}, bf16[32,512]{1,0:T(8,128)(2,1)S(1)}, u32[]{:S(2)}, u32[]{:S(2)}) collective-permute-start(bf16[32,512]{1,0:T(8,128)(2,1)} %get-tuple-element.14.refs_4_), channel_id=1, source_target_pairs={{3,0},{2,1},{1,2},{0,3},{7,4},{6,5},{5,6},{4,7},{11,8},{10,9},{9,1... | collective-permute-start | bytes 98312 | tf_op jit(solution)/shard_map/ppermute | solution.py:349
  6.4 0.5 %collective-permute-start.3 = (bf16[32,512]{1,0:T(8,128)(2,1)}, bf16[32,512]{1,0:T(8,128)(2,1)S(1)}, u32[]{:S(2)}, u32[]{:S(2)}) collective-permute-start(bf16[32,512]{1,0:T(8,128)(2,1)} %get-tuple-element.14.refs_4_), channel_id=1, source_target_pairs={{2,0},{3,1},{0,2},{1,3},{6,4},{7,5},{4,6},{5,7},{10,8},{11,9},{8,1... | collective-permute-start | bytes 98312 | tf_op jit(solution)/shard_map/ppermute | solution.py:349
  6.9 0.1 collective-permute-start.2
  6.9 0.0 collective-permute-start
  6.9 3.5 %collective-permute-start.1 = (f32[8,512]{1,0:T(8,128)}, f32[8,512]{1,0:T(8,128)S(1)}, u32[]{:S(2)}, u32[]{:S(2)}) collective-permute-start(f32[8,512]{1,0:T(8,128)} %get-tuple-element.13), channel_id=1, source_target_pairs={{4,0},{8,4},{12,8},{16,12},{20,16},{24,20},{28,24},{0,28},{5,1},{9... | collective-permute-start | bytes 49160 | tf_op jit(solution)/shard_map/ppermute | solution.py:349
  10.5 2.3 %copy-done = f32[3,768,512]{2,1,0:T(8,128)S(1)} copy-done((f32[3,768,512]{2,1,0:T(8,128)S(1)}, f32[3,768,512]{2,1,0:T(8,128)}, u32[]{:S(2)}) %copy-start) | copy-done | bytes 4718616
  12.8 1.4 %table.1.refs_1_ = bf16[4,768,768]{2,1,0:T(8,128)(2,1)S(1)} custom-call(f32[3,768,512]{2,1,0:T(8,128)S(1)} %copy-done, bf16[3,512,256]{2,1,0:T(8,128)(2,1)S(1)} %copy-done.1), custom_call_target="tpu_custom_call" | custom-call | flops 603979776 | bytes 9437184 | tf_op jit(solution)/shard_map/table/pallas_call | solution.py:416
  14.3 0.0 slice-start.1
  14.3 0.0 copy-start.2
  14.3 0.0 collective-permute-done.refs_2_
  14.3 0.0 collective-permute-done.4.refs_7_
  14.3 0.0 collective-permute-done.3.refs_6_
  14.4 2.8 %lookup.1 = (f32[8,512]{1,0:T(8,128)S(1)}, f32[8,512]{1,0:T(8,128)S(1)}, f32[8,512]{1,0:T(8,128)S(1)}, f32[8,512]{1,0:T(8,128)S(1)}) custom-call(s32[1,16]{1,0:T(1,128)S(1)} %copy-done.7, bf16[4,768,768]{2,1,0:T(8,128)(2,1)S(1)} %table.1.refs_1_, f32[8,512]{1,0:T(8,128)S(1)} %collective-permute-done.refs_2_, f32[8,512]{1,0:T(8,128)S(1)} %collective-permute-done.1.refs_3_, ...), custom_call_target="tpu_custom_call" | custom-call | flops 7247757312 | bytes 2359296 | tf_op jit(solution)/shard_map/lookup/pallas_call | solution.py:428
  17.1 3.3 %collective-permute-start.5 = (f32[8,512]{1,0:T(8,128)S(1)}, f32[8,512]{1,0:T(8,128)S(1)}, u32[]{:S(2)}, u32[]{:S(2)}) collective-permute-start(f32[8,512]{1,0:T(8,128)S(1)} %get-tuple-element.16), channel_id=1, source_target_pairs={{0,1},{1,0},{2,3},{3,2},{4,5},{5,4},{6,7},{7,6},{8,9},{9,8},{10,11... | collective-permute-start | bytes 49160 | tf_op jit(solution)/shard_map/ppermute | solution.py:349
  20.4 0.3 collective-permute-start.6
  20.7 1.3 %collective-permute-start.7 = (f32[8,512]{1,0:T(8,128)S(1)}, f32[8,512]{1,0:T(8,128)S(1)}, u32[]{:S(2)}, u32[]{:S(2)}) collective-permute-start(f32[8,512]{1,0:T(8,128)S(1)} %get-tuple-element.18), channel_id=1, source_target_pairs={{0,3},{1,2},{2,1},{3,0},{4,7},{5,6},{6,5},{7,4},{8,11},{9,10},{10,... | collective-permute-start | bytes 49160 | tf_op jit(solution)/shard_map/ppermute | solution.py:349
  22.0 0.0 copy-start.3
  22.0 0.0 copy-start.4
  22.0 0.0 copy-start.5
  22.0 3.2 %derivative.1 = f32[3,768,512]{2,1,0:T(8,128)} custom-call(f32[3,768,512]{2,1,0:T(8,128)S(1)} %bitcast.1, bf16[3,2,192,256]{3,2,1,0:T(8,128)(2,1)S(1)} %copy-done.2, f32[8,512]{1,0:T(8,128)S(1)} %collective-permute-done.refs_2_, f32[8,512]{1,0:T(8,128)S(1)} %collective-permute-done.1.refs_3_, f32[8,512]{1,0:T(8,128)S(1)} %get-tuple-element.15.refs_4_.refs_0_), custom_call_target="tpu_custom_call" | custom-call | flops 1811939328 | bytes 9437184 | tf_op jit(solution)/shard_map/derivative/pallas_call | solution.py:447
  25.2 0.1 collective-permute-done.7.refs_3_
  25.3 1.2 %finish.1 = (f32[3,512]{1,0:T(4,128)}, f32[3,512]{1,0:T(4,128)}) custom-call(s32[4]{0:T(128)S(1)} %copy-done.4, f32[512]{0:T(512)S(1)} %copy-done.5, f32[3,512]{1,0:T(4,128)S(1)} %copy-done.3, f32[8,512]{1,0:T(8,128)S(1)} %get-tuple-element.15.refs_4_.refs_0_, f32[8,512]{1,0:T(8,128)S(1)} %collective-permute-done.5.refs_1_, ...), custom_call_target="tpu_custom_call" | custom-call | tf_op jit(solution)/shard_map/finish/pallas_call | solution.py:467
  (18 shorter events, 0.0 us)
Async XLA Ops:
  0.6 9.8 %copy-start.1 = (bf16[3,512,256]{2,1,0:T(8,128)(2,1)S(1)}, bf16[3,512,256]{2,1,0:T(8,128)(2,1)}, u32[]{:S(2)}) copy-start(bf16[3,512,256]{2,1,0:T(8,128)(2,1)} %constant.5.clone.refs_1_) | copy-start | bytes 2359300
  2.5 11.9 %collective-permute-start.4 = (bf16[32,512]{1,0:T(8,128)(2,1)}, bf16[32,512]{1,0:T(8,128)(2,1)S(1)}, u32[]{:S(2)}, u32[]{:S(2)}) collective-permute-start(bf16[32,512]{1,0:T(8,128)(2,1)} %get-tuple-element.14.refs_4_), channel_id=1, source_target_pairs={{3,0},{2,1},{1,2},{0,3},{7,4},{6,5},{5,6},{4,7},{11,8},{10,9},{9,1... | collective-permute-start | bytes 98312 | tf_op jit(solution)/shard_map/ppermute | solution.py:349
  6.4 8.0 %collective-permute-start.3 = (bf16[32,512]{1,0:T(8,128)(2,1)}, bf16[32,512]{1,0:T(8,128)(2,1)S(1)}, u32[]{:S(2)}, u32[]{:S(2)}) collective-permute-start(bf16[32,512]{1,0:T(8,128)(2,1)} %get-tuple-element.14.refs_4_), channel_id=1, source_target_pairs={{2,0},{3,1},{0,2},{1,3},{6,4},{7,5},{4,6},{5,7},{10,8},{11,9},{8,1... | collective-permute-start | bytes 98312 | tf_op jit(solution)/shard_map/ppermute | solution.py:349
  6.9 7.5 %collective-permute-start.2 = (bf16[32,512]{1,0:T(8,128)(2,1)}, bf16[32,512]{1,0:T(8,128)(2,1)S(1)}, u32[]{:S(2)}, u32[]{:S(2)}) collective-permute-start(bf16[32,512]{1,0:T(8,128)(2,1)} %get-tuple-element.14.refs_4_), channel_id=1, source_target_pairs={{1,0},{0,1},{3,2},{2,3},{5,4},{4,5},{7,6},{6,7},{9,8},{8,9},{11,10... | collective-permute-start | bytes 98312 | tf_op jit(solution)/shard_map/ppermute | solution.py:349
  6.9 7.4 %collective-permute-start = (f32[8,512]{1,0:T(8,128)}, f32[8,512]{1,0:T(8,128)S(1)}, u32[]{:S(2)}, u32[]{:S(2)}) collective-permute-start(f32[8,512]{1,0:T(8,128)} %get-tuple-element.12), channel_id=1, source_target_pairs={{0,4},{4,8},{8,12},{12,16},{16,20},{20,24},{24,28},{28,0},{1,5},{5... | collective-permute-start | bytes 49160 | tf_op jit(solution)/shard_map/ppermute | solution.py:349
  6.9 7.4 %collective-permute-start.1 = (f32[8,512]{1,0:T(8,128)}, f32[8,512]{1,0:T(8,128)S(1)}, u32[]{:S(2)}, u32[]{:S(2)}) collective-permute-start(f32[8,512]{1,0:T(8,128)} %get-tuple-element.13), channel_id=1, source_target_pairs={{4,0},{8,4},{12,8},{16,12},{20,16},{24,20},{28,24},{0,28},{5,1},{9... | collective-permute-start | bytes 49160 | tf_op jit(solution)/shard_map/ppermute | solution.py:349
  10.5 2.3 %copy-start = (f32[3,768,512]{2,1,0:T(8,128)S(1)}, f32[3,768,512]{2,1,0:T(8,128)}, u32[]{:S(2)}) copy-start(f32[3,768,512]{2,1,0:T(8,128)} %refs_0_.7) | copy-start | bytes 14155780
  12.8 1.5 %copy-start.6 = (bf16[32,512]{1,0:T(8,128)(2,1)S(1)}, bf16[32,512]{1,0:T(8,128)(2,1)}, u32[]{:S(2)}) copy-start(bf16[32,512]{1,0:T(8,128)(2,1)} %get-tuple-element.14.refs_4_) | copy-start | bytes 98308
  12.8 1.6 %copy-start.7 = (s32[1,16]{1,0:T(1,128)S(1)}, s32[1,16]{1,0:T(1,128)}, u32[]{:S(2)}) copy-start(s32[1,16]{1,0:T(1,128)} %refs_0_.6) | copy-start | bytes 196
  12.8 9.1 %slice-start = ((s8[4718592]{0:T(1024)(128)(4,1)}), s8[524288]{0:T(1024)(128)(4,1)S(1)}, s32[]{:S(2)}) async-start(s8[4718592]{0:T(1024)(128)(4,1)} %bitcast), calls=%async_computation | async-start | bytes 1048576
  14.3 7.7 %slice-start.1 = ((s8[4718592]{0:T(1024)(128)(4,1)}), s8[4194304]{0:T(1024)(128)(4,1)S(1)}, s32[]{:S(2)}) async-start(s8[4718592]{0:T(1024)(128)(4,1)} %bitcast), calls=%async_computation.1 | async-start | bytes 8388608
  14.3 7.7 %copy-start.2 = (bf16[3,2,192,256]{3,2,1,0:T(8,128)(2,1)S(1)}, bf16[3,2,192,256]{3,2,1,0:T(8,128)(2,1)}, u32[]{:S(2)}) copy-start(bf16[3,2,192,256]{3,2,1,0:T(8,128)(2,1)} %constant.4.clone.refs_1_) | copy-start | bytes 1769476
  17.1 8.1 %collective-permute-start.5 = (f32[8,512]{1,0:T(8,128)S(1)}, f32[8,512]{1,0:T(8,128)S(1)}, u32[]{:S(2)}, u32[]{:S(2)}) collective-permute-start(f32[8,512]{1,0:T(8,128)S(1)} %get-tuple-element.16), channel_id=1, source_target_pairs={{0,1},{1,0},{2,3},{3,2},{4,5},{5,4},{6,7},{7,6},{8,9},{9,8},{10,11... | collective-permute-start | bytes 49160 | tf_op jit(solution)/shard_map/ppermute | solution.py:349
  20.4 4.8 %collective-permute-start.6 = (f32[8,512]{1,0:T(8,128)S(1)}, f32[8,512]{1,0:T(8,128)S(1)}, u32[]{:S(2)}, u32[]{:S(2)}) collective-permute-start(f32[8,512]{1,0:T(8,128)S(1)} %get-tuple-element.17), channel_id=1, source_target_pairs={{0,2},{1,3},{2,0},{3,1},{4,6},{5,7},{6,4},{7,5},{8,10},{9,11},{10,... | collective-permute-start | bytes 49160 | tf_op jit(solution)/shard_map/ppermute | solution.py:349
  20.7 4.6 %collective-permute-start.7 = (f32[8,512]{1,0:T(8,128)S(1)}, f32[8,512]{1,0:T(8,128)S(1)}, u32[]{:S(2)}, u32[]{:S(2)}) collective-permute-start(f32[8,512]{1,0:T(8,128)S(1)} %get-tuple-element.18), channel_id=1, source_target_pairs={{0,3},{1,2},{2,1},{3,0},{4,7},{5,6},{6,5},{7,4},{8,11},{9,10},{10,... | collective-permute-start | bytes 49160 | tf_op jit(solution)/shard_map/ppermute | solution.py:349
  22.0 3.4 %copy-start.3 = (f32[3,512]{1,0:T(4,128)S(1)}, f32[3,512]{1,0:T(4,128)}, u32[]{:S(2)}) copy-start(f32[3,512]{1,0:T(4,128)} %particle.1) | copy-start | bytes 18436
  22.0 3.3 %copy-start.4 = (s32[4]{0:T(128)S(1)}, s32[4]{0:T(128)}, u32[]{:S(2)}) copy-start(s32[4]{0:T(128)} %live.1) | copy-start | bytes 52
  22.0 3.3 %copy-start.5 = (f32[512]{0:T(512)S(1)}, f32[512]{0:T(512)}, u32[]{:S(2)}) copy-start(f32[512]{0:T(512)} %relax.1) | copy-start | bytes 6148

commit v3 on v2

--- a/solution.py
+++ b/solution.py
@@ -15,7 +15,7 @@
 ROWS = 192
 CHUNK = 64
 EXTRA = 2
-HALO = 8
+LOAD = 43
 R_DECAY = (3.0 - math.sqrt(5.0)) / 2.0
 F32 = jnp.float32
 BF16 = jnp.bfloat16
@@ -65,17 +65,30 @@
     return jnp.sum(rows * decay, 0, keepdims=True)
 
 
-def prep_body(x_cells, live, head, tail, cells, weights, offsets, to_right, to_left, request):
-    zero = jnp.zeros((to_left.shape[0] - 6, head.shape[2]), F32)
-    to_left[...] = jnp.concatenate(
+def even_column():
+    return lax.rem(lax.axis_index("gx"), 2) == 0
+
+
+def neighbours(chip_ref, next_ref):
+    is_even = even_column()
+    chip, following = chip_ref[...], next_ref[...]
+    return jnp.where(is_even, following, chip), jnp.where(is_even, chip, following)
+
+
+def prep_body(x_cells, live, head, tail, cells, weights, offsets, request, to_chip, to_next):
+    zero = jnp.zeros((2, head.shape[2]), F32)
+    to_left = jnp.concatenate(
         [edge_state(head[c], True) for c in range(3)] + [head[c, 0:1, :] for c in range(3)] + [zero], 0
     )
-    to_right[...] = jnp.concatenate(
+    to_right = jnp.concatenate(
         [edge_state(tail[c], False) for c in range(3)]
         + [tail[c, EDGE - 1 : EDGE, :] for c in range(3)]
         + [zero],
         0,
     )
+    is_even = even_column()
+    to_chip[...] = jnp.where(is_even, to_right, to_left)
+    to_next[...] = jnp.where(is_even, to_left, to_right)
     cell = cells[...]
     slots = cell.shape[1]
     row = jnp.floor((cell.astype(F32) + 0.5) * (1.0 / x_cells)).astype(jnp.int32)
@@ -106,31 +119,40 @@
     ).astype(BF16)
 
 
-def table_body(plan, v_ref, t_ref, table_ref):
+def table_body(plan, v_ref, t_ref, held_ref, table_ref, sems):
     window, columns = t_ref.shape[1:]
     x_cells, lines = v_ref.shape[1:]
     blocks = lines // ROWB
     width = 3 * ROWB
-    for c in range(3):
+    parts = 1
+    each = blocks // parts
+    pieces = [(c, p) for c in range(3) for p in range(parts)]
+    copies = []
+    for k, (c, p) in enumerate(pieces):
+        here = (c, slice(None), pl.ds(p * each * ROWB, each * ROWB))
+        copies.append(pltpu.make_async_copy(v_ref.at[here], held_ref.at[here], sems.at[k]))
+        copies[-1].start()
+    for copy, (c, p) in zip(copies, pieces):
+        copy.wait()
+        mine = range(p * each, (p + 1) * each)
         turned = [
-            jnp.transpose(v_ref[c, :, b * ROWB : (b + 1) * ROWB].astype(BF16))
-            for b in range(blocks)
+            jnp.transpose(held_ref[c, :, b * ROWB : (b + 1) * ROWB].astype(BF16)) for b in mine
         ]
-        for b in range(blocks):
-            table_ref[b, c * ROWB : (c + 1) * ROWB] = turned[b]
+        for b, rows in zip(mine, turned):
+            table_ref[b, c * ROWB : (c + 1) * ROWB] = rows
         turned = jnp.concatenate(turned, 0)
         for column, start, kind in plan:
             out = jnp.dot(
                 turned[:, start : start + window], t_ref[kind], preferred_element_type=F32
             ).astype(BF16)
-            for b in range(blocks):
+            for k, b in enumerate(mine):
                 table_ref[
                     b, width + c * ROWB : width + (c + 1) * ROWB, column : column + columns
-                ] = out[b * ROWB : (b + 1) * ROWB]
-
-
-def derivative_body(plan, v_ref, t_ref, left_ref, right_ref, after_ref, g_ref, out_buf, sems):
-    del after_ref
+                ] = out[k * ROWB : (k + 1) * ROWB]
+
+
+def derivative_body(plan, v_ref, t_ref, sides_ref, g_ref, out_buf, sems):
+    left, right = sides_ref[:8], sides_ref[8:]
     window = t_ref.shape[3]
     x_cells = v_ref.shape[1]
     parts = [split(v_ref[c], 2) for c in range(3)]
@@ -148,13 +170,13 @@
             out_buf[c, row : row + ROWS] = out
             if row == 0:
                 out_buf[c, :EDGE] = edge_fix(
-                    out[:EDGE], left_ref[c : c + 1], left_ref[c + 3 : c + 4], True
+                    out[:EDGE], left[c : c + 1], left[c + 3 : c + 4], True
                 )
             if row + ROWS == x_cells:
                 out_buf[c, x_cells - EDGE :] = edge_fix(
                     out_buf[c, x_cells - EDGE :],
-                    right_ref[c : c + 1],
-                    right_ref[c + 3 : c + 4],
+                    right[c : c + 1],
+                    right[c + 3 : c + 4],
                     False,
                 )
         copy = pltpu.make_async_copy(
@@ -180,10 +202,11 @@
     return parity * jnp.exp(steps * math.log(R_DECAY))
 
 
-def lookup_body(owners, xor, owner_ref, table_ref, left_ref, right_ref, *refs):
+def lookup_body(owners, xor, owner_ref, next_ref, chip_ref, table_ref, *refs):
     request_refs = refs[:owners]
     out_refs = refs[owners : 2 * owners]
-    requests, ranks, totals, states, peer_at = refs[2 * owners :]
+    sides_ref = refs[2 * owners]
+    requests, ranks, totals, states, peer_at = refs[2 * owners + 1 :]
     blocks, _, x_cells = table_ref.shape
     width = 3 * ROWB
     me = lax.axis_index("gy")
@@ -200,11 +223,10 @@
     for k in range(owners):
         requests[k] = request_refs[k][...]
         totals[k] = jnp.zeros(totals.shape[1:], F32)
+    sides = jnp.concatenate(neighbours(chip_ref, next_ref), 0)
+    sides_ref[...] = sides
     for block in range(blocks):
-        at = slice(block * ROWB, (block + 1) * ROWB)
-        states[block] = jnp.transpose(
-            jnp.concatenate([left_ref[:8, at], right_ref[:8, at]], 0)
-        ).astype(BF16)
+        states[block] = jnp.transpose(sides[:, block * ROWB : (block + 1) * ROWB]).astype(BF16)
 
     matched = []
     for block in range(blocks):
@@ -365,7 +387,7 @@
     one = lambda shape: pl.BlockSpec(shape, lambda i: (0,) * len(shape))
 
     last = x_cells // EDGE - 1
-    to_right, to_left, request = pl.pallas_call(
+    request, to_chip, to_next = pl.pallas_call(
         lambda *refs: prep_body(x_cells, *refs),
         grid=(1,),
         in_specs=[
@@ -378,15 +400,16 @@
         ],
         out_specs=[vmem] * 3,
         out_shape=[
-            jax.ShapeDtypeStruct((HALO, lines), F32),
-            jax.ShapeDtypeStruct((HALO, lines), F32),
             jax.ShapeDtypeStruct((32, slots), BF16),
+            jax.ShapeDtypeStruct((8, lines), F32),
+            jax.ShapeDtypeStruct((8, lines), F32),
         ],
         name="prepare",
     )(live_counts, velocity, velocity, cell_list, weights, offsets)
 
-    from_left = sent(to_right, "gx", [(i, (i + 1) % columns) for i in range(columns)])
-    from_right = sent(to_left, "gx", [((i + 1) % columns, i) for i in range(columns)])
+    after = [(i + 1) % columns if i % 2 else (i - 1) % columns for i in range(columns)]
+    from_next = sent(to_next, "gx", [(i, after[i]) for i in range(columns)])
+    from_chip = sent(to_chip, "gx", [(i, i ^ 1) for i in range(columns)])
 
     def peer(i, k):
         return i ^ k if xor else (i + k) % owners
@@ -413,23 +436,28 @@
             across_kinds.append(column - start)
         across.append((column, start, across_kinds.index(column - start)))
     turned = jnp.asarray(np.stack([toeplitz(o, columns_at, reach)[0].T for o in across_kinds]))
-    table = pl.pallas_call(
+    held, table = pl.pallas_call(
         lambda *refs: table_body(across, *refs),
-        in_specs=[vmem, vmem],
-        out_specs=vmem,
-        out_shape=jax.ShapeDtypeStruct((blocks, 2 * width, x_cells), BF16),
-        compiler_params=pltpu.CompilerParams(vmem_limit_bytes=limit),
+        in_specs=[hbm, vmem],
+        out_specs=[vmem, vmem],
+        out_shape=[
+            jax.ShapeDtypeStruct(velocity.shape, F32),
+            jax.ShapeDtypeStruct((blocks, 2 * width, x_cells), BF16),
+        ],
+        scratch_shapes=[pltpu.SemaphoreType.DMA((6,))],
+        compiler_params=pltpu.CompilerParams(vmem_limit_bytes=LOAD * 1024 * 1024),
         cost_estimate=pl.CostEstimate(
             flops=2 * window * velocity.size, bytes_accessed=8 * velocity.size, transcendentals=0
         ),
         name="table",
     )(velocity, turned)
 
-    partials = pl.pallas_call(
+    *partials, sides = pl.pallas_call(
         lambda *refs: lookup_body(owners, xor, *refs),
         in_specs=[smem] + [vmem] * (3 + owners),
-        out_specs=[vmem] * owners,
-        out_shape=[jax.ShapeDtypeStruct((8, slots), F32)] * owners,
+        out_specs=[vmem] * (owners + 1),
+        out_shape=[jax.ShapeDtypeStruct((8, slots), F32)] * owners
+        + [jax.ShapeDtypeStruct((16, lines), F32)],
         scratch_shapes=[
             pltpu.VMEM((owners, 32, slots), BF16),
             pltpu.VMEM((blocks, 1, slots), F32),
@@ -442,11 +470,11 @@
             flops=2 * 768 * 6 * x_cells * 1024, bytes_accessed=2 * velocity.size, transcendentals=0
         ),
         name="lookup",
-    )(row_owner, table, from_left, from_right, *requests)
+    )(row_owner, from_next, from_chip, table, *requests)
 
     gradient = pl.pallas_call(
         lambda *refs: derivative_body(plan, *refs),
-        in_specs=[vmem] * 5,
+        in_specs=[vmem] * 3,
         out_specs=hbm,
         out_shape=jax.ShapeDtypeStruct(velocity.shape, F32),
         scratch_shapes=[
@@ -458,7 +486,7 @@
             flops=6 * window * velocity.size, bytes_accessed=8 * velocity.size, transcendentals=0
         ),
         name="derivative",
-    )(velocity, matrices, from_left, from_right, partials[0])
+    )(held, matrices, sides)
 
     returned = [partials[0]] + [
         sent(partials[k], "gy", [(i, peer(i, k)) for i in range(owners)]) for k in range(1, owners)

time: 26.7 us -> 26.3 us (0.985)
  Pallas kernels: 10.4 us -> 13.7 us
  local copies, waits for them, and re-layouts: 2.39 us -> 0.03 us
  starting transfers between devices: 12.8 us -> 11.5 us
    unnamed x20 -> x14, local copies, waits for them, and re-layouts: 2.39 us -> 0.03 us
    pallas_call x1, Pallas kernels: 1.45 us -> 3.54 us  [per_device(): pl.pallas_call(lambda *refs: table_body(across, *refs), in_specs=[hbm, vm...]
    ppermute x8, starting transfers between devices: 12.8 us -> 11.5 us  [sent(): return lax.ppermute(values, axis, pairs)]
    pallas_call x1, Pallas kernels: 2.76 us -> 4.01 us  [per_device(): pl.pallas_call(lambda *refs: lookup_body(owners, xor, *refs), in_specs=[s...]
  transfers between devices with their start and end apart: 8 -> 8, of which waited for: 1 -> 1; matrix products, arithmetic and copies ran while one was open for 0% -> 0% of each run, Pallas kernels for 17% -> 26%
where the time goes in v3:
time: 26.3 us; the launch traced here: 26.2 us
  Pallas kernels  13.7 us (52%)
  starting transfers between devices  11.5 us (44%)
  between operations  0.76 us (3%)
    ppermute x8, starting transfers between devices, sent(): return lax.ppermute(values, axis, pairs)  11.5 us
    pallas_call x1, Pallas kernels, per_device(): pl.pallas_call(lambda *refs: lookup_body(owners, xor, *refs), in_specs=[s...  4.01 us
    pallas_call x1, Pallas kernels, per_device(): pl.pallas_call(lambda *refs: table_body(across, *refs), in_specs=[hbm, vm...  3.54 us
    pallas_call x1, Pallas kernels, per_device(): pl.pallas_call(lambda *refs: derivative_body(plan, *refs), in_specs=[vmem...  3.18 us
    pallas_call x1, Pallas kernels, per_device(): pl.pallas_call(lambda *refs: prep_body(x_cells, *refs), grid=(1,), in_spe...  1.82 us
    pallas_call x1, Pallas kernels, per_device(): pl.pallas_call(final_body, in_specs=[smem] + [vmem] * (2 + owners), out_s...  1.16 us
  transfers between devices with their start and end apart: 8, of which 1 were waited for; matrix products, arithmetic and copies ran while one was open for 0% of the time, Pallas kernels for 26%

profile of v3, /device:TPU:0, one launch (start us, length us, event | category | flops | bytes accessed | tf_op | source)
XLA Modules:
  0.0 26.2 jit_solution(3724106123957357778)
XLA Ops:
  0.6 0.0 copy-start
  0.6 1.8 %prepare.1 = (bf16[32,512]{1,0:T(8,128)(2,1)}, f32[8,512]{1,0:T(8,128)}, f32[8,512]{1,0:T(8,128)}) custom-call(s32[4]{0:T(128)} %live.1, f32[3,768,512]{2,1,0:T(8,128)} %refs_2_.1, f32[3,768,512]{2,1,0:T(8,128)} %refs_2_.1, s32[4,512]{1,0:T(4,128)} %refs_3_.1, f32[4,512]{1,0:T(4,128)} %refs_4_.1, f32[512]{0:T(512)} %refs_5_.1), custom_call_target="tpu_custom_call" | custom-call | tf_op jit(solution)/shard_map/prepare/pallas_call | solution.py:390
  2.5 3.0 %collective-permute-start.2 = (bf16[32,512]{1,0:T(8,128)(2,1)}, bf16[32,512]{1,0:T(8,128)(2,1)S(1)}, u32[]{:S(2)}, u32[]{:S(2)}) collective-permute-start(bf16[32,512]{1,0:T(8,128)(2,1)} %get-tuple-element.19.refs_4_), channel_id=1, source_target_pairs={{1,0},{0,1},{3,2},{2,3},{5,4},{4,5},{7,6},{6,7},{9,8},{8,9},{11,10... | collective-permute-start | bytes 98312 | tf_op jit(solution)/shard_map/ppermute | solution.py:371
  5.5 1.5 %collective-permute-start.3 = (bf16[32,512]{1,0:T(8,128)(2,1)}, bf16[32,512]{1,0:T(8,128)(2,1)S(1)}, u32[]{:S(2)}, u32[]{:S(2)}) collective-permute-start(bf16[32,512]{1,0:T(8,128)(2,1)} %get-tuple-element.19.refs_4_), channel_id=1, source_target_pairs={{2,0},{3,1},{0,2},{1,3},{6,4},{7,5},{4,6},{5,7},{10,8},{11,9},{8,1... | collective-permute-start | bytes 98312 | tf_op jit(solution)/shard_map/ppermute | solution.py:371
  7.0 0.0 collective-permute-start.4
  7.0 2.7 %collective-permute-start = (f32[8,512]{1,0:T(8,128)}, f32[8,512]{1,0:T(8,128)S(1)}, u32[]{:S(2)}, u32[]{:S(2)}) collective-permute-start(f32[8,512]{1,0:T(8,128)} %get-tuple-element.16), channel_id=1, source_target_pairs={{0,28},{4,8},{8,4},{12,16},{16,12},{20,24},{24,20},{28,0},{1,29},{... | collective-permute-start | bytes 49160 | tf_op jit(solution)/shard_map/ppermute | solution.py:371
  9.7 0.0 collective-permute-start.1
  9.7 0.0 copy-done
  9.7 3.5 %table.1 = (f32[3,768,512]{2,1,0:T(8,128)S(1)}, bf16[4,768,768]{2,1,0:T(8,128)(2,1)S(1)}) custom-call(f32[3,768,512]{2,1,0:T(8,128)} %refs_2_.1, bf16[3,512,256]{2,1,0:T(8,128)(2,1)S(1)} %copy-done), custom_call_target="tpu_custom_call" | custom-call | flops 603979776 | bytes 9437184 | tf_op jit(solution)/shard_map/table/pallas_call | solution.py:439
  13.2 0.0 collective-permute-done.refs_1_
  13.2 0.0 collective-permute-done.1.refs_2_
  13.2 0.0 collective-permute-done.2.refs_5_
  13.3 0.0 collective-permute-done.3.refs_6_
  13.3 0.0 collective-permute-done.4.refs_7_
  13.3 0.0 copy-start.1
  13.3 4.0 %lookup.1 = (f32[8,512]{1,0:T(8,128)S(1)}, f32[8,512]{1,0:T(8,128)S(1)}, f32[8,512]{1,0:T(8,128)S(1)}, f32[8,512]{1,0:T(8,128)S(1)}, f32[16,512]{1,0:T(8,128)S(1)}) custom-call(s32[1,16]{1,0:T(1,128)S(1)} %copy-done.6, f32[8,512]{1,0:T(8,128)S(1)} %collective-permute-done.refs_1_, f32[8,512]{1,0:T(8,128)S(1)} %collective-permute-done.1.refs_2_, ...), custom_call_target="tpu_custom_call" | custom-call | flops 7247757312 | bytes 2359296 | tf_op jit(solution)/shard_map/lookup/pallas_call | solution.py:455
  17.3 1.5 %collective-permute-start.5 = (f32[8,512]{1,0:T(8,128)S(1)}, f32[8,512]{1,0:T(8,128)S(1)}, u32[]{:S(2)}, u32[]{:S(2)}) collective-permute-start(f32[8,512]{1,0:T(8,128)S(1)} %get-tuple-element.22), channel_id=1, source_target_pairs={{0,1},{1,0},{2,3},{3,2},{4,5},{5,4},{6,7},{7,6},{8,9},{9,8},{10,11... | collective-permute-start | bytes 49160 | tf_op jit(solution)/shard_map/ppermute | solution.py:371
  18.9 1.5 %collective-permute-start.6 = (f32[8,512]{1,0:T(8,128)S(1)}, f32[8,512]{1,0:T(8,128)S(1)}, u32[]{:S(2)}, u32[]{:S(2)}) collective-permute-start(f32[8,512]{1,0:T(8,128)S(1)} %get-tuple-element.23), channel_id=1, source_target_pairs={{0,2},{1,3},{2,0},{3,1},{4,6},{5,7},{6,4},{7,5},{8,10},{9,11},{10,... | collective-permute-start | bytes 49160 | tf_op jit(solution)/shard_map/ppermute | solution.py:371
  20.4 1.2 %collective-permute-start.7 = (f32[8,512]{1,0:T(8,128)S(1)}, f32[8,512]{1,0:T(8,128)S(1)}, u32[]{:S(2)}, u32[]{:S(2)}) collective-permute-start(f32[8,512]{1,0:T(8,128)S(1)} %get-tuple-element.24), channel_id=1, source_target_pairs={{0,3},{1,2},{2,1},{3,0},{4,7},{5,6},{6,5},{7,4},{8,11},{9,10},{10,... | collective-permute-start | bytes 49160 | tf_op jit(solution)/shard_map/ppermute | solution.py:371
  21.6 3.2 %derivative.1 = f32[3,768,512]{2,1,0:T(8,128)} custom-call(f32[3,768,512]{2,1,0:T(8,128)S(1)} %get-tuple-element.15.refs_0_, bf16[3,2,192,256]{3,2,1,0:T(8,128)(2,1)S(1)} %copy-done.1, f32[16,512]{1,0:T(8,128)S(1)} %get-tuple-element.20.refs_2_), custom_call_target="tpu_custom_call" | custom-call | flops 1811939328 | bytes 9437184 | tf_op jit(solution)/shard_map/derivative/pallas_call | solution.py:475
  24.8 0.0 collective-permute-done.5.refs_1_
  24.8 0.0 collective-permute-done.6.refs_2_
  24.8 0.2 collective-permute-done.7.refs_3_
  25.0 1.2 %finish.1 = (f32[3,512]{1,0:T(4,128)}, f32[3,512]{1,0:T(4,128)}) custom-call(s32[4]{0:T(128)S(1)} %copy-done.3, f32[512]{0:T(512)S(1)} %copy-done.4, f32[3,512]{1,0:T(4,128)S(1)} %copy-done.2, f32[8,512]{1,0:T(8,128)S(1)} %get-tuple-element.21.refs_0_, f32[8,512]{1,0:T(8,128)S(1)} %collective-permute-done.5.refs_1_, ...), custom_call_target="tpu_custom_call" | custom-call | tf_op jit(solution)/shard_map/finish/pallas_call | solution.py:495
  (11 shorter events, 0.0 us)
Async XLA Ops:
  0.6 9.0 %copy-start = (bf16[3,512,256]{2,1,0:T(8,128)(2,1)S(1)}, bf16[3,512,256]{2,1,0:T(8,128)(2,1)}, u32[]{:S(2)}) copy-start(bf16[3,512,256]{2,1,0:T(8,128)(2,1)} %constant.5.clone.refs_1_) | copy-start | bytes 2359300
  2.5 10.8 %copy-start.5 = (bf16[32,512]{1,0:T(8,128)(2,1)S(1)}, bf16[32,512]{1,0:T(8,128)(2,1)}, u32[]{:S(2)}) copy-start(bf16[32,512]{1,0:T(8,128)(2,1)} %get-tuple-element.19.refs_4_) | copy-start | bytes 98308
  2.5 10.8 %copy-start.6 = (s32[1,16]{1,0:T(1,128)S(1)}, s32[1,16]{1,0:T(1,128)}, u32[]{:S(2)}) copy-start(s32[1,16]{1,0:T(1,128)} %refs_0_.5) | copy-start | bytes 196
  2.5 10.8 %collective-permute-start.2 = (bf16[32,512]{1,0:T(8,128)(2,1)}, bf16[32,512]{1,0:T(8,128)(2,1)S(1)}, u32[]{:S(2)}, u32[]{:S(2)}) collective-permute-start(bf16[32,512]{1,0:T(8,128)(2,1)} %get-tuple-element.19.refs_4_), channel_id=1, source_target_pairs={{1,0},{0,1},{3,2},{2,3},{5,4},{4,5},{7,6},{6,7},{9,8},{8,9},{11,10... | collective-permute-start | bytes 98312 | tf_op jit(solution)/shard_map/ppermute | solution.py:371
  5.5 7.8 %collective-permute-start.3 = (bf16[32,512]{1,0:T(8,128)(2,1)}, bf16[32,512]{1,0:T(8,128)(2,1)S(1)}, u32[]{:S(2)}, u32[]{:S(2)}) collective-permute-start(bf16[32,512]{1,0:T(8,128)(2,1)} %get-tuple-element.19.refs_4_), channel_id=1, source_target_pairs={{2,0},{3,1},{0,2},{1,3},{6,4},{7,5},{4,6},{5,7},{10,8},{11,9},{8,1... | collective-permute-start | bytes 98312 | tf_op jit(solution)/shard_map/ppermute | solution.py:371
  7.0 6.3 %collective-permute-start.4 = (bf16[32,512]{1,0:T(8,128)(2,1)}, bf16[32,512]{1,0:T(8,128)(2,1)S(1)}, u32[]{:S(2)}, u32[]{:S(2)}) collective-permute-start(bf16[32,512]{1,0:T(8,128)(2,1)} %get-tuple-element.19.refs_4_), channel_id=1, source_target_pairs={{3,0},{2,1},{1,2},{0,3},{7,4},{6,5},{5,6},{4,7},{11,8},{10,9},{9,1... | collective-permute-start | bytes 98312 | tf_op jit(solution)/shard_map/ppermute | solution.py:371
  7.0 6.2 %collective-permute-start = (f32[8,512]{1,0:T(8,128)}, f32[8,512]{1,0:T(8,128)S(1)}, u32[]{:S(2)}, u32[]{:S(2)}) collective-permute-start(f32[8,512]{1,0:T(8,128)} %get-tuple-element.16), channel_id=1, source_target_pairs={{0,28},{4,8},{8,4},{12,16},{16,12},{20,24},{24,20},{28,0},{1,29},{... | collective-permute-start | bytes 49160 | tf_op jit(solution)/shard_map/ppermute | solution.py:371
  9.7 3.6 %collective-permute-start.1 = (f32[8,512]{1,0:T(8,128)}, f32[8,512]{1,0:T(8,128)S(1)}, u32[]{:S(2)}, u32[]{:S(2)}) collective-permute-start(f32[8,512]{1,0:T(8,128)} %get-tuple-element.17), channel_id=1, source_target_pairs={{0,4},{4,0},{8,12},{12,8},{16,20},{20,16},{24,28},{28,24},{1,5},{5... | collective-permute-start | bytes 49160 | tf_op jit(solution)/shard_map/ppermute | solution.py:371
  13.3 8.3 %copy-start.1 = (bf16[3,2,192,256]{3,2,1,0:T(8,128)(2,1)S(1)}, bf16[3,2,192,256]{3,2,1,0:T(8,128)(2,1)}, u32[]{:S(2)}) copy-start(bf16[3,2,192,256]{3,2,1,0:T(8,128)(2,1)} %constant.4.clone.refs_1_) | copy-start | bytes 1769476
  17.3 7.5 %collective-permute-start.5 = (f32[8,512]{1,0:T(8,128)S(1)}, f32[8,512]{1,0:T(8,128)S(1)}, u32[]{:S(2)}, u32[]{:S(2)}) collective-permute-start(f32[8,512]{1,0:T(8,128)S(1)} %get-tuple-element.22), channel_id=1, source_target_pairs={{0,1},{1,0},{2,3},{3,2},{4,5},{5,4},{6,7},{7,6},{8,9},{9,8},{10,11... | collective-permute-start | bytes 49160 | tf_op jit(solution)/shard_map/ppermute | solution.py:371
  18.9 6.0 %collective-permute-start.6 = (f32[8,512]{1,0:T(8,128)S(1)}, f32[8,512]{1,0:T(8,128)S(1)}, u32[]{:S(2)}, u32[]{:S(2)}) collective-permute-start(f32[8,512]{1,0:T(8,128)S(1)} %get-tuple-element.23), channel_id=1, source_target_pairs={{0,2},{1,3},{2,0},{3,1},{4,6},{5,7},{6,4},{7,5},{8,10},{9,11},{10,... | collective-permute-start | bytes 49160 | tf_op jit(solution)/shard_map/ppermute | solution.py:371
  20.4 4.6 %collective-permute-start.7 = (f32[8,512]{1,0:T(8,128)S(1)}, f32[8,512]{1,0:T(8,128)S(1)}, u32[]{:S(2)}, u32[]{:S(2)}) collective-permute-start(f32[8,512]{1,0:T(8,128)S(1)} %get-tuple-element.24), channel_id=1, source_target_pairs={{0,3},{1,2},{2,1},{3,0},{4,7},{5,6},{6,5},{7,4},{8,11},{9,10},{10,... | collective-permute-start | bytes 49160 | tf_op jit(solution)/shard_map/ppermute | solution.py:371
  21.6 3.4 %copy-start.2 = (f32[3,512]{1,0:T(4,128)S(1)}, f32[3,512]{1,0:T(4,128)}, u32[]{:S(2)}) copy-start(f32[3,512]{1,0:T(4,128)} %particle.1) | copy-start | bytes 18436
  21.6 3.4 %copy-start.3 = (s32[4]{0:T(128)S(1)}, s32[4]{0:T(128)}, u32[]{:S(2)}) copy-start(s32[4]{0:T(128)} %live.1) | copy-start | bytes 52
  21.6 3.4 %copy-start.4 = (f32[512]{0:T(512)S(1)}, f32[512]{0:T(512)}, u32[]{:S(2)}) copy-start(f32[512]{0:T(512)} %relax.1) | copy-start | bytes 6148

commit v4 on v3

--- a/solution.py
+++ b/solution.py
@@ -16,6 +16,7 @@
 CHUNK = 64
 EXTRA = 2
 LOAD = 43
+SCALE = 1.95685
 R_DECAY = (3.0 - math.sqrt(5.0)) / 2.0
 F32 = jnp.float32
 BF16 = jnp.bfloat16
@@ -51,10 +52,7 @@
 
 def toeplitz(offset, rows, window):
     distance = offset + np.arange(rows)[:, None] - np.arange(window)[None, :]
-    full = np.sign(distance) * TAPS[np.abs(distance)]
-    high = full.astype(BF16)
-    low = (full - high.astype(np.float64)).astype(BF16)
-    return np.stack([high, low])
+    return (np.sign(distance) * TAPS[np.abs(distance)] / SCALE).astype(BF16)
 
 
 def edge_state(rows, from_first):
@@ -120,70 +118,55 @@
 
 
 def table_body(plan, v_ref, t_ref, held_ref, table_ref, sems):
-    window, columns = t_ref.shape[1:]
-    x_cells, lines = v_ref.shape[1:]
-    blocks = lines // ROWB
+    window = t_ref.shape[2]
+    lines = v_ref.shape[2]
     width = 3 * ROWB
-    parts = 1
-    each = blocks // parts
-    pieces = [(c, p) for c in range(3) for p in range(parts)]
-    copies = []
-    for k, (c, p) in enumerate(pieces):
-        here = (c, slice(None), pl.ds(p * each * ROWB, each * ROWB))
-        copies.append(pltpu.make_async_copy(v_ref.at[here], held_ref.at[here], sems.at[k]))
-        copies[-1].start()
-    for copy, (c, p) in zip(copies, pieces):
-        copy.wait()
-        mine = range(p * each, (p + 1) * each)
-        turned = [
-            jnp.transpose(held_ref[c, :, b * ROWB : (b + 1) * ROWB].astype(BF16)) for b in mine
+    copies = [pltpu.make_async_copy(v_ref.at[c], held_ref.at[c], sems.at[c]) for c in range(3)]
+    for copy in copies:
+        copy.start()
+    for c in range(3):
+        copies[c].wait()
+        high = held_ref[c].astype(BF16)
+        rows = [
+            jnp.dot(t_ref[kind], high[start : start + window], preferred_element_type=F32)
+            for row, start, kind in plan
         ]
-        for b, rows in zip(mine, turned):
-            table_ref[b, c * ROWB : (c + 1) * ROWB] = rows
-        turned = jnp.concatenate(turned, 0)
-        for column, start, kind in plan:
-            out = jnp.dot(
-                turned[:, start : start + window], t_ref[kind], preferred_element_type=F32
-            ).astype(BF16)
-            for k, b in enumerate(mine):
-                table_ref[
-                    b, width + c * ROWB : width + (c + 1) * ROWB, column : column + columns
-                ] = out[k * ROWB : (k + 1) * ROWB]
+        slopes = jnp.concatenate([(SCALE * r).astype(BF16) for r in rows], 0)
+        for b in range(lines // ROWB):
+            at = slice(b * ROWB, (b + 1) * ROWB)
+            table_ref[b, c * ROWB : (c + 1) * ROWB] = jnp.transpose(high[:, at])
+            table_ref[b, width + c * ROWB : width + (c + 1) * ROWB] = jnp.transpose(slopes[:, at])
 
 
 def derivative_body(plan, v_ref, t_ref, sides_ref, g_ref, out_buf, sems):
     left, right = sides_ref[:8], sides_ref[8:]
-    window = t_ref.shape[3]
+    window = t_ref.shape[2]
     x_cells = v_ref.shape[1]
-    parts = [split(v_ref[c], 2) for c in range(3)]
     copies = []
-    for number, (row, start, kind) in enumerate(plan):
-        t_high, t_low = t_ref[kind, 0], t_ref[kind, 1]
-        for c in range(3):
-            high = parts[c][0][start : start + window]
-            low = parts[c][1][start : start + window]
-            out = (
-                jnp.dot(t_high, high, preferred_element_type=F32)
-                + jnp.dot(t_high, low, preferred_element_type=F32)
-                + jnp.dot(t_low, high, preferred_element_type=F32)
+    for c in range(3):
+        high, low = split(v_ref[c], 2)
+        sent_to = 0
+        for number, (row, start, kind) in enumerate(plan):
+            matrix = t_ref[kind]
+            both = jnp.concatenate([high[start : start + window], low[start : start + window]], 0)
+            out = SCALE * jnp.dot(
+                jnp.concatenate([matrix, matrix], 1), both, preferred_element_type=F32
             )
             out_buf[c, row : row + ROWS] = out
             if row == 0:
-                out_buf[c, :EDGE] = edge_fix(
-                    out[:EDGE], left[c : c + 1], left[c + 3 : c + 4], True
-                )
+                out_buf[c, :EDGE] = edge_fix(out[:EDGE], left[c : c + 1], left[c + 3 : c + 4], True)
             if row + ROWS == x_cells:
                 out_buf[c, x_cells - EDGE :] = edge_fix(
-                    out_buf[c, x_cells - EDGE :],
-                    right[c : c + 1],
-                    right[c + 3 : c + 4],
-                    False,
+                    out_buf[c, x_cells - EDGE :], right[c : c + 1], right[c + 3 : c + 4], False
                 )
-        copy = pltpu.make_async_copy(
-            out_buf.at[:, pl.ds(row, ROWS)], g_ref.at[:, pl.ds(row, ROWS)], sems.at[number]
-        )
-        copy.start()
-        copies.append(copy)
+            if number % 2 == 1 or row + ROWS == x_cells:
+                rows = pl.ds(sent_to, row + ROWS - sent_to)
+                sent_to = row + ROWS
+                copy = pltpu.make_async_copy(
+                    out_buf.at[c, rows], g_ref.at[c, rows], sems.at[len(copies)]
+                )
+                copy.start()
+                copies.append(copy)
     for copy in copies:
         copy.wait()
 
@@ -348,17 +331,13 @@
         out_refs[k][...] = total[0:8] + pltpu.roll(total[0:8], 4, 0) + total[8:16]
 
 
-def final_body(live, relax, particle, *refs):
+def final_body(request, relax, particle, *refs):
     parts, (fluid_ref, updated_ref) = refs[:-2], refs[-2:]
     raw = parts[0][0:3]
     for part in parts[1:]:
         raw = raw + part[0:3]
     slots = raw.shape[1]
-    lane = lax.broadcasted_iota(jnp.int32, (3, slots), 1)
-    limit = jnp.zeros((3, slots), jnp.int32)
-    for k in range(slots // PSIZE):
-        limit = jnp.where(lane // PSIZE == k, live[k], limit)
-    alive = lane % PSIZE < limit
+    alive = jnp.broadcast_to(request[16:32].astype(F32)[6:7], raw.shape) >= 0.0
     fluid = jnp.where(alive, raw, 0.0)
     velocity = particle[...]
     fluid_ref[...] = fluid
@@ -427,30 +406,21 @@
         plan.append((row, start, kinds.index(row - start)))
     matrices = jnp.asarray(np.stack([toeplitz(o, ROWS, window) for o in kinds]))
     width = 3 * ROWB
-    columns_at = 256 if x_cells % 256 == 0 else x_cells
-    reach = min(512, x_cells)
-    across, across_kinds = [], []
-    for column in range(0, x_cells, columns_at):
-        start = min(max(column - ROWB, 0), x_cells - reach)
-        if column - start not in across_kinds:
-            across_kinds.append(column - start)
-        across.append((column, start, across_kinds.index(column - start)))
-    turned = jnp.asarray(np.stack([toeplitz(o, columns_at, reach)[0].T for o in across_kinds]))
     held, table = pl.pallas_call(
-        lambda *refs: table_body(across, *refs),
+        lambda *refs: table_body(plan, *refs),
         in_specs=[hbm, vmem],
         out_specs=[vmem, vmem],
         out_shape=[
             jax.ShapeDtypeStruct(velocity.shape, F32),
             jax.ShapeDtypeStruct((blocks, 2 * width, x_cells), BF16),
         ],
-        scratch_shapes=[pltpu.SemaphoreType.DMA((6,))],
+        scratch_shapes=[pltpu.SemaphoreType.DMA((3,))],
         compiler_params=pltpu.CompilerParams(vmem_limit_bytes=LOAD * 1024 * 1024),
         cost_estimate=pl.CostEstimate(
             flops=2 * window * velocity.size, bytes_accessed=8 * velocity.size, transcendentals=0
         ),
         name="table",
-    )(velocity, turned)
+    )(velocity, matrices)
 
     *partials, sides = pl.pallas_call(
         lambda *refs: lookup_body(owners, xor, *refs),
@@ -479,7 +449,7 @@
         out_shape=jax.ShapeDtypeStruct(velocity.shape, F32),
         scratch_shapes=[
             pltpu.VMEM(velocity.shape, F32),
-            pltpu.SemaphoreType.DMA((len(plan),)),
+            pltpu.SemaphoreType.DMA((3 * len(plan),)),
         ],
         compiler_params=pltpu.CompilerParams(vmem_limit_bytes=limit),
         cost_estimate=pl.CostEstimate(
@@ -494,12 +464,12 @@
     shape = jax.ShapeDtypeStruct((3, slots), F32)
     fluid, updated = pl.pallas_call(
         final_body,
-        in_specs=[smem] + [vmem] * (2 + owners),
+        in_specs=[vmem] * (3 + owners),
         out_specs=[vmem] * 2,
         out_shape=[shape, shape],
         compiler_params=pltpu.CompilerParams(vmem_limit_bytes=limit),
         name="finish",
-    )(live_counts, relax_rate, particle_velocity, *returned)
+    )(request, relax_rate, particle_velocity, *returned)
     return (gradient, fluid, updated)
 
 

time: 26.3 us -> 24.7 us (0.939); the launches traced: 26.2 us -> 25.1 us
  Pallas kernels: 13.7 us -> 12.1 us
  waiting for transfers between devices: 0.21 us -> 1.49 us
  starting transfers between devices: 11.5 us -> 10.8 us
    ppermute x8, waiting for transfers between devices: 0.21 us -> 1.49 us  [sent(): return lax.ppermute(values, axis, pairs)]
    pallas_call x2, Pallas kernels: 4.7 us -> 3.66 us  [the longest x1 3.04 us: per_device(): pl.pallas_call(lambda *refs: table_body(plan, *refs), in_specs=[hbm, vmem...]
    ppermute x8, starting transfers between devices: 11.5 us -> 10.8 us  [sent(): return lax.ppermute(values, axis, pairs)]
    pallas_call x1, Pallas kernels: 3.18 us -> 2.65 us  [per_device(): pl.pallas_call(lambda *refs: derivative_body(plan, *refs), in_specs=[vmem...]
  transfers between devices with their start and end apart: 8 -> 8, of which waited for: 1 -> 1; matrix products, arithmetic and copies ran while one was open for 0% -> 0% of each run, Pallas kernels for 26% -> 23%
where the time goes in v4:
time: 24.7 us; the launch traced here: 25.1 us
  Pallas kernels  12.1 us (49%)
  starting transfers between devices  10.8 us (44%)
  waiting for transfers between devices  1.49 us (6%)
  between operations  0.74 us (3%)
    ppermute x8, starting transfers between devices, sent(): return lax.ppermute(values, axis, pairs)  10.8 us
    pallas_call x1, Pallas kernels, per_device(): pl.pallas_call(lambda *refs: lookup_body(owners, xor, *refs), in_specs=[s...  4.01 us
    pallas_call x1, Pallas kernels, per_device(): pl.pallas_call(lambda *refs: table_body(plan, *refs), in_specs=[hbm, vmem...  3.04 us
    pallas_call x1, Pallas kernels, per_device(): pl.pallas_call(lambda *refs: derivative_body(plan, *refs), in_specs=[vmem...  2.65 us
    pallas_call x1, Pallas kernels, per_device(): pl.pallas_call(lambda *refs: prep_body(x_cells, *refs), grid=(1,), in_spe...  1.79 us
    ppermute x8, waiting for transfers between devices, sent(): return lax.ppermute(values, axis, pairs)  1.49 us
    pallas_call x1, Pallas kernels, per_device(): pl.pallas_call(final_body, in_specs=[vmem] * (3 + owners), out_specs=[vme...  0.62 us
  transfers between devices with their start and end apart: 8, of which 1 were waited for; matrix products, arithmetic and copies ran while one was open for 0% of the time, Pallas kernels for 23%

profile of v4, /device:TPU:0, one launch (start us, length us, event | category | flops | bytes accessed | tf_op | source)
XLA Modules:
  0.0 25.1 jit_solution(4392998295706628689)
XLA Ops:
  0.6 0.0 copy-start
  0.6 1.8 %prepare.1 = (bf16[32,512]{1,0:T(8,128)(2,1)}, f32[8,512]{1,0:T(8,128)}, f32[8,512]{1,0:T(8,128)}) custom-call(s32[4]{0:T(128)} %refs_0_.4, f32[3,768,512]{2,1,0:T(8,128)} %refs_2_.1, f32[3,768,512]{2,1,0:T(8,128)} %refs_2_.1, s32[4,512]{1,0:T(4,128)} %refs_3_.1, f32[4,512]{1,0:T(4,128)} %refs_4_.1, f32[512]{0:T(512)} %refs_5_.1), custom_call_target="tpu_custom_call" | custom-call | tf_op jit(solution)/shard_map/prepare/pallas_call | solution.py:369
  2.4 3.0 %collective-permute-start.2 = (bf16[32,512]{1,0:T(8,128)(2,1)}, bf16[32,512]{1,0:T(8,128)(2,1)S(1)}, u32[]{:S(2)}, u32[]{:S(2)}) collective-permute-start(bf16[32,512]{1,0:T(8,128)(2,1)} %get-tuple-element.19.refs_4_.request), channel_id=1, source_target_pairs={{1,0},{0,1},{3,2},{2,3},{5,4},{4,5},{7,6},{6,7},{9,8},{8,9},{11,10... | collective-permute-start | bytes 98312 | tf_op jit(solution)/shard_map/ppermute | solution.py:350
  5.4 1.5 %collective-permute-start.3 = (bf16[32,512]{1,0:T(8,128)(2,1)}, bf16[32,512]{1,0:T(8,128)(2,1)S(1)}, u32[]{:S(2)}, u32[]{:S(2)}) collective-permute-start(bf16[32,512]{1,0:T(8,128)(2,1)} %get-tuple-element.19.refs_4_.request), channel_id=1, source_target_pairs={{2,0},{3,1},{0,2},{1,3},{6,4},{7,5},{4,6},{5,7},{10,8},{11,9},{8,1... | collective-permute-start | bytes 98312 | tf_op jit(solution)/shard_map/ppermute | solution.py:350
  7.0 0.0 collective-permute-start.4
  7.0 2.7 %collective-permute-start = (f32[8,512]{1,0:T(8,128)}, f32[8,512]{1,0:T(8,128)S(1)}, u32[]{:S(2)}, u32[]{:S(2)}) collective-permute-start(f32[8,512]{1,0:T(8,128)} %get-tuple-element.16), channel_id=1, source_target_pairs={{0,28},{4,8},{8,4},{12,16},{16,12},{20,24},{24,20},{28,0},{1,29},{... | collective-permute-start | bytes 49160 | tf_op jit(solution)/shard_map/ppermute | solution.py:350
  9.6 0.0 collective-permute-start.1
  9.6 0.0 copy-done
  9.6 3.0 %table.1 = (f32[3,768,512]{2,1,0:T(8,128)S(1)}, bf16[4,768,768]{2,1,0:T(8,128)(2,1)S(1)}) custom-call(f32[3,768,512]{2,1,0:T(8,128)} %refs_2_.1, bf16[3,192,256]{2,1,0:T(8,128)(2,1)S(1)} %copy-done), custom_call_target="tpu_custom_call" | custom-call | flops 603979776 | bytes 9437184 | tf_op jit(solution)/shard_map/table/pallas_call | solution.py:409
  12.7 0.0 collective-permute-done.refs_1_
  12.7 0.0 collective-permute-done.1.refs_2_
  12.7 0.0 collective-permute-done.2.refs_5_
  12.7 0.0 collective-permute-done.3.refs_6_
  12.7 0.0 collective-permute-done.4.refs_7_
  12.8 4.0 %lookup.1 = (f32[8,512]{1,0:T(8,128)S(1)}, f32[8,512]{1,0:T(8,128)S(1)}, f32[8,512]{1,0:T(8,128)S(1)}, f32[8,512]{1,0:T(8,128)S(1)}, f32[16,512]{1,0:T(8,128)S(1)}) custom-call(s32[1,16]{1,0:T(1,128)S(1)} %copy-done.4, f32[8,512]{1,0:T(8,128)S(1)} %collective-permute-done.refs_1_, f32[8,512]{1,0:T(8,128)S(1)} %collective-permute-done.1.refs_2_, ...), custom_call_target="tpu_custom_call" | custom-call | flops 7247757312 | bytes 2359296 | tf_op jit(solution)/shard_map/lookup/pallas_call | solution.py:425
  16.8 1.6 %collective-permute-start.5 = (f32[8,512]{1,0:T(8,128)S(1)}, f32[8,512]{1,0:T(8,128)S(1)}, u32[]{:S(2)}, u32[]{:S(2)}) collective-permute-start(f32[8,512]{1,0:T(8,128)S(1)} %get-tuple-element.22), channel_id=1, source_target_pairs={{0,1},{1,0},{2,3},{3,2},{4,5},{5,4},{6,7},{7,6},{8,9},{9,8},{10,11... | collective-permute-start | bytes 49160 | tf_op jit(solution)/shard_map/ppermute | solution.py:350
  18.3 1.5 %collective-permute-start.6 = (f32[8,512]{1,0:T(8,128)S(1)}, f32[8,512]{1,0:T(8,128)S(1)}, u32[]{:S(2)}, u32[]{:S(2)}) collective-permute-start(f32[8,512]{1,0:T(8,128)S(1)} %get-tuple-element.23), channel_id=1, source_target_pairs={{0,2},{1,3},{2,0},{3,1},{4,6},{5,7},{6,4},{7,5},{8,10},{9,11},{10,... | collective-permute-start | bytes 49160 | tf_op jit(solution)/shard_map/ppermute | solution.py:350
  19.9 0.5 %collective-permute-start.7 = (f32[8,512]{1,0:T(8,128)S(1)}, f32[8,512]{1,0:T(8,128)S(1)}, u32[]{:S(2)}, u32[]{:S(2)}) collective-permute-start(f32[8,512]{1,0:T(8,128)S(1)} %get-tuple-element.24), channel_id=1, source_target_pairs={{0,3},{1,2},{2,1},{3,0},{4,7},{5,6},{6,5},{7,4},{8,11},{9,10},{10,... | collective-permute-start | bytes 49160 | tf_op jit(solution)/shard_map/ppermute | solution.py:350
  20.3 2.7 %derivative.1 = f32[3,768,512]{2,1,0:T(8,128)} custom-call(f32[3,768,512]{2,1,0:T(8,128)S(1)} %get-tuple-element.15.refs_0_, bf16[3,192,256]{2,1,0:T(8,128)(2,1)S(1)} %copy-done, f32[16,512]{1,0:T(8,128)S(1)} %get-tuple-element.20.refs_2_), custom_call_target="tpu_custom_call" | custom-call | flops 1811939328 | bytes 9437184 | tf_op jit(solution)/shard_map/derivative/pallas_call | solution.py:445
  23.0 0.0 collective-permute-done.5.refs_1_
  23.0 0.0 collective-permute-done.6.refs_2_
  23.0 1.5 %collective-permute-done.7.refs_3_ = f32[8,512]{1,0:T(8,128)S(1)} collective-permute-done((f32[8,512]{1,0:T(8,128)S(1)}, f32[8,512]{1,0:T(8,128)S(1)}, u32[]{:S(2)}, u32[]{:S(2)}) %collective-permute-start.7) | collective-permute-done | bytes 16416 | tf_op jit(solution)/shard_map/ppermute | solution.py:350
  24.5 0.0 copy-done.2
  24.5 0.6 %finish.1 = (f32[3,512]{1,0:T(4,128)}, f32[3,512]{1,0:T(4,128)}) custom-call(bf16[32,512]{1,0:T(8,128)(2,1)S(1)} %copy-done.1, f32[512]{0:T(512)S(1)} %copy-done.3, f32[3,512]{1,0:T(4,128)S(1)} %copy-done.2, f32[8,512]{1,0:T(8,128)S(1)} %get-tuple-element.21.refs_0_, f32[8,512]{1,0:T(8,128)S(1)} %collective-permute-done.5.refs_1_, ...), custom_call_target="tpu_custom_call" | custom-call | tf_op jit(solution)/shard_map/finish/pallas_call | solution.py:465
  (7 shorter events, 0.0 us)
Async XLA Ops:
  0.6 9.0 %copy-start = (bf16[3,192,256]{2,1,0:T(8,128)(2,1)S(1)}, bf16[3,192,256]{2,1,0:T(8,128)(2,1)}, u32[]{:S(2)}) copy-start(bf16[3,192,256]{2,1,0:T(8,128)(2,1)} %constant.2.clone.refs_1_) | copy-start | bytes 884740
  2.4 10.3 %copy-start.1 = (bf16[32,512]{1,0:T(8,128)(2,1)S(1)}, bf16[32,512]{1,0:T(8,128)(2,1)}, u32[]{:S(2)}) copy-start(bf16[32,512]{1,0:T(8,128)(2,1)} %get-tuple-element.19.refs_4_.request) | copy-start | bytes 98308
  2.4 10.3 %copy-start.4 = (s32[1,16]{1,0:T(1,128)S(1)}, s32[1,16]{1,0:T(1,128)}, u32[]{:S(2)}) copy-start(s32[1,16]{1,0:T(1,128)} %refs_0_.5) | copy-start | bytes 196
  2.4 10.3 %collective-permute-start.2 = (bf16[32,512]{1,0:T(8,128)(2,1)}, bf16[32,512]{1,0:T(8,128)(2,1)S(1)}, u32[]{:S(2)}, u32[]{:S(2)}) collective-permute-start(bf16[32,512]{1,0:T(8,128)(2,1)} %get-tuple-element.19.refs_4_.request), channel_id=1, source_target_pairs={{1,0},{0,1},{3,2},{2,3},{5,4},{4,5},{7,6},{6,7},{9,8},{8,9},{11,10... | collective-permute-start | bytes 98312 | tf_op jit(solution)/shard_map/ppermute | solution.py:350
  5.4 7.3 %collective-permute-start.3 = (bf16[32,512]{1,0:T(8,128)(2,1)}, bf16[32,512]{1,0:T(8,128)(2,1)S(1)}, u32[]{:S(2)}, u32[]{:S(2)}) collective-permute-start(bf16[32,512]{1,0:T(8,128)(2,1)} %get-tuple-element.19.refs_4_.request), channel_id=1, source_target_pairs={{2,0},{3,1},{0,2},{1,3},{6,4},{7,5},{4,6},{5,7},{10,8},{11,9},{8,1... | collective-permute-start | bytes 98312 | tf_op jit(solution)/shard_map/ppermute | solution.py:350
  7.0 5.8 %collective-permute-start.4 = (bf16[32,512]{1,0:T(8,128)(2,1)}, bf16[32,512]{1,0:T(8,128)(2,1)S(1)}, u32[]{:S(2)}, u32[]{:S(2)}) collective-permute-start(bf16[32,512]{1,0:T(8,128)(2,1)} %get-tuple-element.19.refs_4_.request), channel_id=1, source_target_pairs={{3,0},{2,1},{1,2},{0,3},{7,4},{6,5},{5,6},{4,7},{11,8},{10,9},{9,1... | collective-permute-start | bytes 98312 | tf_op jit(solution)/shard_map/ppermute | solution.py:350
  7.0 5.7 %collective-permute-start = (f32[8,512]{1,0:T(8,128)}, f32[8,512]{1,0:T(8,128)S(1)}, u32[]{:S(2)}, u32[]{:S(2)}) collective-permute-start(f32[8,512]{1,0:T(8,128)} %get-tuple-element.16), channel_id=1, source_target_pairs={{0,28},{4,8},{8,4},{12,16},{16,12},{20,24},{24,20},{28,0},{1,29},{... | collective-permute-start | bytes 49160 | tf_op jit(solution)/shard_map/ppermute | solution.py:350
  9.6 3.1 %collective-permute-start.1 = (f32[8,512]{1,0:T(8,128)}, f32[8,512]{1,0:T(8,128)S(1)}, u32[]{:S(2)}, u32[]{:S(2)}) collective-permute-start(f32[8,512]{1,0:T(8,128)} %get-tuple-element.17), channel_id=1, source_target_pairs={{0,4},{4,0},{8,12},{12,8},{16,20},{20,16},{24,28},{28,24},{1,5},{5... | collective-permute-start | bytes 49160 | tf_op jit(solution)/shard_map/ppermute | solution.py:350
  16.8 6.2 %collective-permute-start.5 = (f32[8,512]{1,0:T(8,128)S(1)}, f32[8,512]{1,0:T(8,128)S(1)}, u32[]{:S(2)}, u32[]{:S(2)}) collective-permute-start(f32[8,512]{1,0:T(8,128)S(1)} %get-tuple-element.22), channel_id=1, source_target_pairs={{0,1},{1,0},{2,3},{3,2},{4,5},{5,4},{6,7},{7,6},{8,9},{9,8},{10,11... | collective-permute-start | bytes 49160 | tf_op jit(solution)/shard_map/ppermute | solution.py:350
  18.3 4.7 %collective-permute-start.6 = (f32[8,512]{1,0:T(8,128)S(1)}, f32[8,512]{1,0:T(8,128)S(1)}, u32[]{:S(2)}, u32[]{:S(2)}) collective-permute-start(f32[8,512]{1,0:T(8,128)S(1)} %get-tuple-element.23), channel_id=1, source_target_pairs={{0,2},{1,3},{2,0},{3,1},{4,6},{5,7},{6,4},{7,5},{8,10},{9,11},{10,... | collective-permute-start | bytes 49160 | tf_op jit(solution)/shard_map/ppermute | solution.py:350
  19.9 4.6 %collective-permute-start.7 = (f32[8,512]{1,0:T(8,128)S(1)}, f32[8,512]{1,0:T(8,128)S(1)}, u32[]{:S(2)}, u32[]{:S(2)}) collective-permute-start(f32[8,512]{1,0:T(8,128)S(1)} %get-tuple-element.24), channel_id=1, source_target_pairs={{0,3},{1,2},{2,1},{3,0},{4,7},{5,6},{6,5},{7,4},{8,11},{9,10},{10,... | collective-permute-start | bytes 49160 | tf_op jit(solution)/shard_map/ppermute | solution.py:350
  20.3 4.2 %copy-start.2 = (f32[3,512]{1,0:T(4,128)S(1)}, f32[3,512]{1,0:T(4,128)}, u32[]{:S(2)}) copy-start(f32[3,512]{1,0:T(4,128)} %particle.1) | copy-start | bytes 18436
  20.3 4.2 %copy-start.3 = (f32[512]{0:T(512)S(1)}, f32[512]{0:T(512)}, u32[]{:S(2)}) copy-start(f32[512]{0:T(512)} %relax.1) | copy-start | bytes 6148

commit v5 on v4

--- a/solution.py
+++ b/solution.py
@@ -95,8 +95,9 @@
     slot = (row >> 7)[0:1]
     lane = lax.broadcasted_iota(jnp.int32, (1, slots), 1)
     limit = jnp.zeros((1, slots), jnp.int32)
+    counts = live[...].reshape(1, slots // PSIZE)
     for k in range(slots // PSIZE):
-        limit = jnp.where(lane // PSIZE == k, live[k], limit)
+        limit = jnp.where(lane // PSIZE == k, counts[:, k : k + 1], limit)
     alive = lane % PSIZE < limit
     key = jnp.where(alive, slot, -1).astype(F32)
     w_high, w_low = split(weights[...], 2)
@@ -198,9 +199,12 @@
     groups = slots // ROWB
     cells = STEN * CHUNK
 
+    row_owners = owner_ref[...].astype(F32)
+    row_lane = lax.broadcasted_iota(jnp.int32, row_owners.shape, 1)
     peers = []
     for block in range(blocks):
-        owner = owner_ref[0, me * blocks + block]
+        mine = jnp.where(row_lane == me * blocks + block, row_owners, 0.0)
+        owner = jnp.sum(mine).astype(jnp.int32)
         peers.append((owner ^ me) if xor else lax.rem(owner - me + owners, owners))
         peer_at[block] = peers[block]
     for k in range(owners):
@@ -311,8 +315,6 @@
             )
             totals[peer] += jnp.dot(back.astype(BF16), pick, preferred_element_type=F32)
 
-    batch([(block, peers[block], jnp.int32(0)) for block in range(blocks)])
-
     def extra(number):
         block = jnp.int32(0)
         first = jnp.int32(0)
@@ -322,7 +324,19 @@
             first = jnp.where(past, ends[b], first)
         return block, peer_at[block], number - first + 1
 
-    @pl.loop(0, (ends[-1] + EXTRA - 1) // EXTRA)
+    base = [(block, peers[block], jnp.int32(0)) for block in range(blocks)]
+    extras = ends[-1]
+    sizes = [0, EXTRA, 2 * EXTRA]
+    for size, above in zip(sizes, sizes[1:] + [None]):
+        fits = extras > size - EXTRA
+        if above is not None:
+            fits = jnp.logical_and(fits, extras <= size)
+
+        @pl.when(fits)
+        def _(size=size):
+            batch(base + [extra(jnp.int32(t)) for t in range(size)])
+
+    @pl.loop(2, (extras + EXTRA - 1) // EXTRA)
     def _(i):
         batch([extra(i * EXTRA + t) for t in range(EXTRA)])
 
@@ -370,7 +384,7 @@
         lambda *refs: prep_body(x_cells, *refs),
         grid=(1,),
         in_specs=[
-            smem,
+            one((slots // PSIZE,)),
             pl.BlockSpec((3, EDGE, lines), lambda i: (0, 0, 0)),
             pl.BlockSpec((3, EDGE, lines), lambda i: (0, last, 0)),
             one((STEN, slots)),
@@ -424,7 +438,7 @@
 
     *partials, sides = pl.pallas_call(
         lambda *refs: lookup_body(owners, xor, *refs),
-        in_specs=[smem] + [vmem] * (3 + owners),
+        in_specs=[vmem] * (4 + owners),
         out_specs=[vmem] * (owners + 1),
         out_shape=[jax.ShapeDtypeStruct((8, slots), F32)] * owners
         + [jax.ShapeDtypeStruct((16, lines), F32)],

time: 24.7 us -> 24.5 us (level); the launches traced: 25.1 us -> 24.4 us
  Pallas kernels: 12.1 us -> 11.4 us
    pallas_call x1, Pallas kernels: 4.01 us -> 3.25 us  [per_device(): pl.pallas_call(lambda *refs: lookup_body(owners, xor, *refs), in_specs=[v...]
where the time goes in v5:
time: 24.5 us; the launch traced here: 24.4 us
  Pallas kernels  11.4 us (47%)
  starting transfers between devices  10.7 us (44%)
  waiting for transfers between devices  1.48 us (6%)
  between operations  0.74 us (3%)
    ppermute x8, starting transfers between devices, sent(): return lax.ppermute(values, axis, pairs)  10.7 us
    pallas_call x1, Pallas kernels, per_device(): pl.pallas_call(lambda *refs: lookup_body(owners, xor, *refs), in_specs=[v...  3.25 us
    pallas_call x1, Pallas kernels, per_device(): pl.pallas_call(lambda *refs: table_body(plan, *refs), in_specs=[hbm, vmem...  3.05 us
    pallas_call x1, Pallas kernels, per_device(): pl.pallas_call(lambda *refs: derivative_body(plan, *refs), in_specs=[vmem...  2.66 us
    pallas_call x1, Pallas kernels, per_device(): pl.pallas_call(lambda *refs: prep_body(x_cells, *refs), grid=(1,), in_spe...  1.79 us
    ppermute x8, waiting for transfers between devices, sent(): return lax.ppermute(values, axis, pairs)  1.48 us
    pallas_call x1, Pallas kernels, per_device(): pl.pallas_call(final_body, in_specs=[vmem] * (3 + owners), out_specs=[vme...  0.62 us
  transfers between devices with their start and end apart: 8, of which 1 were waited for; matrix products, arithmetic and copies ran while one was open for 0% of the time, Pallas kernels for 23%

profile of v5, /device:TPU:0, one launch (start us, length us, event | category | flops | bytes accessed | tf_op | source)
XLA Modules:
  0.0 24.4 jit_solution(10551326301537146765)
XLA Ops:
  0.6 0.0 copy-start
  0.6 1.8 %prepare.1 = (bf16[32,512]{1,0:T(8,128)(2,1)}, f32[8,512]{1,0:T(8,128)}, f32[8,512]{1,0:T(8,128)}) custom-call(s32[4]{0:T(128)} %refs_0_.4, f32[3,768,512]{2,1,0:T(8,128)} %refs_2_.1, f32[3,768,512]{2,1,0:T(8,128)} %refs_2_.1, s32[4,512]{1,0:T(4,128)} %refs_3_.1, f32[4,512]{1,0:T(4,128)} %refs_4_.1, f32[512]{0:T(512)} %refs_5_.1), custom_call_target="tpu_custom_call" | custom-call | tf_op jit(solution)/shard_map/prepare/pallas_call | solution.py:383
  2.4 3.0 %collective-permute-start.2 = (bf16[32,512]{1,0:T(8,128)(2,1)}, bf16[32,512]{1,0:T(8,128)(2,1)S(1)}, u32[]{:S(2)}, u32[]{:S(2)}) collective-permute-start(bf16[32,512]{1,0:T(8,128)(2,1)} %get-tuple-element.19.refs_4_.request), channel_id=1, source_target_pairs={{1,0},{0,1},{3,2},{2,3},{5,4},{4,5},{7,6},{6,7},{9,8},{8,9},{11,10... | collective-permute-start | bytes 98312 | tf_op jit(solution)/shard_map/ppermute | solution.py:364
  5.4 1.5 %collective-permute-start.3 = (bf16[32,512]{1,0:T(8,128)(2,1)}, bf16[32,512]{1,0:T(8,128)(2,1)S(1)}, u32[]{:S(2)}, u32[]{:S(2)}) collective-permute-start(bf16[32,512]{1,0:T(8,128)(2,1)} %get-tuple-element.19.refs_4_.request), channel_id=1, source_target_pairs={{2,0},{3,1},{0,2},{1,3},{6,4},{7,5},{4,6},{5,7},{10,8},{11,9},{8,1... | collective-permute-start | bytes 98312 | tf_op jit(solution)/shard_map/ppermute | solution.py:364
  7.0 0.0 collective-permute-start.4
  7.0 2.7 %collective-permute-start = (f32[8,512]{1,0:T(8,128)}, f32[8,512]{1,0:T(8,128)S(1)}, u32[]{:S(2)}, u32[]{:S(2)}) collective-permute-start(f32[8,512]{1,0:T(8,128)} %get-tuple-element.16), channel_id=1, source_target_pairs={{0,28},{4,8},{8,4},{12,16},{16,12},{20,24},{24,20},{28,0},{1,29},{... | collective-permute-start | bytes 49160 | tf_op jit(solution)/shard_map/ppermute | solution.py:364
  9.6 0.0 collective-permute-start.1
  9.6 3.1 %table.1 = (f32[3,768,512]{2,1,0:T(8,128)S(1)}, bf16[4,768,768]{2,1,0:T(8,128)(2,1)S(1)}) custom-call(f32[3,768,512]{2,1,0:T(8,128)} %refs_2_.1, bf16[3,192,256]{2,1,0:T(8,128)(2,1)S(1)} %copy-done), custom_call_target="tpu_custom_call" | custom-call | flops 603979776 | bytes 9437184 | tf_op jit(solution)/shard_map/table/pallas_call | solution.py:423
  12.7 0.0 collective-permute-done.refs_1_
  12.7 0.0 collective-permute-done.1.refs_2_
  12.7 0.0 collective-permute-done.2.refs_5_
  12.7 0.0 collective-permute-done.3.refs_6_
  12.7 0.0 collective-permute-done.4.refs_7_
  12.8 0.0 copy-done.1
  12.8 0.0 copy-done.4
  12.8 3.3 %lookup.1 = (f32[8,512]{1,0:T(8,128)S(1)}, f32[8,512]{1,0:T(8,128)S(1)}, f32[8,512]{1,0:T(8,128)S(1)}, f32[8,512]{1,0:T(8,128)S(1)}, f32[16,512]{1,0:T(8,128)S(1)}) custom-call(s32[1,16]{1,0:T(1,128)S(1)} %copy-done.4, f32[8,512]{1,0:T(8,128)S(1)} %collective-permute-done.refs_1_, f32[8,512]{1,0:T(8,128)S(1)} %collective-permute-done.1.refs_2_, ...), custom_call_target="tpu_custom_call" | custom-call | flops 7247757312 | bytes 2359296 | tf_op jit(solution)/shard_map/lookup/pallas_call | solution.py:439
  16.0 1.6 %collective-permute-start.5 = (f32[8,512]{1,0:T(8,128)S(1)}, f32[8,512]{1,0:T(8,128)S(1)}, u32[]{:S(2)}, u32[]{:S(2)}) collective-permute-start(f32[8,512]{1,0:T(8,128)S(1)} %get-tuple-element.22), channel_id=1, source_target_pairs={{0,1},{1,0},{2,3},{3,2},{4,5},{5,4},{6,7},{7,6},{8,9},{9,8},{10,11... | collective-permute-start | bytes 49160 | tf_op jit(solution)/shard_map/ppermute | solution.py:364
  17.6 1.5 %collective-permute-start.6 = (f32[8,512]{1,0:T(8,128)S(1)}, f32[8,512]{1,0:T(8,128)S(1)}, u32[]{:S(2)}, u32[]{:S(2)}) collective-permute-start(f32[8,512]{1,0:T(8,128)S(1)} %get-tuple-element.23), channel_id=1, source_target_pairs={{0,2},{1,3},{2,0},{3,1},{4,6},{5,7},{6,4},{7,5},{8,10},{9,11},{10,... | collective-permute-start | bytes 49160 | tf_op jit(solution)/shard_map/ppermute | solution.py:364
  19.1 0.5 %collective-permute-start.7 = (f32[8,512]{1,0:T(8,128)S(1)}, f32[8,512]{1,0:T(8,128)S(1)}, u32[]{:S(2)}, u32[]{:S(2)}) collective-permute-start(f32[8,512]{1,0:T(8,128)S(1)} %get-tuple-element.24), channel_id=1, source_target_pairs={{0,3},{1,2},{2,1},{3,0},{4,7},{5,6},{6,5},{7,4},{8,11},{9,10},{10,... | collective-permute-start | bytes 49160 | tf_op jit(solution)/shard_map/ppermute | solution.py:364
  19.6 2.7 %derivative.1 = f32[3,768,512]{2,1,0:T(8,128)} custom-call(f32[3,768,512]{2,1,0:T(8,128)S(1)} %get-tuple-element.15.refs_0_, bf16[3,192,256]{2,1,0:T(8,128)(2,1)S(1)} %copy-done, f32[16,512]{1,0:T(8,128)S(1)} %get-tuple-element.20.refs_2_), custom_call_target="tpu_custom_call" | custom-call | flops 1811939328 | bytes 9437184 | tf_op jit(solution)/shard_map/derivative/pallas_call | solution.py:459
  22.3 0.0 collective-permute-done.5.refs_1_
  22.3 0.0 collective-permute-done.6.refs_2_
  22.3 1.5 %collective-permute-done.7.refs_3_ = f32[8,512]{1,0:T(8,128)S(1)} collective-permute-done((f32[8,512]{1,0:T(8,128)S(1)}, f32[8,512]{1,0:T(8,128)S(1)}, u32[]{:S(2)}, u32[]{:S(2)}) %collective-permute-start.7) | collective-permute-done | bytes 16416 | tf_op jit(solution)/shard_map/ppermute | solution.py:364
  23.7 0.6 %finish.1 = (f32[3,512]{1,0:T(4,128)}, f32[3,512]{1,0:T(4,128)}) custom-call(bf16[32,512]{1,0:T(8,128)(2,1)S(1)} %copy-done.1, f32[512]{0:T(512)S(1)} %copy-done.3, f32[3,512]{1,0:T(4,128)S(1)} %copy-done.2, f32[8,512]{1,0:T(8,128)S(1)} %get-tuple-element.21.refs_0_, f32[8,512]{1,0:T(8,128)S(1)} %collective-permute-done.5.refs_1_, ...), custom_call_target="tpu_custom_call" | custom-call | tf_op jit(solution)/shard_map/finish/pallas_call | solution.py:479
  (7 shorter events, 0.0 us)
Async XLA Ops:
  0.6 9.0 %copy-start = (bf16[3,192,256]{2,1,0:T(8,128)(2,1)S(1)}, bf16[3,192,256]{2,1,0:T(8,128)(2,1)}, u32[]{:S(2)}) copy-start(bf16[3,192,256]{2,1,0:T(8,128)(2,1)} %constant.2.clone.refs_1_) | copy-start | bytes 884740
  2.4 10.3 %copy-start.1 = (bf16[32,512]{1,0:T(8,128)(2,1)S(1)}, bf16[32,512]{1,0:T(8,128)(2,1)}, u32[]{:S(2)}) copy-start(bf16[32,512]{1,0:T(8,128)(2,1)} %get-tuple-element.19.refs_4_.request) | copy-start | bytes 98308
  2.4 10.3 %copy-start.4 = (s32[1,16]{1,0:T(1,128)S(1)}, s32[1,16]{1,0:T(1,128)}, u32[]{:S(2)}) copy-start(s32[1,16]{1,0:T(1,128)} %refs_0_.5) | copy-start | bytes 196
  2.4 10.3 %collective-permute-start.2 = (bf16[32,512]{1,0:T(8,128)(2,1)}, bf16[32,512]{1,0:T(8,128)(2,1)S(1)}, u32[]{:S(2)}, u32[]{:S(2)}) collective-permute-start(bf16[32,512]{1,0:T(8,128)(2,1)} %get-tuple-element.19.refs_4_.request), channel_id=1, source_target_pairs={{1,0},{0,1},{3,2},{2,3},{5,4},{4,5},{7,6},{6,7},{9,8},{8,9},{11,10... | collective-permute-start | bytes 98312 | tf_op jit(solution)/shard_map/ppermute | solution.py:364
  5.4 7.3 %collective-permute-start.3 = (bf16[32,512]{1,0:T(8,128)(2,1)}, bf16[32,512]{1,0:T(8,128)(2,1)S(1)}, u32[]{:S(2)}, u32[]{:S(2)}) collective-permute-start(bf16[32,512]{1,0:T(8,128)(2,1)} %get-tuple-element.19.refs_4_.request), channel_id=1, source_target_pairs={{2,0},{3,1},{0,2},{1,3},{6,4},{7,5},{4,6},{5,7},{10,8},{11,9},{8,1... | collective-permute-start | bytes 98312 | tf_op jit(solution)/shard_map/ppermute | solution.py:364
  7.0 5.8 %collective-permute-start.4 = (bf16[32,512]{1,0:T(8,128)(2,1)}, bf16[32,512]{1,0:T(8,128)(2,1)S(1)}, u32[]{:S(2)}, u32[]{:S(2)}) collective-permute-start(bf16[32,512]{1,0:T(8,128)(2,1)} %get-tuple-element.19.refs_4_.request), channel_id=1, source_target_pairs={{3,0},{2,1},{1,2},{0,3},{7,4},{6,5},{5,6},{4,7},{11,8},{10,9},{9,1... | collective-permute-start | bytes 98312 | tf_op jit(solution)/shard_map/ppermute | solution.py:364
  7.0 5.7 %collective-permute-start = (f32[8,512]{1,0:T(8,128)}, f32[8,512]{1,0:T(8,128)S(1)}, u32[]{:S(2)}, u32[]{:S(2)}) collective-permute-start(f32[8,512]{1,0:T(8,128)} %get-tuple-element.16), channel_id=1, source_target_pairs={{0,28},{4,8},{8,4},{12,16},{16,12},{20,24},{24,20},{28,0},{1,29},{... | collective-permute-start | bytes 49160 | tf_op jit(solution)/shard_map/ppermute | solution.py:364
  9.6 3.1 %collective-permute-start.1 = (f32[8,512]{1,0:T(8,128)}, f32[8,512]{1,0:T(8,128)S(1)}, u32[]{:S(2)}, u32[]{:S(2)}) collective-permute-start(f32[8,512]{1,0:T(8,128)} %get-tuple-element.17), channel_id=1, source_target_pairs={{0,4},{4,0},{8,12},{12,8},{16,20},{20,16},{24,28},{28,24},{1,5},{5... | collective-permute-start | bytes 49160 | tf_op jit(solution)/shard_map/ppermute | solution.py:364
  16.0 6.2 %collective-permute-start.5 = (f32[8,512]{1,0:T(8,128)S(1)}, f32[8,512]{1,0:T(8,128)S(1)}, u32[]{:S(2)}, u32[]{:S(2)}) collective-permute-start(f32[8,512]{1,0:T(8,128)S(1)} %get-tuple-element.22), channel_id=1, source_target_pairs={{0,1},{1,0},{2,3},{3,2},{4,5},{5,4},{6,7},{7,6},{8,9},{9,8},{10,11... | collective-permute-start | bytes 49160 | tf_op jit(solution)/shard_map/ppermute | solution.py:364
  17.6 4.7 %collective-permute-start.6 = (f32[8,512]{1,0:T(8,128)S(1)}, f32[8,512]{1,0:T(8,128)S(1)}, u32[]{:S(2)}, u32[]{:S(2)}) collective-permute-start(f32[8,512]{1,0:T(8,128)S(1)} %get-tuple-element.23), channel_id=1, source_target_pairs={{0,2},{1,3},{2,0},{3,1},{4,6},{5,7},{6,4},{7,5},{8,10},{9,11},{10,... | collective-permute-start | bytes 49160 | tf_op jit(solution)/shard_map/ppermute | solution.py:364
  19.1 4.6 %collective-permute-start.7 = (f32[8,512]{1,0:T(8,128)S(1)}, f32[8,512]{1,0:T(8,128)S(1)}, u32[]{:S(2)}, u32[]{:S(2)}) collective-permute-start(f32[8,512]{1,0:T(8,128)S(1)} %get-tuple-element.24), channel_id=1, source_target_pairs={{0,3},{1,2},{2,1},{3,0},{4,7},{5,6},{6,5},{7,4},{8,11},{9,10},{10,... | collective-permute-start | bytes 49160 | tf_op jit(solution)/shard_map/ppermute | solution.py:364
  19.6 4.2 %copy-start.2 = (f32[3,512]{1,0:T(4,128)S(1)}, f32[3,512]{1,0:T(4,128)}, u32[]{:S(2)}) copy-start(f32[3,512]{1,0:T(4,128)} %particle.1) | copy-start | bytes 18436
  19.6 4.2 %copy-start.3 = (f32[512]{0:T(512)S(1)}, f32[512]{0:T(512)}, u32[]{:S(2)}) copy-start(f32[512]{0:T(512)} %relax.1) | copy-start | bytes 6148

commit v6 on v5

--- a/solution.py
+++ b/solution.py
@@ -186,7 +186,7 @@
     return parity * jnp.exp(steps * math.log(R_DECAY))
 
 
-def lookup_body(owners, xor, owner_ref, next_ref, chip_ref, table_ref, *refs):
+def lookup_body(owners, xor, order, owner_ref, next_ref, chip_ref, table_ref, *refs):
     request_refs = refs[:owners]
     out_refs = refs[owners : 2 * owners]
     sides_ref = refs[2 * owners]
@@ -208,7 +208,7 @@
         peers.append((owner ^ me) if xor else lax.rem(owner - me + owners, owners))
         peer_at[block] = peers[block]
     for k in range(owners):
-        requests[k] = request_refs[k][...]
+        requests[order[k]] = request_refs[k][...]
         totals[k] = jnp.zeros(totals.shape[1:], F32)
     sides = jnp.concatenate(neighbours(chip_ref, next_ref), 0)
     sides_ref[...] = sides
@@ -407,8 +407,9 @@
     def peer(i, k):
         return i ^ k if xor else (i + k) % owners
 
+    far_first = sorted(range(1, owners), key=lambda k: -bin(k).count("1"))
     requests = [request] + [
-        sent(request, "gy", [(peer(i, k), i) for i in range(owners)]) for k in range(1, owners)
+        sent(request, "gy", [(peer(i, k), i) for i in range(owners)]) for k in far_first
     ]
 
     window = min(256, x_cells)
@@ -437,7 +438,7 @@
     )(velocity, matrices)
 
     *partials, sides = pl.pallas_call(
-        lambda *refs: lookup_body(owners, xor, *refs),
+        lambda *refs: lookup_body(owners, xor, [0] + far_first, *refs),
         in_specs=[vmem] * (4 + owners),
         out_specs=[vmem] * (owners + 1),
         out_shape=[jax.ShapeDtypeStruct((8, slots), F32)] * owners
@@ -473,7 +474,7 @@
     )(held, matrices, sides)
 
     returned = [partials[0]] + [
-        sent(partials[k], "gy", [(i, peer(i, k)) for i in range(owners)]) for k in range(1, owners)
+        sent(partials[k], "gy", [(i, peer(i, k)) for i in range(owners)]) for k in far_first
     ]
     shape = jax.ShapeDtypeStruct((3, slots), F32)
     fluid, updated = pl.pallas_call(

time: 24.5 us -> 23.3 us (0.951)
  waiting for transfers between devices: 1.48 us -> 0.02 us
    ppermute x8, waiting for transfers between devices: 1.48 us -> 0.02 us  [sent(): return lax.ppermute(values, axis, pairs)]
  transfers between devices with their start and end apart: 8 -> 8, of which waited for: 1 -> 0; matrix products, arithmetic and copies ran while one was open for 0% -> 0% of each run, Pallas kernels for 23% -> 25%
where the time goes in v6:
time: 23.3 us; the launch traced here: 22.9 us
  Pallas kernels  11.4 us (49%)
  starting transfers between devices  10.8 us (46%)
  between operations  0.77 us (3%)
    ppermute x8, starting transfers between devices, sent(): return lax.ppermute(values, axis, pairs)  10.8 us
    pallas_call x1, Pallas kernels, per_device(): pl.pallas_call(lambda *refs: lookup_body(owners, xor, [0] + far_first, *r...  3.25 us
    pallas_call x1, Pallas kernels, per_device(): pl.pallas_call(lambda *refs: table_body(plan, *refs), in_specs=[hbm, vmem...  3.06 us
    pallas_call x1, Pallas kernels, per_device(): pl.pallas_call(lambda *refs: derivative_body(plan, *refs), in_specs=[vmem...  2.66 us
    pallas_call x1, Pallas kernels, per_device(): pl.pallas_call(lambda *refs: prep_body(x_cells, *refs), grid=(1,), in_spe...  1.79 us
    pallas_call x1, Pallas kernels, per_device(): pl.pallas_call(final_body, in_specs=[vmem] * (3 + owners), out_specs=[vme...  0.62 us
  transfers between devices with their start and end apart: 8, of which 0 were waited for; matrix products, arithmetic and copies ran while one was open for 0% of the time, Pallas kernels for 25%

profile of v6, /device:TPU:0, one launch (start us, length us, event | category | flops | bytes accessed | tf_op | source)
XLA Modules:
  0.0 22.9 jit_solution(11354366659287361742)
XLA Ops:
  0.6 0.0 copy-start
  0.6 1.8 %prepare.1 = (bf16[32,512]{1,0:T(8,128)(2,1)}, f32[8,512]{1,0:T(8,128)}, f32[8,512]{1,0:T(8,128)}) custom-call(s32[4]{0:T(128)} %refs_0_.4, f32[3,768,512]{2,1,0:T(8,128)} %refs_2_.1, f32[3,768,512]{2,1,0:T(8,128)} %refs_2_.1, s32[4,512]{1,0:T(4,128)} %refs_3_.1, f32[4,512]{1,0:T(4,128)} %refs_4_.1, f32[512]{0:T(512)} %refs_5_.1), custom_call_target="tpu_custom_call" | custom-call | tf_op jit(solution)/shard_map/prepare/pallas_call | solution.py:383
  2.4 4.0 %collective-permute-start.2 = (bf16[32,512]{1,0:T(8,128)(2,1)}, bf16[32,512]{1,0:T(8,128)(2,1)S(1)}, u32[]{:S(2)}, u32[]{:S(2)}) collective-permute-start(bf16[32,512]{1,0:T(8,128)(2,1)} %get-tuple-element.19.refs_4_.request), channel_id=1, source_target_pairs={{3,0},{2,1},{1,2},{0,3},{7,4},{6,5},{5,6},{4,7},{11,8},{10,9},{9,1... | collective-permute-start | bytes 98312 | tf_op jit(solution)/shard_map/ppermute | solution.py:364
  6.4 0.5 %collective-permute-start.3 = (bf16[32,512]{1,0:T(8,128)(2,1)}, bf16[32,512]{1,0:T(8,128)(2,1)S(1)}, u32[]{:S(2)}, u32[]{:S(2)}) collective-permute-start(bf16[32,512]{1,0:T(8,128)(2,1)} %get-tuple-element.19.refs_4_.request), channel_id=1, source_target_pairs={{1,0},{0,1},{3,2},{2,3},{5,4},{4,5},{7,6},{6,7},{9,8},{8,9},{11,10... | collective-permute-start | bytes 98312 | tf_op jit(solution)/shard_map/ppermute | solution.py:364
  6.9 0.1 collective-permute-start.4
  7.0 2.6 %collective-permute-start = (f32[8,512]{1,0:T(8,128)}, f32[8,512]{1,0:T(8,128)S(1)}, u32[]{:S(2)}, u32[]{:S(2)}) collective-permute-start(f32[8,512]{1,0:T(8,128)} %get-tuple-element.16), channel_id=1, source_target_pairs={{0,28},{4,8},{8,4},{12,16},{16,12},{20,24},{24,20},{28,0},{1,29},{... | collective-permute-start | bytes 49160 | tf_op jit(solution)/shard_map/ppermute | solution.py:364
  9.6 0.0 collective-permute-start.1
  9.6 0.0 copy-done
  9.6 3.1 %table.1 = (f32[3,768,512]{2,1,0:T(8,128)S(1)}, bf16[4,768,768]{2,1,0:T(8,128)(2,1)S(1)}) custom-call(f32[3,768,512]{2,1,0:T(8,128)} %refs_2_.1, bf16[3,192,256]{2,1,0:T(8,128)(2,1)S(1)} %copy-done), custom_call_target="tpu_custom_call" | custom-call | flops 603979776 | bytes 9437184 | tf_op jit(solution)/shard_map/table/pallas_call | solution.py:424
  12.7 0.0 collective-permute-done.refs_1_
  12.7 0.0 collective-permute-done.1.refs_2_
  12.7 0.0 collective-permute-done.2.refs_5_
  12.7 0.0 collective-permute-done.3.refs_6_
  12.8 0.0 collective-permute-done.4.refs_7_
  12.8 0.0 copy-done.1
  12.8 3.3 %lookup.1 = (f32[8,512]{1,0:T(8,128)S(1)}, f32[8,512]{1,0:T(8,128)S(1)}, f32[8,512]{1,0:T(8,128)S(1)}, f32[8,512]{1,0:T(8,128)S(1)}, f32[16,512]{1,0:T(8,128)S(1)}) custom-call(s32[1,16]{1,0:T(1,128)S(1)} %copy-done.4, f32[8,512]{1,0:T(8,128)S(1)} %collective-permute-done.refs_1_, f32[8,512]{1,0:T(8,128)S(1)} %collective-permute-done.1.refs_2_, ...), custom_call_target="tpu_custom_call" | custom-call | flops 7247757312 | bytes 2359296 | tf_op jit(solution)/shard_map/lookup/pallas_call | solution.py:440
  16.0 2.5 %collective-permute-start.5 = (f32[8,512]{1,0:T(8,128)S(1)}, f32[8,512]{1,0:T(8,128)S(1)}, u32[]{:S(2)}, u32[]{:S(2)}) collective-permute-start(f32[8,512]{1,0:T(8,128)S(1)} %get-tuple-element.22), channel_id=1, source_target_pairs={{0,3},{1,2},{2,1},{3,0},{4,7},{5,6},{6,5},{7,4},{8,11},{9,10},{10,... | collective-permute-start | bytes 49160 | tf_op jit(solution)/shard_map/ppermute | solution.py:364
  18.5 0.0 collective-permute-start.6
  18.5 1.1 %collective-permute-start.7 = (f32[8,512]{1,0:T(8,128)S(1)}, f32[8,512]{1,0:T(8,128)S(1)}, u32[]{:S(2)}, u32[]{:S(2)}) collective-permute-start(f32[8,512]{1,0:T(8,128)S(1)} %get-tuple-element.24), channel_id=1, source_target_pairs={{0,2},{1,3},{2,0},{3,1},{4,6},{5,7},{6,4},{7,5},{8,10},{9,11},{10,... | collective-permute-start | bytes 49160 | tf_op jit(solution)/shard_map/ppermute | solution.py:364
  19.6 2.7 %derivative.1 = f32[3,768,512]{2,1,0:T(8,128)} custom-call(f32[3,768,512]{2,1,0:T(8,128)S(1)} %get-tuple-element.15.refs_0_, bf16[3,192,256]{2,1,0:T(8,128)(2,1)S(1)} %copy-done, f32[16,512]{1,0:T(8,128)S(1)} %get-tuple-element.20.refs_2_), custom_call_target="tpu_custom_call" | custom-call | flops 1811939328 | bytes 9437184 | tf_op jit(solution)/shard_map/derivative/pallas_call | solution.py:460
  22.3 0.0 collective-permute-done.5.refs_1_
  22.3 0.0 collective-permute-done.6.refs_2_
  22.3 0.0 collective-permute-done.7.refs_3_
  22.3 0.6 %finish.1 = (f32[3,512]{1,0:T(4,128)}, f32[3,512]{1,0:T(4,128)}) custom-call(bf16[32,512]{1,0:T(8,128)(2,1)S(1)} %copy-done.1, f32[512]{0:T(512)S(1)} %copy-done.3, f32[3,512]{1,0:T(4,128)S(1)} %copy-done.2, f32[8,512]{1,0:T(8,128)S(1)} %get-tuple-element.21.refs_0_, f32[8,512]{1,0:T(8,128)S(1)} %collective-permute-done.5.refs_1_, ...), custom_call_target="tpu_custom_call" | custom-call | tf_op jit(solution)/shard_map/finish/pallas_call | solution.py:480
  (7 shorter events, 0.0 us)
Async XLA Ops:
  0.6 9.0 %copy-start = (bf16[3,192,256]{2,1,0:T(8,128)(2,1)S(1)}, bf16[3,192,256]{2,1,0:T(8,128)(2,1)}, u32[]{:S(2)}) copy-start(bf16[3,192,256]{2,1,0:T(8,128)(2,1)} %constant.2.clone.refs_1_) | copy-start | bytes 884740
  2.4 10.3 %copy-start.1 = (bf16[32,512]{1,0:T(8,128)(2,1)S(1)}, bf16[32,512]{1,0:T(8,128)(2,1)}, u32[]{:S(2)}) copy-start(bf16[32,512]{1,0:T(8,128)(2,1)} %get-tuple-element.19.refs_4_.request) | copy-start | bytes 98308
  2.4 10.3 %copy-start.4 = (s32[1,16]{1,0:T(1,128)S(1)}, s32[1,16]{1,0:T(1,128)}, u32[]{:S(2)}) copy-start(s32[1,16]{1,0:T(1,128)} %refs_0_.5) | copy-start | bytes 196
  2.4 10.3 %collective-permute-start.2 = (bf16[32,512]{1,0:T(8,128)(2,1)}, bf16[32,512]{1,0:T(8,128)(2,1)S(1)}, u32[]{:S(2)}, u32[]{:S(2)}) collective-permute-start(bf16[32,512]{1,0:T(8,128)(2,1)} %get-tuple-element.19.refs_4_.request), channel_id=1, source_target_pairs={{3,0},{2,1},{1,2},{0,3},{7,4},{6,5},{5,6},{4,7},{11,8},{10,9},{9,1... | collective-permute-start | bytes 98312 | tf_op jit(solution)/shard_map/ppermute | solution.py:364
  6.4 6.4 %collective-permute-start.3 = (bf16[32,512]{1,0:T(8,128)(2,1)}, bf16[32,512]{1,0:T(8,128)(2,1)S(1)}, u32[]{:S(2)}, u32[]{:S(2)}) collective-permute-start(bf16[32,512]{1,0:T(8,128)(2,1)} %get-tuple-element.19.refs_4_.request), channel_id=1, source_target_pairs={{1,0},{0,1},{3,2},{2,3},{5,4},{4,5},{7,6},{6,7},{9,8},{8,9},{11,10... | collective-permute-start | bytes 98312 | tf_op jit(solution)/shard_map/ppermute | solution.py:364
  6.9 5.8 %collective-permute-start.4 = (bf16[32,512]{1,0:T(8,128)(2,1)}, bf16[32,512]{1,0:T(8,128)(2,1)S(1)}, u32[]{:S(2)}, u32[]{:S(2)}) collective-permute-start(bf16[32,512]{1,0:T(8,128)(2,1)} %get-tuple-element.19.refs_4_.request), channel_id=1, source_target_pairs={{2,0},{3,1},{0,2},{1,3},{6,4},{7,5},{4,6},{5,7},{10,8},{11,9},{8,1... | collective-permute-start | bytes 98312 | tf_op jit(solution)/shard_map/ppermute | solution.py:364
  7.0 5.7 %collective-permute-start = (f32[8,512]{1,0:T(8,128)}, f32[8,512]{1,0:T(8,128)S(1)}, u32[]{:S(2)}, u32[]{:S(2)}) collective-permute-start(f32[8,512]{1,0:T(8,128)} %get-tuple-element.16), channel_id=1, source_target_pairs={{0,28},{4,8},{8,4},{12,16},{16,12},{20,24},{24,20},{28,0},{1,29},{... | collective-permute-start | bytes 49160 | tf_op jit(solution)/shard_map/ppermute | solution.py:364
  9.6 3.1 %collective-permute-start.1 = (f32[8,512]{1,0:T(8,128)}, f32[8,512]{1,0:T(8,128)S(1)}, u32[]{:S(2)}, u32[]{:S(2)}) collective-permute-start(f32[8,512]{1,0:T(8,128)} %get-tuple-element.17), channel_id=1, source_target_pairs={{0,4},{4,0},{8,12},{12,8},{16,20},{20,16},{24,28},{28,24},{1,5},{5... | collective-permute-start | bytes 49160 | tf_op jit(solution)/shard_map/ppermute | solution.py:364
  16.0 6.2 %collective-permute-start.5 = (f32[8,512]{1,0:T(8,128)S(1)}, f32[8,512]{1,0:T(8,128)S(1)}, u32[]{:S(2)}, u32[]{:S(2)}) collective-permute-start(f32[8,512]{1,0:T(8,128)S(1)} %get-tuple-element.22), channel_id=1, source_target_pairs={{0,3},{1,2},{2,1},{3,0},{4,7},{5,6},{6,5},{7,4},{8,11},{9,10},{10,... | collective-permute-start | bytes 49160 | tf_op jit(solution)/shard_map/ppermute | solution.py:364
  18.5 3.8 %collective-permute-start.6 = (f32[8,512]{1,0:T(8,128)S(1)}, f32[8,512]{1,0:T(8,128)S(1)}, u32[]{:S(2)}, u32[]{:S(2)}) collective-permute-start(f32[8,512]{1,0:T(8,128)S(1)} %get-tuple-element.23), channel_id=1, source_target_pairs={{0,1},{1,0},{2,3},{3,2},{4,5},{5,4},{6,7},{7,6},{8,9},{9,8},{10,11... | collective-permute-start | bytes 49160 | tf_op jit(solution)/shard_map/ppermute | solution.py:364
  18.5 3.8 %collective-permute-start.7 = (f32[8,512]{1,0:T(8,128)S(1)}, f32[8,512]{1,0:T(8,128)S(1)}, u32[]{:S(2)}, u32[]{:S(2)}) collective-permute-start(f32[8,512]{1,0:T(8,128)S(1)} %get-tuple-element.24), channel_id=1, source_target_pairs={{0,2},{1,3},{2,0},{3,1},{4,6},{5,7},{6,4},{7,5},{8,10},{9,11},{10,... | collective-permute-start | bytes 49160 | tf_op jit(solution)/shard_map/ppermute | solution.py:364
  19.6 2.7 %copy-start.2 = (f32[3,512]{1,0:T(4,128)S(1)}, f32[3,512]{1,0:T(4,128)}, u32[]{:S(2)}) copy-start(f32[3,512]{1,0:T(4,128)} %particle.1) | copy-start | bytes 18436
  19.6 2.7 %copy-start.3 = (f32[512]{0:T(512)S(1)}, f32[512]{0:T(512)}, u32[]{:S(2)}) copy-start(f32[512]{0:T(512)} %relax.1) | copy-start | bytes 6148

commit v7 on v6

--- a/solution.py
+++ b/solution.py
@@ -11,7 +11,7 @@
 ROWB = 128
 PSIZE = 128
 STEN = 4
-EDGE = 32
+EDGE = 24
 ROWS = 192
 CHUNK = 64
 EXTRA = 2
@@ -55,12 +55,16 @@
     return (np.sign(distance) * TAPS[np.abs(distance)] / SCALE).astype(BF16)
 
 
-def edge_state(rows, from_first):
-    index = lax.broadcasted_iota(jnp.int32, rows.shape, 0)
+def edge_state(rows, decay):
+    return jnp.sum(rows * decay, 0, keepdims=True)
+
+
+def edge_decay(lines, from_first):
+    index = lax.broadcasted_iota(jnp.int32, (EDGE, ROWB), 0)
     steps = index + 1 if from_first else EDGE - index
     parity = 1.0 - 2.0 * (steps & 1).astype(F32)
     decay = parity * jnp.exp(steps.astype(F32) * math.log(R_DECAY))
-    return jnp.sum(rows * decay, 0, keepdims=True)
+    return jnp.concatenate([decay] * (lines // ROWB), 1)
 
 
 def even_column():
@@ -75,11 +79,12 @@
 
 def prep_body(x_cells, live, head, tail, cells, weights, offsets, request, to_chip, to_next):
     zero = jnp.zeros((2, head.shape[2]), F32)
+    from_head, from_tail = edge_decay(head.shape[2], True), edge_decay(head.shape[2], False)
     to_left = jnp.concatenate(
-        [edge_state(head[c], True) for c in range(3)] + [head[c, 0:1, :] for c in range(3)] + [zero], 0
+        [edge_state(head[c], from_head) for c in range(3)] + [head[c, 0:1, :] for c in range(3)] + [zero], 0
     )
     to_right = jnp.concatenate(
-        [edge_state(tail[c], False) for c in range(3)]
+        [edge_state(tail[c], from_tail) for c in range(3)]
         + [tail[c, EDGE - 1 : EDGE, :] for c in range(3)]
         + [zero],
         0,
@@ -415,7 +420,7 @@
     window = min(256, x_cells)
     plan, kinds = [], []
     for row in range(0, x_cells, ROWS):
-        start = min(max(row - EDGE, 0), x_cells - window)
+        start = min(max(row - 32, 0), x_cells - window)
         if row - start not in kinds:
             kinds.append(row - start)
         plan.append((row, start, kinds.index(row - start)))

time: 23.3 us -> 23.3 us (level)
  no operation moved by 1% of the time
where the time goes in v7:
time: 23.3 us; the launch traced here: 22.9 us
  Pallas kernels  11.3 us (48%)
  starting transfers between devices  10.8 us (46%)
  between operations  0.75 us (3%)
    ppermute x8, starting transfers between devices, sent(): return lax.ppermute(values, axis, pairs)  10.8 us
    pallas_call x1, Pallas kernels, per_device(): pl.pallas_call(lambda *refs: lookup_body(owners, xor, [0] + far_first, *r...  3.25 us
    pallas_call x1, Pallas kernels, per_device(): pl.pallas_call(lambda *refs: table_body(plan, *refs), in_specs=[hbm, vmem...  3.05 us
    pallas_call x1, Pallas kernels, per_device(): pl.pallas_call(lambda *refs: derivative_body(plan, *refs), in_specs=[vmem...  2.66 us
    pallas_call x1, Pallas kernels, per_device(): pl.pallas_call(lambda *refs: prep_body(x_cells, *refs), grid=(1,), in_spe...  1.75 us
    pallas_call x1, Pallas kernels, per_device(): pl.pallas_call(final_body, in_specs=[vmem] * (3 + owners), out_specs=[vme...  0.62 us
  transfers between devices with their start and end apart: 8, of which 0 were waited for; matrix products, arithmetic and copies ran while one was open for 0% of the time, Pallas kernels for 25%

profile of v7, /device:TPU:0, one launch (start us, length us, event | category | flops | bytes accessed | tf_op | source)
XLA Modules:
  0.0 22.9 jit_solution(14371802288139515093)
XLA Ops:
  0.6 0.0 copy-start
  0.6 1.8 %prepare.1 = (bf16[32,512]{1,0:T(8,128)(2,1)}, f32[8,512]{1,0:T(8,128)}, f32[8,512]{1,0:T(8,128)}) custom-call(s32[4]{0:T(128)} %refs_0_.4, f32[3,768,512]{2,1,0:T(8,128)} %refs_2_.1, f32[3,768,512]{2,1,0:T(8,128)} %refs_2_.1, s32[4,512]{1,0:T(4,128)} %refs_3_.1, f32[4,512]{1,0:T(4,128)} %refs_4_.1, f32[512]{0:T(512)} %refs_5_.1), custom_call_target="tpu_custom_call" | custom-call | tf_op jit(solution)/shard_map/prepare/pallas_call | solution.py:388
  2.4 4.0 %collective-permute-start.2 = (bf16[32,512]{1,0:T(8,128)(2,1)}, bf16[32,512]{1,0:T(8,128)(2,1)S(1)}, u32[]{:S(2)}, u32[]{:S(2)}) collective-permute-start(bf16[32,512]{1,0:T(8,128)(2,1)} %get-tuple-element.19.refs_4_.request), channel_id=1, source_target_pairs={{3,0},{2,1},{1,2},{0,3},{7,4},{6,5},{5,6},{4,7},{11,8},{10,9},{9,1... | collective-permute-start | bytes 98312 | tf_op jit(solution)/shard_map/ppermute | solution.py:369
  6.4 0.5 %collective-permute-start.3 = (bf16[32,512]{1,0:T(8,128)(2,1)}, bf16[32,512]{1,0:T(8,128)(2,1)S(1)}, u32[]{:S(2)}, u32[]{:S(2)}) collective-permute-start(bf16[32,512]{1,0:T(8,128)(2,1)} %get-tuple-element.19.refs_4_.request), channel_id=1, source_target_pairs={{1,0},{0,1},{3,2},{2,3},{5,4},{4,5},{7,6},{6,7},{9,8},{8,9},{11,10... | collective-permute-start | bytes 98312 | tf_op jit(solution)/shard_map/ppermute | solution.py:369
  6.9 0.1 collective-permute-start.4
  7.0 2.6 %collective-permute-start = (f32[8,512]{1,0:T(8,128)}, f32[8,512]{1,0:T(8,128)S(1)}, u32[]{:S(2)}, u32[]{:S(2)}) collective-permute-start(f32[8,512]{1,0:T(8,128)} %get-tuple-element.16), channel_id=1, source_target_pairs={{0,28},{4,8},{8,4},{12,16},{16,12},{20,24},{24,20},{28,0},{1,29},{... | collective-permute-start | bytes 49160 | tf_op jit(solution)/shard_map/ppermute | solution.py:369
  9.6 0.0 collective-permute-start.1
  9.6 3.1 %table.1 = (f32[3,768,512]{2,1,0:T(8,128)S(1)}, bf16[4,768,768]{2,1,0:T(8,128)(2,1)S(1)}) custom-call(f32[3,768,512]{2,1,0:T(8,128)} %refs_2_.1, bf16[3,192,256]{2,1,0:T(8,128)(2,1)S(1)} %copy-done), custom_call_target="tpu_custom_call" | custom-call | flops 603979776 | bytes 9437184 | tf_op jit(solution)/shard_map/table/pallas_call | solution.py:429
  12.7 0.0 collective-permute-done.refs_1_
  12.7 0.0 collective-permute-done.1.refs_2_
  12.7 0.0 collective-permute-done.2.refs_5_
  12.7 0.0 collective-permute-done.3.refs_6_
  12.7 0.0 collective-permute-done.4.refs_7_
  12.7 3.3 %lookup.1 = (f32[8,512]{1,0:T(8,128)S(1)}, f32[8,512]{1,0:T(8,128)S(1)}, f32[8,512]{1,0:T(8,128)S(1)}, f32[8,512]{1,0:T(8,128)S(1)}, f32[16,512]{1,0:T(8,128)S(1)}) custom-call(s32[1,16]{1,0:T(1,128)S(1)} %copy-done.4, f32[8,512]{1,0:T(8,128)S(1)} %collective-permute-done.refs_1_, f32[8,512]{1,0:T(8,128)S(1)} %collective-permute-done.1.refs_2_, ...), custom_call_target="tpu_custom_call" | custom-call | flops 7247757312 | bytes 2359296 | tf_op jit(solution)/shard_map/lookup/pallas_call | solution.py:445
  16.0 2.5 %collective-permute-start.5 = (f32[8,512]{1,0:T(8,128)S(1)}, f32[8,512]{1,0:T(8,128)S(1)}, u32[]{:S(2)}, u32[]{:S(2)}) collective-permute-start(f32[8,512]{1,0:T(8,128)S(1)} %get-tuple-element.22), channel_id=1, source_target_pairs={{0,3},{1,2},{2,1},{3,0},{4,7},{5,6},{6,5},{7,4},{8,11},{9,10},{10,... | collective-permute-start | bytes 49160 | tf_op jit(solution)/shard_map/ppermute | solution.py:369
  18.5 0.0 collective-permute-start.6
  18.5 1.0 %collective-permute-start.7 = (f32[8,512]{1,0:T(8,128)S(1)}, f32[8,512]{1,0:T(8,128)S(1)}, u32[]{:S(2)}, u32[]{:S(2)}) collective-permute-start(f32[8,512]{1,0:T(8,128)S(1)} %get-tuple-element.24), channel_id=1, source_target_pairs={{0,2},{1,3},{2,0},{3,1},{4,6},{5,7},{6,4},{7,5},{8,10},{9,11},{10,... | collective-permute-start | bytes 49160 | tf_op jit(solution)/shard_map/ppermute | solution.py:369
  19.6 2.7 %derivative.1 = f32[3,768,512]{2,1,0:T(8,128)} custom-call(f32[3,768,512]{2,1,0:T(8,128)S(1)} %get-tuple-element.15.refs_0_, bf16[3,192,256]{2,1,0:T(8,128)(2,1)S(1)} %copy-done, f32[16,512]{1,0:T(8,128)S(1)} %get-tuple-element.20.refs_2_), custom_call_target="tpu_custom_call" | custom-call | flops 1811939328 | bytes 9437184 | tf_op jit(solution)/shard_map/derivative/pallas_call | solution.py:465
  22.2 0.0 collective-permute-done.5.refs_1_
  22.2 0.0 collective-permute-done.6.refs_2_
  22.2 0.0 collective-permute-done.7.refs_3_
  22.3 0.0 copy-done.2
  22.3 0.0 copy-done.3
  22.3 0.6 %finish.1 = (f32[3,512]{1,0:T(4,128)}, f32[3,512]{1,0:T(4,128)}) custom-call(bf16[32,512]{1,0:T(8,128)(2,1)S(1)} %copy-done.1, f32[512]{0:T(512)S(1)} %copy-done.3, f32[3,512]{1,0:T(4,128)S(1)} %copy-done.2, f32[8,512]{1,0:T(8,128)S(1)} %get-tuple-element.21.refs_0_, f32[8,512]{1,0:T(8,128)S(1)} %collective-permute-done.5.refs_1_, ...), custom_call_target="tpu_custom_call" | custom-call | tf_op jit(solution)/shard_map/finish/pallas_call | solution.py:485
  (7 shorter events, 0.0 us)
Async XLA Ops:
  0.6 9.0 %copy-start = (bf16[3,192,256]{2,1,0:T(8,128)(2,1)S(1)}, bf16[3,192,256]{2,1,0:T(8,128)(2,1)}, u32[]{:S(2)}) copy-start(bf16[3,192,256]{2,1,0:T(8,128)(2,1)} %constant.2.clone.refs_1_) | copy-start | bytes 884740
  2.4 10.3 %copy-start.1 = (bf16[32,512]{1,0:T(8,128)(2,1)S(1)}, bf16[32,512]{1,0:T(8,128)(2,1)}, u32[]{:S(2)}) copy-start(bf16[32,512]{1,0:T(8,128)(2,1)} %get-tuple-element.19.refs_4_.request) | copy-start | bytes 98308
  2.4 10.3 %copy-start.4 = (s32[1,16]{1,0:T(1,128)S(1)}, s32[1,16]{1,0:T(1,128)}, u32[]{:S(2)}) copy-start(s32[1,16]{1,0:T(1,128)} %refs_0_.5) | copy-start | bytes 196
  2.4 10.3 %collective-permute-start.2 = (bf16[32,512]{1,0:T(8,128)(2,1)}, bf16[32,512]{1,0:T(8,128)(2,1)S(1)}, u32[]{:S(2)}, u32[]{:S(2)}) collective-permute-start(bf16[32,512]{1,0:T(8,128)(2,1)} %get-tuple-element.19.refs_4_.request), channel_id=1, source_target_pairs={{3,0},{2,1},{1,2},{0,3},{7,4},{6,5},{5,6},{4,7},{11,8},{10,9},{9,1... | collective-permute-start | bytes 98312 | tf_op jit(solution)/shard_map/ppermute | solution.py:369
  6.4 6.3 %collective-permute-start.3 = (bf16[32,512]{1,0:T(8,128)(2,1)}, bf16[32,512]{1,0:T(8,128)(2,1)S(1)}, u32[]{:S(2)}, u32[]{:S(2)}) collective-permute-start(bf16[32,512]{1,0:T(8,128)(2,1)} %get-tuple-element.19.refs_4_.request), channel_id=1, source_target_pairs={{1,0},{0,1},{3,2},{2,3},{5,4},{4,5},{7,6},{6,7},{9,8},{8,9},{11,10... | collective-permute-start | bytes 98312 | tf_op jit(solution)/shard_map/ppermute | solution.py:369
  6.9 5.8 %collective-permute-start.4 = (bf16[32,512]{1,0:T(8,128)(2,1)}, bf16[32,512]{1,0:T(8,128)(2,1)S(1)}, u32[]{:S(2)}, u32[]{:S(2)}) collective-permute-start(bf16[32,512]{1,0:T(8,128)(2,1)} %get-tuple-element.19.refs_4_.request), channel_id=1, source_target_pairs={{2,0},{3,1},{0,2},{1,3},{6,4},{7,5},{4,6},{5,7},{10,8},{11,9},{8,1... | collective-permute-start | bytes 98312 | tf_op jit(solution)/shard_map/ppermute | solution.py:369
  7.0 5.7 %collective-permute-start = (f32[8,512]{1,0:T(8,128)}, f32[8,512]{1,0:T(8,128)S(1)}, u32[]{:S(2)}, u32[]{:S(2)}) collective-permute-start(f32[8,512]{1,0:T(8,128)} %get-tuple-element.16), channel_id=1, source_target_pairs={{0,28},{4,8},{8,4},{12,16},{16,12},{20,24},{24,20},{28,0},{1,29},{... | collective-permute-start | bytes 49160 | tf_op jit(solution)/shard_map/ppermute | solution.py:369
  9.6 3.1 %collective-permute-start.1 = (f32[8,512]{1,0:T(8,128)}, f32[8,512]{1,0:T(8,128)S(1)}, u32[]{:S(2)}, u32[]{:S(2)}) collective-permute-start(f32[8,512]{1,0:T(8,128)} %get-tuple-element.17), channel_id=1, source_target_pairs={{0,4},{4,0},{8,12},{12,8},{16,20},{20,16},{24,28},{28,24},{1,5},{5... | collective-permute-start | bytes 49160 | tf_op jit(solution)/shard_map/ppermute | solution.py:369
  16.0 6.2 %collective-permute-start.5 = (f32[8,512]{1,0:T(8,128)S(1)}, f32[8,512]{1,0:T(8,128)S(1)}, u32[]{:S(2)}, u32[]{:S(2)}) collective-permute-start(f32[8,512]{1,0:T(8,128)S(1)} %get-tuple-element.22), channel_id=1, source_target_pairs={{0,3},{1,2},{2,1},{3,0},{4,7},{5,6},{6,5},{7,4},{8,11},{9,10},{10,... | collective-permute-start | bytes 49160 | tf_op jit(solution)/shard_map/ppermute | solution.py:369
  18.5 3.7 %collective-permute-start.6 = (f32[8,512]{1,0:T(8,128)S(1)}, f32[8,512]{1,0:T(8,128)S(1)}, u32[]{:S(2)}, u32[]{:S(2)}) collective-permute-start(f32[8,512]{1,0:T(8,128)S(1)} %get-tuple-element.23), channel_id=1, source_target_pairs={{0,1},{1,0},{2,3},{3,2},{4,5},{5,4},{6,7},{7,6},{8,9},{9,8},{10,11... | collective-permute-start | bytes 49160 | tf_op jit(solution)/shard_map/ppermute | solution.py:369
  18.5 3.7 %collective-permute-start.7 = (f32[8,512]{1,0:T(8,128)S(1)}, f32[8,512]{1,0:T(8,128)S(1)}, u32[]{:S(2)}, u32[]{:S(2)}) collective-permute-start(f32[8,512]{1,0:T(8,128)S(1)} %get-tuple-element.24), channel_id=1, source_target_pairs={{0,2},{1,3},{2,0},{3,1},{4,6},{5,7},{6,4},{7,5},{8,10},{9,11},{10,... | collective-permute-start | bytes 49160 | tf_op jit(solution)/shard_map/ppermute | solution.py:369
  19.6 2.7 %copy-start.2 = (f32[3,512]{1,0:T(4,128)S(1)}, f32[3,512]{1,0:T(4,128)}, u32[]{:S(2)}) copy-start(f32[3,512]{1,0:T(4,128)} %particle.1) | copy-start | bytes 18436
  19.6 2.7 %copy-start.3 = (f32[512]{0:T(512)S(1)}, f32[512]{0:T(512)}, u32[]{:S(2)}) copy-start(f32[512]{0:T(512)} %relax.1) | copy-start | bytes 6148

commit v8 on v6

--- a/solution.py
+++ b/solution.py
@@ -409,7 +409,7 @@
 
     far_first = sorted(range(1, owners), key=lambda k: -bin(k).count("1"))
     requests = [request] + [
-        sent(request, "gy", [(peer(i, k), i) for i in range(owners)]) for k in far_first
+        sent(request, "gy", [(peer(i, k), i) for i in range(owners)]) for k in range(1, owners)
     ]
 
     window = min(256, x_cells)
@@ -438,7 +438,7 @@
     )(velocity, matrices)
 
     *partials, sides = pl.pallas_call(
-        lambda *refs: lookup_body(owners, xor, [0] + far_first, *refs),
+        lambda *refs: lookup_body(owners, xor, list(range(owners)), *refs),
         in_specs=[vmem] * (4 + owners),
         out_specs=[vmem] * (owners + 1),
         out_shape=[jax.ShapeDtypeStruct((8, slots), F32)] * owners

time: 23.3 us -> 23.6 us (1.013)
  waiting for transfers between devices: 0.02 us -> 1.06 us
  Pallas kernels: 11.4 us -> 10.6 us
    ppermute x8, waiting for transfers between devices: 0.02 us -> 1.06 us  [sent(): return lax.ppermute(values, axis, pairs)]
    pallas_call x1, Pallas kernels: 3.25 us -> 2.44 us  [per_device(): pl.pallas_call(lambda *refs: lookup_body(owners, xor, list(range(owners))...]
    ppermute x8, starting transfers between devices: 10.8 us -> 11 us  [sent(): return lax.ppermute(values, axis, pairs)]
  transfers between devices with their start and end apart: 8 -> 8, of which waited for: 0 -> 1; matrix products, arithmetic and copies ran while one was open for 0% -> 0% of each run, Pallas kernels for 25% -> 24%
where the time goes in v8:
time: 23.6 us; the launch traced here: 23.4 us
  starting transfers between devices  11 us (47%)
  Pallas kernels  10.6 us (45%)
  waiting for transfers between devices  1.06 us (4%)
  between operations  0.74 us (3%)
    ppermute x8, starting transfers between devices, sent(): return lax.ppermute(values, axis, pairs)  11 us
    pallas_call x1, Pallas kernels, per_device(): pl.pallas_call(lambda *refs: table_body(plan, *refs), in_specs=[hbm, vmem...  3.05 us
    pallas_call x1, Pallas kernels, per_device(): pl.pallas_call(lambda *refs: derivative_body(plan, *refs), in_specs=[vmem...  2.66 us
    pallas_call x1, Pallas kernels, per_device(): pl.pallas_call(lambda *refs: lookup_body(owners, xor, list(range(owners))...  2.44 us
    pallas_call x1, Pallas kernels, per_device(): pl.pallas_call(lambda *refs: prep_body(x_cells, *refs), grid=(1,), in_spe...  1.79 us
    ppermute x8, waiting for transfers between devices, sent(): return lax.ppermute(values, axis, pairs)  1.06 us
    pallas_call x1, Pallas kernels, per_device(): pl.pallas_call(final_body, in_specs=[vmem] * (3 + owners), out_specs=[vme...  0.62 us
  transfers between devices with their start and end apart: 8, of which 1 were waited for; matrix products, arithmetic and copies ran while one was open for 0% of the time, Pallas kernels for 24%

profile of v8, /device:TPU:0, one launch (start us, length us, event | category | flops | bytes accessed | tf_op | source)
XLA Modules:
  0.0 23.4 jit_solution(12593716368976730901)
XLA Ops:
  0.6 0.0 copy-start
  0.6 1.8 %prepare.1 = (bf16[32,512]{1,0:T(8,128)(2,1)}, f32[8,512]{1,0:T(8,128)}, f32[8,512]{1,0:T(8,128)}) custom-call(s32[4]{0:T(128)} %refs_0_.4, f32[3,768,512]{2,1,0:T(8,128)} %refs_2_.1, f32[3,768,512]{2,1,0:T(8,128)} %refs_2_.1, s32[4,512]{1,0:T(4,128)} %refs_3_.1, f32[4,512]{1,0:T(4,128)} %refs_4_.1, f32[512]{0:T(512)} %refs_5_.1), custom_call_target="tpu_custom_call" | custom-call | tf_op jit(solution)/shard_map/prepare/pallas_call | solution.py:383
  2.4 3.0 %collective-permute-start.2 = (bf16[32,512]{1,0:T(8,128)(2,1)}, bf16[32,512]{1,0:T(8,128)(2,1)S(1)}, u32[]{:S(2)}, u32[]{:S(2)}) collective-permute-start(bf16[32,512]{1,0:T(8,128)(2,1)} %get-tuple-element.19.refs_4_.request), channel_id=1, source_target_pairs={{1,0},{0,1},{3,2},{2,3},{5,4},{4,5},{7,6},{6,7},{9,8},{8,9},{11,10... | collective-permute-start | bytes 98312 | tf_op jit(solution)/shard_map/ppermute | solution.py:364
  5.4 1.5 %collective-permute-start.3 = (bf16[32,512]{1,0:T(8,128)(2,1)}, bf16[32,512]{1,0:T(8,128)(2,1)S(1)}, u32[]{:S(2)}, u32[]{:S(2)}) collective-permute-start(bf16[32,512]{1,0:T(8,128)(2,1)} %get-tuple-element.19.refs_4_.request), channel_id=1, source_target_pairs={{2,0},{3,1},{0,2},{1,3},{6,4},{7,5},{4,6},{5,7},{10,8},{11,9},{8,1... | collective-permute-start | bytes 98312 | tf_op jit(solution)/shard_map/ppermute | solution.py:364
  7.0 0.0 collective-permute-start.4
  7.0 2.7 %collective-permute-start = (f32[8,512]{1,0:T(8,128)}, f32[8,512]{1,0:T(8,128)S(1)}, u32[]{:S(2)}, u32[]{:S(2)}) collective-permute-start(f32[8,512]{1,0:T(8,128)} %get-tuple-element.16), channel_id=1, source_target_pairs={{0,28},{4,8},{8,4},{12,16},{16,12},{20,24},{24,20},{28,0},{1,29},{... | collective-permute-start | bytes 49160 | tf_op jit(solution)/shard_map/ppermute | solution.py:364
  9.6 0.0 collective-permute-start.1
  9.6 0.0 copy-done
  9.6 3.1 %table.1 = (f32[3,768,512]{2,1,0:T(8,128)S(1)}, bf16[4,768,768]{2,1,0:T(8,128)(2,1)S(1)}) custom-call(f32[3,768,512]{2,1,0:T(8,128)} %refs_2_.1, bf16[3,192,256]{2,1,0:T(8,128)(2,1)S(1)} %copy-done), custom_call_target="tpu_custom_call" | custom-call | flops 603979776 | bytes 9437184 | tf_op jit(solution)/shard_map/table/pallas_call | solution.py:424
  12.7 0.0 collective-permute-done.refs_1_
  12.7 0.0 collective-permute-done.1.refs_2_
  12.7 0.0 collective-permute-done.2.refs_5_
  12.7 0.0 collective-permute-done.3.refs_6_
  12.7 0.0 collective-permute-done.4.refs_7_
  12.8 0.0 copy-done.1
  12.8 2.4 %lookup.1 = (f32[8,512]{1,0:T(8,128)S(1)}, f32[8,512]{1,0:T(8,128)S(1)}, f32[8,512]{1,0:T(8,128)S(1)}, f32[8,512]{1,0:T(8,128)S(1)}, f32[16,512]{1,0:T(8,128)S(1)}) custom-call(s32[1,16]{1,0:T(1,128)S(1)} %copy-done.4, f32[8,512]{1,0:T(8,128)S(1)} %collective-permute-done.refs_1_, f32[8,512]{1,0:T(8,128)S(1)} %collective-permute-done.1.refs_2_, ...), custom_call_target="tpu_custom_call" | custom-call | flops 7247757312 | bytes 2359296 | tf_op jit(solution)/shard_map/lookup/pallas_call | solution.py:440
  15.2 2.5 %collective-permute-start.5 = (f32[8,512]{1,0:T(8,128)S(1)}, f32[8,512]{1,0:T(8,128)S(1)}, u32[]{:S(2)}, u32[]{:S(2)}) collective-permute-start(f32[8,512]{1,0:T(8,128)S(1)} %get-tuple-element.22), channel_id=1, source_target_pairs={{0,3},{1,2},{2,1},{3,0},{4,7},{5,6},{6,5},{7,4},{8,11},{9,10},{10,... | collective-permute-start | bytes 49160 | tf_op jit(solution)/shard_map/ppermute | solution.py:364
  17.7 1.3 %collective-permute-start.6 = (f32[8,512]{1,0:T(8,128)S(1)}, f32[8,512]{1,0:T(8,128)S(1)}, u32[]{:S(2)}, u32[]{:S(2)}) collective-permute-start(f32[8,512]{1,0:T(8,128)S(1)} %get-tuple-element.23), channel_id=1, source_target_pairs={{0,1},{1,0},{2,3},{3,2},{4,5},{5,4},{6,7},{7,6},{8,9},{9,8},{10,11... | collective-permute-start | bytes 49160 | tf_op jit(solution)/shard_map/ppermute | solution.py:364
  19.1 0.0 collective-permute-start.7
  19.1 2.7 %derivative.1 = f32[3,768,512]{2,1,0:T(8,128)} custom-call(f32[3,768,512]{2,1,0:T(8,128)S(1)} %get-tuple-element.15.refs_0_, bf16[3,192,256]{2,1,0:T(8,128)(2,1)S(1)} %copy-done, f32[16,512]{1,0:T(8,128)S(1)} %get-tuple-element.20.refs_2_), custom_call_target="tpu_custom_call" | custom-call | flops 1811939328 | bytes 9437184 | tf_op jit(solution)/shard_map/derivative/pallas_call | solution.py:460
  21.7 0.0 collective-permute-done.5.refs_1_
  21.7 0.0 collective-permute-done.6.refs_2_
  21.8 1.0 %collective-permute-done.7.refs_3_ = f32[8,512]{1,0:T(8,128)S(1)} collective-permute-done((f32[8,512]{1,0:T(8,128)S(1)}, f32[8,512]{1,0:T(8,128)S(1)}, u32[]{:S(2)}, u32[]{:S(2)}) %collective-permute-start.7) | collective-permute-done | bytes 16416 | tf_op jit(solution)/shard_map/ppermute | solution.py:364
  22.8 0.6 %finish.1 = (f32[3,512]{1,0:T(4,128)}, f32[3,512]{1,0:T(4,128)}) custom-call(bf16[32,512]{1,0:T(8,128)(2,1)S(1)} %copy-done.1, f32[512]{0:T(512)S(1)} %copy-done.3, f32[3,512]{1,0:T(4,128)S(1)} %copy-done.2, f32[8,512]{1,0:T(8,128)S(1)} %get-tuple-element.21.refs_0_, f32[8,512]{1,0:T(8,128)S(1)} %collective-permute-done.5.refs_1_, ...), custom_call_target="tpu_custom_call" | custom-call | tf_op jit(solution)/shard_map/finish/pallas_call | solution.py:480
  (7 shorter events, 0.0 us)
Async XLA Ops:
  0.6 9.0 %copy-start = (bf16[3,192,256]{2,1,0:T(8,128)(2,1)S(1)}, bf16[3,192,256]{2,1,0:T(8,128)(2,1)}, u32[]{:S(2)}) copy-start(bf16[3,192,256]{2,1,0:T(8,128)(2,1)} %constant.2.clone.refs_1_) | copy-start | bytes 884740
  2.4 10.3 %copy-start.1 = (bf16[32,512]{1,0:T(8,128)(2,1)S(1)}, bf16[32,512]{1,0:T(8,128)(2,1)}, u32[]{:S(2)}) copy-start(bf16[32,512]{1,0:T(8,128)(2,1)} %get-tuple-element.19.refs_4_.request) | copy-start | bytes 98308
  2.4 10.3 %copy-start.4 = (s32[1,16]{1,0:T(1,128)S(1)}, s32[1,16]{1,0:T(1,128)}, u32[]{:S(2)}) copy-start(s32[1,16]{1,0:T(1,128)} %refs_0_.5) | copy-start | bytes 196
  2.4 10.3 %collective-permute-start.2 = (bf16[32,512]{1,0:T(8,128)(2,1)}, bf16[32,512]{1,0:T(8,128)(2,1)S(1)}, u32[]{:S(2)}, u32[]{:S(2)}) collective-permute-start(bf16[32,512]{1,0:T(8,128)(2,1)} %get-tuple-element.19.refs_4_.request), channel_id=1, source_target_pairs={{1,0},{0,1},{3,2},{2,3},{5,4},{4,5},{7,6},{6,7},{9,8},{8,9},{11,10... | collective-permute-start | bytes 98312 | tf_op jit(solution)/shard_map/ppermute | solution.py:364
  5.4 7.3 %collective-permute-start.3 = (bf16[32,512]{1,0:T(8,128)(2,1)}, bf16[32,512]{1,0:T(8,128)(2,1)S(1)}, u32[]{:S(2)}, u32[]{:S(2)}) collective-permute-start(bf16[32,512]{1,0:T(8,128)(2,1)} %get-tuple-element.19.refs_4_.request), channel_id=1, source_target_pairs={{2,0},{3,1},{0,2},{1,3},{6,4},{7,5},{4,6},{5,7},{10,8},{11,9},{8,1... | collective-permute-start | bytes 98312 | tf_op jit(solution)/shard_map/ppermute | solution.py:364
  7.0 5.8 %collective-permute-start.4 = (bf16[32,512]{1,0:T(8,128)(2,1)}, bf16[32,512]{1,0:T(8,128)(2,1)S(1)}, u32[]{:S(2)}, u32[]{:S(2)}) collective-permute-start(bf16[32,512]{1,0:T(8,128)(2,1)} %get-tuple-element.19.refs_4_.request), channel_id=1, source_target_pairs={{3,0},{2,1},{1,2},{0,3},{7,4},{6,5},{5,6},{4,7},{11,8},{10,9},{9,1... | collective-permute-start | bytes 98312 | tf_op jit(solution)/shard_map/ppermute | solution.py:364
  7.0 5.7 %collective-permute-start = (f32[8,512]{1,0:T(8,128)}, f32[8,512]{1,0:T(8,128)S(1)}, u32[]{:S(2)}, u32[]{:S(2)}) collective-permute-start(f32[8,512]{1,0:T(8,128)} %get-tuple-element.16), channel_id=1, source_target_pairs={{0,28},{4,8},{8,4},{12,16},{16,12},{20,24},{24,20},{28,0},{1,29},{... | collective-permute-start | bytes 49160 | tf_op jit(solution)/shard_map/ppermute | solution.py:364
  9.6 3.1 %collective-permute-start.1 = (f32[8,512]{1,0:T(8,128)}, f32[8,512]{1,0:T(8,128)S(1)}, u32[]{:S(2)}, u32[]{:S(2)}) collective-permute-start(f32[8,512]{1,0:T(8,128)} %get-tuple-element.17), channel_id=1, source_target_pairs={{0,4},{4,0},{8,12},{12,8},{16,20},{20,16},{24,28},{28,24},{1,5},{5... | collective-permute-start | bytes 49160 | tf_op jit(solution)/shard_map/ppermute | solution.py:364
  15.2 6.5 %collective-permute-start.5 = (f32[8,512]{1,0:T(8,128)S(1)}, f32[8,512]{1,0:T(8,128)S(1)}, u32[]{:S(2)}, u32[]{:S(2)}) collective-permute-start(f32[8,512]{1,0:T(8,128)S(1)} %get-tuple-element.22), channel_id=1, source_target_pairs={{0,3},{1,2},{2,1},{3,0},{4,7},{5,6},{6,5},{7,4},{8,11},{9,10},{10,... | collective-permute-start | bytes 49160 | tf_op jit(solution)/shard_map/ppermute | solution.py:364
  17.7 4.0 %collective-permute-start.6 = (f32[8,512]{1,0:T(8,128)S(1)}, f32[8,512]{1,0:T(8,128)S(1)}, u32[]{:S(2)}, u32[]{:S(2)}) collective-permute-start(f32[8,512]{1,0:T(8,128)S(1)} %get-tuple-element.23), channel_id=1, source_target_pairs={{0,1},{1,0},{2,3},{3,2},{4,5},{5,4},{6,7},{7,6},{8,9},{9,8},{10,11... | collective-permute-start | bytes 49160 | tf_op jit(solution)/shard_map/ppermute | solution.py:364
  19.1 3.7 %collective-permute-start.7 = (f32[8,512]{1,0:T(8,128)S(1)}, f32[8,512]{1,0:T(8,128)S(1)}, u32[]{:S(2)}, u32[]{:S(2)}) collective-permute-start(f32[8,512]{1,0:T(8,128)S(1)} %get-tuple-element.24), channel_id=1, source_target_pairs={{0,2},{1,3},{2,0},{3,1},{4,6},{5,7},{6,4},{7,5},{8,10},{9,11},{10,... | collective-permute-start | bytes 49160 | tf_op jit(solution)/shard_map/ppermute | solution.py:364
  19.1 3.7 %copy-start.2 = (f32[3,512]{1,0:T(4,128)S(1)}, f32[3,512]{1,0:T(4,128)}, u32[]{:S(2)}) copy-start(f32[3,512]{1,0:T(4,128)} %particle.1) | copy-start | bytes 18436
  19.1 3.7 %copy-start.3 = (f32[512]{0:T(512)S(1)}, f32[512]{0:T(512)}, u32[]{:S(2)}) copy-start(f32[512]{0:T(512)} %relax.1) | copy-start | bytes 6148
